TPU v7x, 512 devices: a whole 4x8x8 slice. The times are simulated.
512 devices in a mesh: row: 16 (over y, core), col: 32 (over z, x).
Axes of the slice: x: 4, y: 8, z: 8, core: 2. Of those that a mesh axis runs over, the one named last changes fastest.
Arguments:
- fronts: bfloat16 [32, 4096, 4096], P('col', 'row')
- pivots: int32 [32], replicated, may hold values from 1 to 3, as said below
- targets: int32 [32, 16], replicated, may hold values from 0 to 31, as said below
- ancestor: bfloat16 [2, 4096, 8192], P(None, 'row', 'col'), may hold values from -1.5 to 1.5
Outputs:
- factor: float32 [32, 4096, 768], P('col', 'row')
- assembled: float32 [2, 4096, 8192], P(None, 'row', 'col')
Inputs may be any that keep to these rules, and one draw needn't show every extreme that they name: `pivots`: every sibling eliminates at least one pivot block column; counts of 1 and of 3 both occur. targets[s, j] is j or j + 16; both ends of the range occur.
All inputs are finite; a program needn't handle non-finite values.
Results may differ from a plain program's by a relative error of at most 0.0011.
Values may be sent and summed in bfloat16 or wider, within the bound.
No kernel may reach another device: no remote copies, remote signals or barrier semaphores. Data moves between devices by JAX's collectives and lax.ppermute only.
A program may use at most 128 MiB of HBM per device.

v0:
```python
import jax
import jax.numpy as jnp
from jax import lax
from jax.sharding import PartitionSpec as P

STEPS = 3


def broadcast(shard, axis, root):
    mine = lax.axis_index(axis) == root
    return lax.psum(jnp.where(mine, shard, jnp.zeros_like(shard)), axis)


def contract(left_rows, right_rows):
    return lax.dot_general(
        left_rows, right_rows, (((1,), (1,)), ((), ())), preferred_element_type=jnp.float32
    )


def shards(fronts, pivots, targets, ancestor):
    row_index = lax.axis_index("row")
    col_index = lax.axis_index("col")
    col_count = lax.axis_size("col")
    block_size = fronts.shape[1]
    width = fronts.shape[2]
    block_count = width // block_size
    sibling_ids = jnp.arange(pivots.shape[0], dtype=jnp.int32)
    pivot_count = jnp.sum(jnp.where(sibling_ids == col_index, pivots, 0))
    working = fronts[0].astype(jnp.float32)
    factor_blocks = []
    for section in range(STEPS):
        lower_edge = section * block_size
        upper_edge = lower_edge + block_size
        column_block = working[:, lower_edge:upper_edge]
        diagonal = broadcast(column_block, "row", section)
        lower_block = jnp.linalg.cholesky(diagonal)
        solved = jax.scipy.linalg.solve_triangular(lower_block, column_block.T, lower=True).T
        is_active = section < pivot_count
        own_block = jnp.where(
            row_index > section, solved, jnp.where(row_index == section, lower_block, 0.0)
        )
        factor_blocks.append(jnp.where(is_active, own_block, 0.0))
        outgoing = jnp.where(is_active & (row_index > section), solved, 0.0).astype(jnp.bfloat16)

        def panel_product(piece_rows, first_row, outgoing=outgoing):
            return contract(outgoing, piece_rows)

        working = working - panel_product(
            lax.all_gather(outgoing, "row", axis=0, tiled=True), jnp.int32(0)
        )
    factor = jnp.concatenate(factor_blocks, axis=1)[None]
    row_blocks = working.reshape(block_size, block_count, block_size)
    my_targets = jnp.sum(jnp.where(sibling_ids[:, None] == col_index, targets, 0), axis=0)
    dest_ids = jnp.arange(col_count, dtype=jnp.int32)
    source_ids = dest_ids % block_count
    owned_target = jnp.concatenate([my_targets, my_targets])
    keep = (owned_target == dest_ids) & (source_ids >= pivot_count) & (row_index >= pivot_count)
    outgoing_blocks = jnp.where(
        keep[None, :, None], jnp.concatenate([row_blocks, row_blocks], axis=1), 0.0
    )
    received = lax.all_to_all(outgoing_blocks, "col", split_axis=1, concat_axis=1, tiled=True)
    block_ids = jnp.arange(block_count, dtype=jnp.int32)
    row_targets = jnp.sum(jnp.where(block_ids[None, :] == row_index, targets, 0), axis=1)
    halves = row_targets // block_count
    selector = (halves[None, :] == jnp.arange(2, dtype=jnp.int32)[:, None]).astype(jnp.float32)
    summed = jnp.einsum("hc,tcb->htb", selector, received, precision=lax.Precision.HIGHEST)
    assembled = ancestor.astype(jnp.float32) + summed
    return (factor, assembled)


def solution(mesh):
    in_specs = (P("col", "row", None), P(), P(), P(None, "row", "col"))
    out_specs = (P("col", "row", None), P(None, "row", "col"))
    return jax.shard_map(shards, mesh=mesh, in_specs=in_specs, out_specs=out_specs, check_vma=False)
```

profile of v0, /device:TPU:215, one launch (start us, length us, event | category | flops | bytes accessed | tf_op | source)
XLA Modules:
  0.0 948.4 jit_solution(6064967765680813457)
XLA Ops:
  7.2 3.3 copy.27
  10.5 2.3 bitcast_convert_fusion
  12.8 1.7 slice_select_fusion.2
  14.5 0.6 select_reduce_fusion.8
  15.8 114.1 %all-reduce.5.cloned.1.call-done = f32[256,256]{0,1:T(8,128)} async-done(((f32[256,256]{0,1:T(8,128)}), f32[256,256]{0,1:T(8,128)}) %all-reduce.5.cloned.1.call-update) | async-done | bytes 262160 | tf_op jit(solution)/shard_map/psum | solution.py:11
  129.9 1.1 copy.28
  131.0 1.0 fusion.7
  132.0 11.7 %cholesky.172 = f32[128,128]{1,0:T(8,128)S(1)} custom-call(f32[128,128]{1,0:T(8,128)S(1)} %cholesky.270), custom_call_target="Cholesky" | custom-call | tf_op jit(solution)/shard_map/jit(cholesky)/cholesky | solution.py:36
  143.9 9.8 %custom-call.15 = f32[1,128,128]{1,2,0:T(8,128)S(1)} custom-call(f32[1,128,128]{2,1,0:T(8,128)S(1)} %get-tuple-element.98), custom_call_target="InvertDiagBlocksLowerTriangular" | custom-call | tf_op jit(solution)/shard_map/jit(cholesky)/cholesky | solution.py:36
  154.3 11.7 %cholesky.189 = f32[128,128]{1,0:T(8,128)S(1)} custom-call(f32[128,128]{1,0:T(8,128)S(1)} %convolution_subtract_fusion.8), custom_call_target="Cholesky" | custom-call | tf_op jit(solution)/shard_map/jit(cholesky)/cholesky | solution.py:36
  166.1 0.7 compare_reduce_fusion.4
  168.3 4.6 while.6
  168.6 0.6 fusion.61
  169.2 1.4 dynamic-slice.17
  170.8 0.6 fusion.61
  171.4 1.4 dynamic-slice.17
  172.9 19.7 %custom-call.16 = f32[2,128,128]{1,2,0:T(8,128)S(1)} custom-call(f32[2,128,128]{2,1,0:T(8,128)S(1)} %get-tuple-element.24), custom_call_target="InvertDiagBlocksLowerTriangular" | custom-call | tf_op jit(solution)/shard_map/jit(_solve_triangular)/triangular_solve | solution.py:37
  193.6 0.7 select_convert_fusion.2
  194.3 44.9 %all-gather.4.cloned.1.call-done = bf16[4096,256]{0,1:T(8,128)(2,1)} async-done(((bf16[256,256]{0,1:T(8,128)(2,1)}), bf16[4096,256]{0,1:T(8,128)(2,1)}) %all-gather.4.cloned.1.call-update) | async-done | bytes 2097168 | tf_op jit(solution)/shard_map/all_gather | solution.py:49
  239.2 2.7 convolution_subtract_fusion.2
  241.9 1.9 copy-done
  243.9 0.7 slice_select_fusion.1
  245.2 112.0 %all-reduce.7.cloned.1.call-done = f32[256,256]{0,1:T(8,128)} async-done(((f32[256,256]{0,1:T(8,128)}), f32[256,256]{0,1:T(8,128)}) %all-reduce.7.cloned.1.call-update) | async-done | bytes 262160 | tf_op jit(solution)/shard_map/psum | solution.py:11
  357.2 1.1 copy.33
  358.3 1.0 fusion.6
  359.3 11.7 %cholesky.206 = f32[128,128]{1,0:T(8,128)S(1)} custom-call(f32[128,128]{1,0:T(8,128)S(1)} %cholesky.273), custom_call_target="Cholesky" | custom-call | tf_op jit(solution)/shard_map/jit(cholesky)/cholesky | solution.py:36
  371.2 9.8 %custom-call.17 = f32[1,128,128]{1,2,0:T(8,128)S(1)} custom-call(f32[1,128,128]{2,1,0:T(8,128)S(1)} %get-tuple-element.96), custom_call_target="InvertDiagBlocksLowerTriangular" | custom-call | tf_op jit(solution)/shard_map/jit(cholesky)/cholesky | solution.py:36
  381.6 11.7 %cholesky.223 = f32[128,128]{1,0:T(8,128)S(1)} custom-call(f32[128,128]{1,0:T(8,128)S(1)} %convolution_subtract_fusion.7), custom_call_target="Cholesky" | custom-call | tf_op jit(solution)/shard_map/jit(cholesky)/cholesky | solution.py:36
  393.5 0.6 compare_reduce_fusion.3
  394.1 0.6 compare_reduce_fusion.2
  396.1 14.5 %while.7 = (s32[]{:T(128)}, f32[256,256]{0,1:T(8,128)S(1)}, s32[2,2]{1,0:T(2,128)S(1)}, f32[2,128,128]{2,1,0:T(8,128)S(1)}, s32[]{:T(128)}) while((s32[]{:T(128)}, f32[256,256]{0,1:T(8,128)S(1)}, s32[2,2]{1,0:T(2,128)S(1)}, f32[2,128,128]{2,1,0:T(8,128)S(1)}, s32[]{:T(128)}) %tuple.94), condition=%wide.while_cond.clone, body=%wide.while_body.clone.sunk | while | flops 2 | bytes 393329 | solution.py:37
  406.5 0.6 fusion.62
  407.0 1.4 dynamic-slice.19
  409.1 1.4 dynamic-slice.19
  410.6 19.7 %custom-call.18 = f32[2,128,128]{1,2,0:T(8,128)S(1)} custom-call(f32[2,128,128]{2,1,0:T(8,128)S(1)} %get-tuple-element.25), custom_call_target="InvertDiagBlocksLowerTriangular" | custom-call | tf_op jit(solution)/shard_map/jit(_solve_triangular)/triangular_solve | solution.py:37
  431.3 0.7 select_convert_fusion.1
  432.0 44.9 %all-gather.6.cloned.1.call-done = bf16[4096,256]{0,1:T(8,128)(2,1)} async-done(((bf16[256,256]{0,1:T(8,128)(2,1)}), bf16[4096,256]{0,1:T(8,128)(2,1)}) %all-gather.6.cloned.1.call-update) | async-done | bytes 2097168 | tf_op jit(solution)/shard_map/all_gather | solution.py:49
  476.9 3.8 convolution_subtract_fusion.1
  480.8 1.9 copy-done.1
  482.7 0.7 slice_bitcast_fusion
  484.1 112.2 %all-reduce.9.cloned.1.call-done = f32[256,256]{0,1:T(8,128)} async-done(((f32[256,256]{0,1:T(8,128)}), f32[256,256]{0,1:T(8,128)}) %all-reduce.9.cloned.1.call-update) | async-done | bytes 262160 | tf_op jit(solution)/shard_map/psum | solution.py:11
  596.3 1.1 copy.38
  597.3 1.0 fusion.5
  598.4 11.7 %cholesky.240 = f32[128,128]{1,0:T(8,128)S(1)} custom-call(f32[128,128]{1,0:T(8,128)S(1)} %cholesky.276), custom_call_target="Cholesky" | custom-call | tf_op jit(solution)/shard_map/jit(cholesky)/cholesky | solution.py:36
  610.2 9.8 %custom-call.19 = f32[1,128,128]{1,2,0:T(8,128)S(1)} custom-call(f32[1,128,128]{2,1,0:T(8,128)S(1)} %get-tuple-element.94), custom_call_target="InvertDiagBlocksLowerTriangular" | custom-call | tf_op jit(solution)/shard_map/jit(cholesky)/cholesky | solution.py:36
  620.6 11.7 %cholesky.257 = f32[128,128]{1,0:T(8,128)S(1)} custom-call(f32[128,128]{1,0:T(8,128)S(1)} %convolution_subtract_fusion.6), custom_call_target="Cholesky" | custom-call | tf_op jit(solution)/shard_map/jit(cholesky)/cholesky | solution.py:36
  632.5 0.6 compare_reduce_fusion.1
  633.1 0.6 compare_reduce_fusion
  635.1 4.4 while.8
  635.3 0.6 fusion.63
  635.9 1.4 dynamic-slice.21
  638.0 1.4 dynamic-slice.21
  639.5 19.7 %custom-call.20 = f32[2,128,128]{1,2,0:T(8,128)S(1)} custom-call(f32[2,128,128]{2,1,0:T(8,128)S(1)} %get-tuple-element.26), custom_call_target="InvertDiagBlocksLowerTriangular" | custom-call | tf_op jit(solution)/shard_map/jit(_solve_triangular)/triangular_solve | solution.py:37
  660.1 0.7 select_convert_fusion
  661.6 0.7 and_and_fusion
  662.2 43.6 %all-gather.8.cloned.1.call-done = bf16[4096,256]{0,1:T(8,128)(2,1)} async-done(((bf16[256,256]{0,1:T(8,128)(2,1)}), bf16[4096,256]{0,1:T(8,128)(2,1)}) %all-gather.8.cloned.1.call-update) | async-done | bytes 2097168 | tf_op jit(solution)/shard_map/all_gather | solution.py:49
  705.8 5.8 convolution_subtract_fusion
  711.6 5.3 copy.44
  716.9 7.9 maximum_select_fusion
  724.8 9.9 %all-to-all-start = ((f32[256,32,256]{2,0,1:T(8,128)}), f32[256,32,256]{2,0,1:T(8,128)}, u32[]{:S(2)}, u32[]{:S(2)}) async-start(f32[256,32,256]{2,0,1:T(8,128)} %maximum_select_fusion), calls=%async_computation | async-start | bytes 16777216 | tf_op jit(solution)/shard_map/all_to_all | solution.py:61
  735.0 1.1 copy.47
  736.2 193.6 %all-to-all-done = f32[256,32,256]{2,0,1:T(8,128)} async-done(((f32[256,32,256]{2,0,1:T(8,128)}), f32[256,32,256]{2,0,1:T(8,128)}, u32[]{:S(2)}, u32[]{:S(2)}) %all-to-all-start) | async-done | bytes 8388640 | tf_op jit(solution)/shard_map/all_to_all | solution.py:61
  929.8 10.5 %fusion.2 = f32[2,256,256]{2,0,1:T(2,128)S(1)} fusion(f32[256,32,256]{2,0,1:T(8,128)} %all-to-all-done, bf16[2,256,256]{2,1,0:T(8,128)(2,1)S(1)} %copy-done.2, s32[32]{0:T(128)S(1)} %and_select_fusion.1), kind=kOutput, calls=%fused_computation.13 | convolution fusion | flops 50593856 | bytes 9175168 | tf_op jit(solution)/shard_map/hc,tcb->htb/dot_general | solution.py:66
  940.3 0.8 copy.48
  (92 shorter events, 8.1 us)
Async XLA Ops:
  7.2 122.8 %all-reduce.5.cloned.1.call-start = ((), (), s32[]{:S(2)}) async-start(), calls=%async_computation.1 | async-start | bytes 524288 | tf_op jit(solution)/shard_map/psum | solution.py:11
  10.5 4.0 copy-start.4
  14.5 224.8 %all-gather.4.cloned.1.call-start = ((), (), s32[]{:S(2)}) async-start(), calls=%async_computation.2 | async-start | bytes 2228224 | tf_op jit(solution)/shard_map/all_gather | solution.py:49
  194.3 163.0 %all-reduce.7.cloned.1.call-start = ((), (), s32[]{:S(2)}) async-start(), calls=%async_computation.3 | async-start | bytes 524288 | tf_op jit(solution)/shard_map/psum | solution.py:11
  241.9 1.9 copy-start
  244.6 232.3 %all-gather.6.cloned.1.call-start = ((), (), s32[]{:S(2)}) async-start(), calls=%async_computation.4 | async-start | bytes 2228224 | tf_op jit(solution)/shard_map/all_gather | solution.py:49
  432.0 164.3 %all-reduce.9.cloned.1.call-start = ((), (), s32[]{:S(2)}) async-start(), calls=%async_computation.5 | async-start | bytes 524288 | tf_op jit(solution)/shard_map/psum | solution.py:11
  480.8 1.9 copy-start.1
  482.7 178.8 %copy-start.3 = (s32[32,16]{0,1:T(8,128)S(1)}, s32[32,16]{0,1:T(8,128)}, u32[]{:S(2)}) copy-start(s32[32,16]{0,1:T(8,128)} %param.9) | copy-start | bytes 6148
  483.4 222.4 %all-gather.8.cloned.1.call-start = ((), (), s32[]{:S(2)}) async-start(), calls=%async_computation.6 | async-start | bytes 2228224 | tf_op jit(solution)/shard_map/all_gather | solution.py:49
  724.8 204.9 %all-to-all-start = ((f32[256,32,256]{2,0,1:T(8,128)}), f32[256,32,256]{2,0,1:T(8,128)}, u32[]{:S(2)}, u32[]{:S(2)}) async-start(f32[256,32,256]{2,0,1:T(8,128)} %maximum_select_fusion), calls=%async_computation | async-start | bytes 16777216 | tf_op jit(solution)/shard_map/all_to_all | solution.py:61
  734.7 195.0 %copy-start.2 = (bf16[2,256,256]{2,1,0:T(8,128)(2,1)S(1)}, bf16[2,256,256]{2,1,0:T(8,128)(2,1)}, u32[]{:S(2)}) copy-start(bf16[2,256,256]{2,1,0:T(8,128)(2,1)} %param.10) | copy-start | bytes 786436
Sparse Core Ops, SparseCore 0:
  14.6 115.2 all-reduce.4
  194.4 44.8 all-gather.3
  244.7 112.4 all-reduce.6
  432.1 44.7 all-gather.5
  483.6 112.6 all-reduce.8
  661.0 44.7 all-gather.7
where the time goes:
time: 958 us; the launch traced here: 948 us
  waiting for transfers between devices  665 us (69%)
  other arithmetic  182 us (19%)
  local copies, waits for them, and re-layouts  30.9 us (3%)
  matrix products  27.3 us (3%)
  between operations  21.3 us (2%)
  loops' own time  11.1 us (1%)
  starting transfers between devices  10.1 us (1%)
    psum x3, waiting for transfers between devices, broadcast(): return lax.psum(jnp.where(mine, shard, jnp.zeros_like(shard)), axis)  338 us
    all_to_all x1, waiting for transfers between devices, shards(): lax.all_to_all(outgoing_blocks, 'col', split_axis=1, concat_axis=1, tiled...  194 us
    all_gather x3, waiting for transfers between devices, shards(): lax.all_gather(outgoing, 'row', axis=0, tiled=True)  133 us
    another operation x20, other arithmetic, shards(): lower_block = jnp.linalg.cholesky(diagonal)  103 us
    another operation x7, other arithmetic, shards(): jax.scipy.linalg.solve_triangular(lower_block, column_block.T, lower=True)  59.1 us
  transfers between devices with their start and end apart: 7, of which 7 were waited for; matrix products, arithmetic and copies ran while one was open for 0% of the time, Pallas kernels for 0%

commit v1 on v0

v1 whole, which is shorter than its diff:
```python
import jax
import jax.numpy as jnp
from jax import lax
from jax.experimental import pallas as pl
from jax.experimental.pallas import tpu as pltpu
from jax.sharding import PartitionSpec as P

STEPS = 3
B = 256
SUB = 8
F32 = jnp.float32
BF16 = jnp.bfloat16
HIGHEST = lax.Precision.HIGHEST


def dot_nt(a, b, precision=None):
    return lax.dot_general(
        a, b, (((1,), (1,)), ((), ())), precision=precision, preferred_element_type=F32
    )


def small_inverse_columns(x, k0):
    sub = lax.broadcasted_iota(jnp.int32, (SUB, 128), 0)
    e = [[None] * SUB for _ in range(SUB)]
    for a in range(SUB):
        for b in range(a + 1):
            e[a][b] = jnp.broadcast_to(x[a : a + 1, k0 + b : k0 + b + 1], (SUB, 128))
    m = [[None] * SUB for _ in range(SUB)]
    for k in range(SUB):
        rc = 1.0 / e[k][k]
        for a in range(k + 1, SUB):
            m[a][k] = e[a][k] * rc
        for a in range(k + 1, SUB):
            for b in range(k + 1, a + 1):
                e[a][b] = e[a][b] - m[a][k] * e[b][k]
    inv = [[None] * SUB for _ in range(SUB)]
    for b in range(SUB):
        for a in range(b + 1, SUB):
            v = m[a][b]
            for c in range(b + 1, a):
                v = v + m[a][c] * inv[c][b]
            inv[a][b] = -v
    piv = e[0][0]
    for a in range(1, SUB):
        piv = jnp.where(sub == a, e[a][a], piv)
    scale = lax.rsqrt(piv)
    cols = []
    for b in range(SUB):
        v = jnp.where(sub == b, 1.0, 0.0)
        for a in range(b + 1, SUB):
            v = jnp.where(sub == a, inv[a][b], v)
        cols.append(v * scale)
    return cols


def cholesky_in_place(t_ref):
    lane = lax.broadcasted_iota(jnp.int32, (SUB, B), 1)
    sub = lax.broadcasted_iota(jnp.int32, (SUB, B), 0)
    for p in range(B // SUB):
        k0 = SUB * p
        x = t_ref[k0 : k0 + SUB, :]
        cols = small_inverse_columns(x, k0)
        r = None
        z = 0.0
        for b in range(SUB):
            wide = jnp.concatenate([cols[b], cols[b]], axis=1)
            term = wide * jnp.broadcast_to(x[b : b + 1, :], (SUB, B))
            r = term if r is None else r + term
            z = jnp.where(lane == k0 + b, wide, z)
        in_block = (lane >= k0) & (lane < k0 + SUB)
        t_ref[k0 : k0 + SUB, :] = jnp.where(in_block & (lane <= k0 + sub), z, r)
        if k0 + SUB < B:
            left = r.T[k0 + SUB :, :]
            update = jnp.dot(
                left, jnp.where(in_block, z, r), precision=HIGHEST, preferred_element_type=F32
            )
            lanes = lax.broadcasted_iota(jnp.int32, (B - k0 - SUB, B), 1)
            old = t_ref[k0 + SUB :, :]
            old = jnp.where((lanes >= k0) & (lanes < k0 + SUB), 0.0, old)
            t_ref[k0 + SUB :, :] = old - update


def chain_kernel(a_ref, low_ref, inv_ref, pan_ref, w_ref, t_ref):
    t = pl.program_id(0)

    @pl.when(t == 0)
    def _():
        w_ref[...] = a_ref[...].astype(F32)

    for s in range(STEPS):

        @pl.when(t == s)
        def _(s=s):
            d = w_ref[s * B : (s + 1) * B, s * B : (s + 1) * B]
            t_ref[...] = 0.5 * (d + d.T)

    cholesky_in_place(t_ref)
    t_val = t_ref[...]
    ri = lax.broadcasted_iota(jnp.int32, (B, B), 0)
    ci = lax.broadcasted_iota(jnp.int32, (B, B), 1)
    inv = jnp.where(ci <= ri, t_val, 0.0)
    inv_ref[0] = inv
    low_ref[0] = jnp.where(ci > ri, t_val, jnp.where(ci == ri, 1.0 / t_val, 0.0)).T

    for s in range(STEPS - 1):

        @pl.when(t == s)
        def _(s=s):
            panels = []
            for r in range(s + 1, STEPS):
                w = w_ref[r * B : (r + 1) * B, s * B : (s + 1) * B]
                panel = dot_nt(w, inv, HIGHEST).astype(BF16)
                panels.append(panel)
                pan_ref[s + r - 1] = panel
            for r in range(s + 1, STEPS):
                for c in range(s + 1, r + 1):
                    w_ref[r * B : (r + 1) * B, c * B : (c + 1) * B] -= dot_nt(
                        panels[r - s - 1], panels[c - s - 1]
                    )


def factor_corner(corner):
    return pl.pallas_call(
        chain_kernel,
        grid=(STEPS,),
        in_specs=[pl.BlockSpec((STEPS * B, STEPS * B), lambda t: (0, 0))],
        out_specs=[
            pl.BlockSpec((1, B, B), lambda t: (t, 0, 0)),
            pl.BlockSpec((1, B, B), lambda t: (t, 0, 0)),
            pl.BlockSpec((STEPS, B, B), lambda t: (0, 0, 0)),
        ],
        out_shape=[
            jax.ShapeDtypeStruct((STEPS, B, B), F32),
            jax.ShapeDtypeStruct((STEPS, B, B), F32),
            jax.ShapeDtypeStruct((STEPS, B, B), BF16),
        ],
        scratch_shapes=[pltpu.VMEM((STEPS * B, STEPS * B), F32), pltpu.VMEM((B, B), F32)],
        compiler_params=pltpu.CompilerParams(vmem_limit_bytes=40 << 20),
        cost_estimate=pl.CostEstimate(
            flops=60_000_000_000, bytes_accessed=4 << 20, transcendentals=0
        ),
    )(corner)


def solve_rows(a, inv_ref, pan_ref, precision):
    solved = []
    panels = []
    for t in range(STEPS):
        w = a[:, t * B : (t + 1) * B].astype(F32)
        for s in range(t):
            w = w - dot_nt(panels[s], pan_ref[t + s - 1])
        x = dot_nt(w, inv_ref[t], precision)
        solved.append(x)
        panels.append(x.astype(BF16))
    return solved, panels


def update_kernel(
    scalars, own_ref, all_ref, low_ref, inv_ref, pan_ref, factor_ref, u_ref, mine_ref
):
    pivots = scalars[0]
    row = scalars[1]

    @pl.when(pl.program_id(0) == 0)
    def _():
        solved, panels = solve_rows(own_ref[...], inv_ref, pan_ref, HIGHEST)
        for t in range(STEPS):
            active = t < pivots
            block = jnp.where(row > t, solved[t], jnp.where(row == t, low_ref[t], 0.0))
            factor_ref[:, t * B : (t + 1) * B] = jnp.where(active, block, 0.0)
            mine_ref[:, t * B : (t + 1) * B] = jnp.where(active, panels[t], 0.0).astype(BF16)

    _, panels = solve_rows(all_ref[0], inv_ref, pan_ref, HIGHEST)
    other = jnp.concatenate(
        [jnp.where(t < pivots, panels[t], 0.0).astype(BF16) for t in range(STEPS)], axis=1
    )
    u_ref[0] = dot_nt(mine_ref[...], other).astype(BF16)


def solve_and_update(scalars, own, gathered, low, inv, pan):
    blocks = gathered.shape[0]
    whole = lambda j: (0, 0, 0)
    return pl.pallas_call(
        update_kernel,
        grid=(blocks,),
        in_specs=[
            pl.BlockSpec(memory_space=pltpu.SMEM),
            pl.BlockSpec((B, STEPS * B), lambda j: (0, 0)),
            pl.BlockSpec((1, B, STEPS * B), lambda j: (j, 0, 0)),
            pl.BlockSpec((STEPS, B, B), whole),
            pl.BlockSpec((STEPS, B, B), whole),
            pl.BlockSpec((STEPS, B, B), whole),
        ],
        out_specs=[
            pl.BlockSpec((B, STEPS * B), lambda j: (0, 0)),
            pl.BlockSpec((1, B, B), lambda j: (j, 0, 0)),
        ],
        out_shape=[
            jax.ShapeDtypeStruct((B, STEPS * B), F32),
            jax.ShapeDtypeStruct((blocks, B, B), BF16),
        ],
        scratch_shapes=[pltpu.VMEM((B, STEPS * B), BF16)],
        compiler_params=pltpu.CompilerParams(vmem_limit_bytes=40 << 20),
        cost_estimate=pl.CostEstimate(
            flops=16_000_000_000, bytes_accessed=16 << 20, transcendentals=0
        ),
    )(scalars, own, gathered, low, inv, pan)


def sum_kernel(slots, f_ref, u_ref, anc_ref, acc_ref):
    k = pl.program_id(0)

    @pl.when(k == 0)
    def _():
        acc_ref[0:2] = anc_ref[...].astype(F32)
        acc_ref[2:4] = jnp.zeros((2, B, B), F32)

    slot = slots[k]

    @pl.when(slot < 4)
    def _():
        acc_ref[slot] += f_ref[0].astype(F32) - u_ref[0].astype(F32)


def sum_blocks(slots, f, u, ancestor):
    count = f.shape[0]
    return pl.pallas_call(
        sum_kernel,
        grid=(count,),
        in_specs=[
            pl.BlockSpec(memory_space=pltpu.SMEM),
            pl.BlockSpec((1, B, B), lambda k: (k, 0, 0)),
            pl.BlockSpec((1, B, B), lambda k: (k, 0, 0)),
            pl.BlockSpec((2, B, B), lambda k: (0, 0, 0)),
        ],
        out_specs=pl.BlockSpec((4, B, B), lambda k: (0, 0, 0)),
        out_shape=jax.ShapeDtypeStruct((4, B, B), F32),
        compiler_params=pltpu.CompilerParams(vmem_limit_bytes=40 << 20),
        cost_estimate=pl.CostEstimate(
            flops=4_000_000, bytes_accessed=6 << 20, transcendentals=0
        ),
    )(slots, f, u, ancestor)


def shards(fronts, pivots, targets, ancestor):
    row = lax.axis_index("row")
    col = lax.axis_index("col")
    cols = lax.axis_size("col")
    blocks = fronts.shape[2] // B
    half = cols // 2
    groups = [list(range(half)), list(range(half, cols))]
    front = fronts[0]

    own = front[:, : STEPS * B]
    gathered = lax.all_gather(own, "row", axis=0, tiled=False)
    f = front.reshape(B, blocks, B).swapaxes(0, 1)
    f = lax.all_to_all(f, "col", 0, 0, axis_index_groups=groups, tiled=True)

    low, inv, pan = factor_corner(gathered[:STEPS].reshape(STEPS * B, STEPS * B))
    scalars = jnp.stack([pivots[col], row.astype(jnp.int32)])
    factor, u = solve_and_update(scalars, own, gathered, low, inv, pan)
    u = lax.all_to_all(u, "col", 0, 0, axis_index_groups=groups, tiled=True)

    side = col // half
    block_col = col % half
    first = side * half
    piv = lax.dynamic_slice_in_dim(pivots, first, half)
    tgt = lax.dynamic_slice_in_dim(targets, first, half, axis=0)
    col_half = lax.dynamic_index_in_dim(tgt, block_col, 1, keepdims=False) // blocks
    row_half = lax.dynamic_index_in_dim(tgt, row, 1, keepdims=False) // blocks
    keep = (block_col >= piv) & (row >= piv)
    slots = jnp.where(keep, jnp.where(col_half == side, 0, 2) + row_half, 4).astype(jnp.int32)
    acc = sum_blocks(slots, f, u, ancestor)
    received = lax.ppermute(acc[2:4], "col", [(c, (c + half) % cols) for c in range(cols)])
    return factor[None], acc[0:2] + received


def solution(mesh):
    in_specs = (P("col", "row", None), P(), P(), P(None, "row", "col"))
    out_specs = (P("col", "row", None), P(None, "row", "col"))
    return jax.shard_map(shards, mesh=mesh, in_specs=in_specs, out_specs=out_specs, check_vma=False)
```

time: 958 us -> 258 us (0.27)
  the two profiles are of different devices: /device:TPU:215 before, /device:TPU:69 now
where the time goes in v1:
time: 258 us
  waiting for transfers between devices  111 us (43%)
  Pallas kernels  97.7 us (38%)
  starting transfers between devices  21.4 us (8%)
  between operations  14.1 us (5%)
  local copies, waits for them, and re-layouts  11 us (4%)
    pallas_call x1, Pallas kernels, factor_corner(): pl.pallas_call(chain_kernel, grid=(STEPS,), in_specs=[pl.BlockSpec((STEPS...  56.1 us
    all_to_all x1, waiting for transfers between devices, shards(): u = lax.all_to_all(u, 'col', 0, 0, axis_index_groups=groups, tiled=True)  46.7 us
    all_gather x1, waiting for transfers between devices, shards(): gathered = lax.all_gather(own, 'row', axis=0, tiled=False)  38.6 us
    pallas_call x1, Pallas kernels, solve_and_update(): pl.pallas_call(update_kernel, grid=(blocks,), in_specs=[pl.BlockSpec(memo...  33.8 us
    ppermute x1, waiting for transfers between devices, shards(): lax.ppermute(acc[2:4], 'col', [(c, (c + half) % cols) for c in range(cols)])  25.7 us
    all_to_all x1, starting transfers between devices, shards(): f = lax.all_to_all(f, 'col', 0, 0, axis_index_groups=groups, tiled=True)  8.91 us
    pallas_call x1, Pallas kernels, sum_blocks(): pl.pallas_call(sum_kernel, grid=(count,), in_specs=[pl.BlockSpec(memory_s...  7.79 us
    all_to_all x1, starting transfers between devices, shards(): u = lax.all_to_all(u, 'col', 0, 0, axis_index_groups=groups, tiled=True)  7.45 us
  transfers between devices with their start and end apart: 4, of which 3 were waited for; matrix products, arithmetic and copies ran while one was open for 4% of the time, Pallas kernels for 35%

profile of v1, /device:TPU:69, one launch (start us, length us, event | category | flops | bytes accessed | tf_op | source)
XLA Modules:
  0.0 257.6 jit_solution(4057520806497833032)
XLA Ops:
  7.2 0.0 all-gather.3.cloned.1.call-start
  7.2 1.8 slice.17.own_ref
  9.0 0.0 all-gather.3.cloned.1.call-update
  9.0 3.3 %copy.6 = bf16[1,256,4096]{1,2,0:T(8,128)(2,1)S(1)} copy(bf16[1,256,4096]{2,1,0:T(8,128)(2,1)} %param.4) | data formatting | bytes 4194304 | tf_op args[0]
  12.3 2.5 copy.7
  14.8 0.0 copy-start.3
  14.8 8.9 %all-to-all-start = ((bf16[16,256,256]{2,1,0:T(8,128)(2,1)}), bf16[16,256,256]{2,1,0:T(8,128)(2,1)S(1)}, u32[]{:S(2)}, u32[]{:S(2)}) async-start(bf16[16,256,256]{2,1,0:T(8,128)(2,1)} %bitcast.29), calls=%async_computation | async-start | bytes 4194304 | tf_op jit(solution)/shard_map/all_to_all | solution.py:257
  23.7 0.0 copy-done.3
  23.7 0.6 dynamic_slice.14
  24.3 0.7 pad_add_fusion.scalars
  25.0 38.6 %all-gather.3.cloned.1.call-done = bf16[4096,768]{1,0:T(8,128)(2,1)} async-done(((bf16[256,768]{1,0:T(8,128)(2,1)}), bf16[4096,768]{1,0:T(8,128)(2,1)}) %all-gather.3.cloned.1.call-update) | async-done | bytes 6291472 | tf_op jit(solution)/shard_map/all_gather | solution.py:255
  63.5 0.0 slice-start
  63.5 1.5 slice.18.a_ref
  65.0 0.0 copy-start.1
  65.0 0.0 slice-start.1
  65.1 56.1 %shard_map.59 = (f32[3,256,256]{2,1,0:T(8,128)S(1)}, f32[3,256,256]{2,1,0:T(8,128)S(1)}, bf16[3,256,256]{2,1,0:T(8,128)(2,1)S(1)}) custom-call(bf16[768,768]{1,0:T(8,128)(2,1)S(1)} %slice.18.a_ref), custom_call_target="tpu_custom_call" | custom-call | flops 60000002048 | bytes 4194304 | tf_op jit(solution)/shard_map/pallas_call | solution.py:123
  121.1 0.0 slice-done
  121.1 0.0 copy-done.1
  121.2 0.0 slice-done.1
  121.2 33.8 %shard_map.60 = (f32[256,768]{1,0:T(8,128)}, bf16[16,256,256]{2,1,0:T(8,128)(2,1)S(1)}) custom-call(s32[2]{0:T(128)S(1)} %pad_add_fusion.scalars, bf16[256,768]{1,0:T(8,128)(2,1)S(1)} %copy-done.1, bf16[16,256,768]{2,1,0:T(8,128)(2,1)S(1)} %bitcast.28, f32[3,256,256]{2,1,0:T(8,128)S(1)} %get-tuple-element.7.low_ref, ...), custom_call_target="tpu_custom_call" | custom-call | flops 16000000000 | bytes 16777216 | tf_op jit(solution)/shard_map/pallas_call | solution.py:183
  155.0 0.0 copy-start
  155.0 1.3 copy-done
  156.3 0.0 all-to-all-done.f_ref
  156.3 0.0 copy-start.2
  156.3 7.5 %all-to-all-start.1 = ((bf16[16,256,256]{2,1,0:T(8,128)(2,1)}), bf16[16,256,256]{2,1,0:T(8,128)(2,1)}, u32[]{:S(2)}, u32[]{:S(2)}) async-start(bf16[16,256,256]{2,1,0:T(8,128)(2,1)} %copy-done), calls=%async_computation.1 | async-start | bytes 4194304 | tf_op jit(solution)/shard_map/all_to_all | solution.py:262
  163.8 0.8 and_select_fusion.2.slots
  164.7 46.7 %all-to-all-done.1.u_ref = bf16[16,256,256]{2,1,0:T(8,128)(2,1)} async-done(((bf16[16,256,256]{2,1,0:T(8,128)(2,1)}), bf16[16,256,256]{2,1,0:T(8,128)(2,1)}, u32[]{:S(2)}, u32[]{:S(2)}) %all-to-all-start.1) | async-done | bytes 2097184 | tf_op jit(solution)/shard_map/all_to_all | solution.py:262
  211.3 0.0 copy-done.2
  211.3 7.8 %shard_map.61 = f32[4,256,256]{2,1,0:T(8,128)S(1)} custom-call(s32[16]{0:T(128)S(1)} %and_select_fusion.2.slots, bf16[16,256,256]{2,1,0:T(8,128)(2,1)S(1)} %all-to-all-done.f_ref, bf16[16,256,256]{2,1,0:T(8,128)(2,1)} %all-to-all-done.1.u_ref, bf16[2,256,256]{2,1,0:T(8,128)(2,1)S(1)} %copy-done.2), custom_call_target="tpu_custom_call" | custom-call | flops 4000000 | bytes 6291456 | tf_op jit(solution)/shard_map/pallas_call | solution.py:227
  219.2 5.0 %collective-permute-start = (f32[2,256,256]{2,1,0:T(8,128)S(1)}, f32[2,256,256]{2,1,0:T(8,128)S(1)}, u32[]{:S(2)}, u32[]{:S(2)}) collective-permute-start(f32[2,256,256]{2,1,0:T(8,128)S(1)} %slice.20), channel_id=1, source_target_pairs={{0,16},{1,17},{2,18},{3,19},{4,20},{5,21},{6,22},{7,23},{8,24},{9,... | collective-permute-start | bytes 1572872 | tf_op jit(solution)/shard_map/ppermute | solution.py:274
  224.2 25.7 %collective-permute-done = f32[2,256,256]{2,1,0:T(8,128)S(1)} collective-permute-done((f32[2,256,256]{2,1,0:T(8,128)S(1)}, f32[2,256,256]{2,1,0:T(8,128)S(1)}, u32[]{:S(2)}, u32[]{:S(2)}) %collective-permute-start) | collective-permute-done | bytes 524320 | tf_op jit(solution)/shard_map/ppermute | solution.py:274
  249.9 0.9 slice_add_fusion
  (2 shorter events, 0.0 us)
Async XLA Ops:
  7.2 56.4 %all-gather.3.cloned.1.call-start = ((), (), s32[]{:S(2)}) async-start(), calls=%async_computation.2 | async-start | bytes 6684672 | tf_op jit(solution)/shard_map/all_gather | solution.py:255
  14.8 8.9 %copy-start.3 = (s32[32]{0:T(128)S(1)}, s32[32]{0:T(128)}, u32[]{:S(2)}) copy-start(s32[32]{0:T(128)} %param.5) | copy-start | bytes 388
  14.8 141.6 %all-to-all-start = ((bf16[16,256,256]{2,1,0:T(8,128)(2,1)}), bf16[16,256,256]{2,1,0:T(8,128)(2,1)S(1)}, u32[]{:S(2)}, u32[]{:S(2)}) async-start(bf16[16,256,256]{2,1,0:T(8,128)(2,1)} %bitcast.29), calls=%async_computation | async-start | bytes 4194304 | tf_op jit(solution)/shard_map/all_to_all | solution.py:257
  63.5 57.6 %slice-start = ((s8[6291456]{0:T(1024)(128)(4,1)}), s8[4194304]{0:T(1024)(128)(4,1)S(1)}, s32[]{:S(2)}) async-start(s8[6291456]{0:T(1024)(128)(4,1)} %bitcast.26), calls=%async_computation.3 | async-start | bytes 8388608
  65.0 56.1 %copy-start.1 = (bf16[256,768]{1,0:T(8,128)(2,1)S(1)}, bf16[256,768]{1,0:T(8,128)(2,1)}, u32[]{:S(2)}) copy-start(bf16[256,768]{1,0:T(8,128)(2,1)} %slice.17.own_ref) | copy-start | bytes 1179652
  65.0 56.1 %slice-start.1 = ((s8[6291456]{0:T(1024)(128)(4,1)}), s8[2097152]{0:T(1024)(128)(4,1)S(1)}, s32[]{:S(2)}) async-start(s8[6291456]{0:T(1024)(128)(4,1)} %bitcast.26), calls=%async_computation.4 | async-start | bytes 4194304
  155.0 1.3 copy-start
  156.3 55.0 %copy-start.2 = (bf16[2,256,256]{2,1,0:T(8,128)(2,1)S(1)}, bf16[2,256,256]{2,1,0:T(8,128)(2,1)}, u32[]{:S(2)}) copy-start(bf16[2,256,256]{2,1,0:T(8,128)(2,1)} %anc_ref.1) | copy-start | bytes 786436
  156.3 55.0 %all-to-all-start.1 = ((bf16[16,256,256]{2,1,0:T(8,128)(2,1)}), bf16[16,256,256]{2,1,0:T(8,128)(2,1)}, u32[]{:S(2)}, u32[]{:S(2)}) async-start(bf16[16,256,256]{2,1,0:T(8,128)(2,1)} %copy-done), calls=%async_computation.1 | async-start | bytes 4194304 | tf_op jit(solution)/shard_map/all_to_all | solution.py:262
  219.2 30.8 %collective-permute-start = (f32[2,256,256]{2,1,0:T(8,128)S(1)}, f32[2,256,256]{2,1,0:T(8,128)S(1)}, u32[]{:S(2)}, u32[]{:S(2)}) collective-permute-start(f32[2,256,256]{2,1,0:T(8,128)S(1)} %slice.20), channel_id=1, source_target_pairs={{0,16},{1,17},{2,18},{3,19},{4,20},{5,21},{6,22},{7,23},{8,24},{9,... | collective-permute-start | bytes 1572872 | tf_op jit(solution)/shard_map/ppermute | solution.py:274
Sparse Core Ops, SparseCore 0:
  10.7 52.7 all-gather.2

commit v2 on v0

v2 whole, which is shorter than its diff:
```python
import jax
import jax.numpy as jnp
from jax import lax
from jax.experimental import pallas as pl
from jax.experimental.pallas import tpu as pltpu
from jax.sharding import PartitionSpec as P

STEPS = 3
B = 256
SUB = 8
PANEL = 32
GROUP = 4
VMEM = pl.BlockSpec(memory_space=pltpu.VMEM)
ANY = pl.BlockSpec(memory_space=pl.ANY)
F32 = jnp.float32
BF16 = jnp.bfloat16
HIGHEST = lax.Precision.HIGHEST


def dot_nt(a, b, precision=None):
    return lax.dot_general(
        a, b, (((1,), (1,)), ((), ())), precision=precision, preferred_element_type=F32
    )


def wide(v):
    return jnp.concatenate([v, v], axis=1)


def tree_sum(terms):
    terms = list(terms)
    while len(terms) > 1:
        pairs = [terms[i : i + 2] for i in range(0, len(terms), 2)]
        terms = [p[0] + p[1] if len(p) == 2 else p[0] for p in pairs]
    return terms[0]


def small_ldl(e):
    m = [[None] * SUB for _ in range(SUB)]
    rc = [None] * SUB
    for k in range(SUB):
        rc[k] = 1.0 / e[k][k]
        for a in range(k + 1, SUB):
            m[a][k] = e[a][k] * rc[k]
        for a in range(k + 1, SUB):
            for b in range(k + 1, a + 1):
                e[a][b] = e[a][b] - m[a][k] * e[b][k]
    inv = [[None] * SUB for _ in range(SUB)]
    for b in range(SUB):
        for a in range(b + 1, SUB):
            v = m[a][b]
            for c in range(b + 1, a):
                v = v + m[a][c] * inv[c][b]
            inv[a][b] = -v
    return inv, rc, [e[k][k] for k in range(SUB)]


def factor_tiles(tiles, b0):
    count = len(tiles)
    lane = lax.broadcasted_iota(jnp.int32, (SUB, B), 1)
    sub = lax.broadcasted_iota(jnp.int32, (SUB, B), 0)
    narrow = lax.broadcasted_iota(jnp.int32, (SUB, 128), 0)
    tiles = list(tiles)
    keep = []
    update = []
    for i in range(count):
        k0 = b0 + SUB * i
        x = tiles[i]
        e = [[None] * SUB for _ in range(SUB)]
        for a in range(SUB):
            for b in range(a + 1):
                e[a][b] = jnp.broadcast_to(x[a : a + 1, k0 + b : k0 + b + 1], (SUB, 128))
        inv, rc, d = small_ldl(e)
        cols = []
        for b in range(SUB):
            v = jnp.where(narrow == b, 1.0, 0.0)
            for a in range(b + 1, SUB):
                v = jnp.where(narrow == a, inv[a][b], v)
            cols.append(v)
        pivot = d[0]
        for a in range(1, SUB):
            pivot = jnp.where(narrow == a, d[a], pivot)
        scale = wide(lax.rsqrt(pivot))
        r = tree_sum(
            wide(cols[b]) * jnp.broadcast_to(x[b : b + 1, :], (SUB, B)) for b in range(SUB)
        )
        z = 0.0
        for b in range(SUB):
            z = jnp.where(lane == k0 + b, wide(cols[b]), z)
        in_block = (lane >= k0) & (lane < k0 + SUB)
        y = jnp.where(in_block, z, r)
        if i < count - 1:
            rows = []
            for a in range(SUB):
                v = jnp.where(narrow == a, rc[a], 0.0)
                for b in range(a):
                    v = jnp.where(narrow == b, inv[a][b] * rc[a], v)
                rows.append(v)
            g = tree_sum(
                wide(rows[a]) * jnp.broadcast_to(y[a : a + 1, :], (SUB, B)) for a in range(SUB)
            )
            for j in range(i + 1, count):
                t = tiles[j]
                tiles[j] = jnp.where(in_block, 0.0, t) - tree_sum(
                    jnp.broadcast_to(t[:, k0 + b : k0 + b + 1], (SUB, B))
                    * jnp.broadcast_to(g[b : b + 1, :], (SUB, B))
                    for b in range(SUB)
                )
        scaled = y * scale
        keep.append(jnp.where(in_block & (lane > k0 + sub), r * scale, scaled))
        later = (lane >= k0 + SUB) & (lane < b0 + SUB * count)
        update.append(jnp.where(later, 0.0, scaled))
    return keep, update


def cholesky_in_place(t_ref):
    count = PANEL // SUB
    tiles = [t_ref[SUB * i : SUB * (i + 1), :] for i in range(count)]
    for b0 in range(0, B, PANEL):
        b1 = b0 + PANEL
        keep, update = factor_tiles(tiles, b0)
        for i in range(count):
            t_ref[b0 + SUB * i : b0 + SUB * (i + 1), :] = keep[i]
        if b1 == B:
            break
        right = jnp.concatenate(update, axis=0)
        left = right.T

        def below(lo, hi):
            lanes = lax.broadcasted_iota(jnp.int32, (hi - lo, B), 1)
            old = jnp.where((lanes >= b0) & (lanes < b1), 0.0, t_ref[lo:hi, :])
            return old - jnp.dot(
                left[lo:hi], right, precision=HIGHEST, preferred_element_type=F32
            )

        ahead = below(b1, b1 + PANEL)
        tiles = [ahead[SUB * i : SUB * (i + 1), :] for i in range(count)]
        if b1 + PANEL < B:
            t_ref[b1 + PANEL :, :] = below(b1 + PANEL, B)


def factor_block(d, t_ref, low_ref, inv_ref, s):
    t_ref[...] = 0.5 * (d + d.T)
    cholesky_in_place(t_ref)
    t = t_ref[...]
    ri = lax.broadcasted_iota(jnp.int32, (B, B), 0)
    ci = lax.broadcasted_iota(jnp.int32, (B, B), 1)
    inv = jnp.where(ci <= ri, t, 0.0)
    inv_ref[s] = inv
    low_ref[s] = jnp.where(ci > ri, t, jnp.where(ci == ri, 1.0 / t, 0.0)).T
    return inv


def first_kernel(a_ref, low_ref, inv_ref, t_ref):
    factor_block(a_ref[...].astype(F32), t_ref, low_ref, inv_ref, 0)


def factor_first(block):
    return pl.pallas_call(
        first_kernel,
        in_specs=[VMEM],
        out_specs=[VMEM, VMEM],
        out_shape=[jax.ShapeDtypeStruct((1, B, B), F32)] * 2,
        scratch_shapes=[pltpu.VMEM((B, B), F32)],
        compiler_params=pltpu.CompilerParams(vmem_limit_bytes=40 << 20),
        cost_estimate=pl.CostEstimate(
            flops=10_000_000_000, bytes_accessed=1 << 20, transcendentals=0
        ),
    )(block)


def rest_kernel(a_ref, inv0_ref, low_ref, inv_ref, pan_ref, w_ref, t_ref):
    inv = inv0_ref[0]
    w_ref[...] = a_ref[...].astype(F32)
    for s in range(STEPS - 1):
        panels = []
        for r in range(s + 1, STEPS):
            w = w_ref[(r - 1) * B : r * B, s * B : (s + 1) * B]
            panel = dot_nt(w, inv, HIGHEST).astype(BF16)
            panels.append(panel)
            pan_ref[s + r - 1] = panel
        for r in range(s + 1, STEPS):
            for c in range(s + 1, r + 1):
                w_ref[(r - 1) * B : r * B, c * B : (c + 1) * B] -= dot_nt(
                    panels[r - s - 1], panels[c - s - 1]
                )
        d = w_ref[s * B : (s + 1) * B, (s + 1) * B : (s + 2) * B]
        inv = factor_block(d, t_ref, low_ref, inv_ref, s)


def factor_rest(rows, inv0):
    return pl.pallas_call(
        rest_kernel,
        in_specs=[VMEM, VMEM],
        out_specs=[VMEM, VMEM, VMEM],
        out_shape=[
            jax.ShapeDtypeStruct((STEPS - 1, B, B), F32),
            jax.ShapeDtypeStruct((STEPS - 1, B, B), F32),
            jax.ShapeDtypeStruct((STEPS, B, B), BF16),
        ],
        scratch_shapes=[pltpu.VMEM(((STEPS - 1) * B, STEPS * B), F32), pltpu.VMEM((B, B), F32)],
        compiler_params=pltpu.CompilerParams(vmem_limit_bytes=40 << 20),
        cost_estimate=pl.CostEstimate(
            flops=20_000_000_000, bytes_accessed=4 << 20, transcendentals=0
        ),
    )(rows, inv0)


def split(x):
    high = x.astype(BF16)
    return high, (x - high.astype(F32)).astype(BF16)


def solve_own(a, invs, pan_ref):
    solved = []
    panels = []
    for t in range(STEPS):
        w = a[:, t * B : (t + 1) * B].astype(F32)
        for s in range(t):
            w = w - dot_nt(panels[s], pan_ref[t + s - 1])
        x = dot_nt(w, invs[t], HIGHEST)
        solved.append(x)
        panels.append(x.astype(BF16))
    return solved, panels


def solve_panels(a, parts_ref, pan_ref):
    panels = []
    for t in range(STEPS):
        w = a[:, t * B : (t + 1) * B]
        high, low = parts_ref[t, 0], parts_ref[t, 1]
        if t == 0:
            x = dot_nt(w, high) + dot_nt(w, low)
        else:
            w = w.astype(F32)
            for s in range(t):
                w = w - dot_nt(panels[s], pan_ref[t + s - 1])
            wh, wl = split(w)
            x = dot_nt(wh, high) + (dot_nt(wl, high) + dot_nt(wh, low))
        panels.append(x.astype(BF16))
    return panels


def update_kernel(
    scalars,
    own_ref,
    all_ref,
    low0_ref,
    inv0_ref,
    low_ref,
    inv_ref,
    pan_ref,
    factor_ref,
    u_ref,
    mine_ref,
    parts_ref,
    rows_ref,
    out_ref,
    in_sems,
    out_sems,
):
    groups = u_ref.shape[0] // GROUP

    def fetch(i):
        part = pl.ds(i * GROUP, GROUP)
        return pltpu.make_async_copy(all_ref.at[part], rows_ref.at[part], in_sems.at[i])

    def send(i):
        part = pl.ds(i * GROUP, GROUP)
        return pltpu.make_async_copy(out_ref.at[part], u_ref.at[part], out_sems.at[i])

    for i in range(groups):
        fetch(i).start()
    pivots = scalars[0]
    row = scalars[1]
    lows = [low0_ref[0], low_ref[0], low_ref[1]]
    invs = [inv0_ref[0], inv_ref[0], inv_ref[1]]
    solved, panels = solve_own(own_ref[...], invs, pan_ref)
    for t in range(STEPS):
        active = t < pivots
        block = jnp.where(row > t, solved[t], jnp.where(row == t, lows[t], 0.0))
        factor_ref[:, t * B : (t + 1) * B] = jnp.where(active, block, 0.0)
        mine_ref[:, t * B : (t + 1) * B] = jnp.where(active, panels[t], 0.0).astype(BF16)
        parts_ref[t, 0], parts_ref[t, 1] = split(invs[t])

    def group(i, carry):
        fetch(i).wait()
        a = rows_ref[pl.ds(i * GROUP, GROUP)].reshape(GROUP * B, STEPS * B)
        panels = solve_panels(a, parts_ref, pan_ref)
        other = jnp.concatenate(
            [jnp.where(t < pivots, panels[t], 0.0).astype(BF16) for t in range(STEPS)], axis=1
        )
        for k in range(GROUP):
            out_ref[i * GROUP + k] = dot_nt(
                mine_ref[...], other[k * B : (k + 1) * B]
            ).astype(BF16)
        send(i).start()
        return carry

    lax.fori_loop(0, groups, group, 0)
    for i in range(groups):
        send(i).wait()


def solve_and_update(scalars, own, gathered, low0, inv0, low, inv, pan):
    blocks = gathered.shape[0]
    return pl.pallas_call(
        update_kernel,
        in_specs=[pl.BlockSpec(memory_space=pltpu.SMEM), VMEM, ANY] + [VMEM] * 5,
        out_specs=[VMEM, ANY],
        out_shape=[
            jax.ShapeDtypeStruct((B, STEPS * B), F32),
            jax.ShapeDtypeStruct((blocks, B, B), BF16),
        ],
        scratch_shapes=[
            pltpu.VMEM((B, STEPS * B), BF16),
            pltpu.VMEM((STEPS, 2, B, B), BF16),
            pltpu.VMEM((blocks, B, STEPS * B), BF16),
            pltpu.VMEM((blocks, B, B), BF16),
            pltpu.SemaphoreType.DMA((blocks // GROUP,)),
            pltpu.SemaphoreType.DMA((blocks // GROUP,)),
        ],
        compiler_params=pltpu.CompilerParams(vmem_limit_bytes=48 << 20),
        cost_estimate=pl.CostEstimate(
            flops=16_000_000_000, bytes_accessed=10 << 20, transcendentals=0
        ),
    )(scalars, own, gathered, low0, inv0, low, inv, pan)


def relayout_kernel(x_ref, y_ref, sems):
    copies = [
        pltpu.make_async_copy(x_ref.at[:, j * B : (j + 1) * B], y_ref.at[j], sems.at[j])
        for j in range(y_ref.shape[0])
    ]
    for copy in copies:
        copy.start()
    for copy in copies:
        copy.wait()


def block_columns(front):
    blocks = front.shape[1] // B
    return pl.pallas_call(
        relayout_kernel,
        in_specs=[ANY],
        out_specs=ANY,
        out_shape=jax.ShapeDtypeStruct((blocks, B, B), front.dtype),
        scratch_shapes=[pltpu.SemaphoreType.DMA((blocks,))],
        cost_estimate=pl.CostEstimate(flops=0, bytes_accessed=4 << 20, transcendentals=0),
    )(front)


def start_sum_kernel(slots, x_ref, anc_ref, acc_ref):
    k = pl.program_id(0)

    @pl.when(k == 0)
    def _():
        acc_ref[0:2] = anc_ref[...].astype(F32)
        acc_ref[2:4] = jnp.zeros((2, B, B), F32)

    for i in range(GROUP):
        slot = slots[k * GROUP + i]

        @pl.when(slot < 4)
        def _(i=i, slot=slot):
            acc_ref[slot] += x_ref[i].astype(F32)


def end_sum_kernel(slots, x_ref, start_ref, acc_ref):
    k = pl.program_id(0)

    @pl.when(k == 0)
    def _():
        acc_ref[...] = start_ref[...]

    for i in range(GROUP):
        slot = slots[k * GROUP + i]

        @pl.when(slot < 4)
        def _(i=i, slot=slot):
            acc_ref[slot] -= x_ref[i].astype(F32)


def sum_blocks(kernel, slots, x, start):
    return pl.pallas_call(
        kernel,
        grid=(x.shape[0] // GROUP,),
        in_specs=[
            pl.BlockSpec(memory_space=pltpu.SMEM),
            pl.BlockSpec((GROUP, B, B), lambda k: (k, 0, 0)),
            pl.BlockSpec(start.shape, lambda k: (0, 0, 0)),
        ],
        out_specs=pl.BlockSpec((4, B, B), lambda k: (0, 0, 0)),
        out_shape=jax.ShapeDtypeStruct((4, B, B), F32),
        compiler_params=pltpu.CompilerParams(vmem_limit_bytes=40 << 20),
        cost_estimate=pl.CostEstimate(
            flops=4_000_000_000, bytes_accessed=4 << 20, transcendentals=0
        ),
    )(slots, x, start)


def broadcast_first(block, row):
    size = lax.axis_size("row")
    step = size // 2
    while step:
        pairs = [(i, i + step) for i in range(0, size, 2 * step)]
        got = lax.ppermute(block, "row", pairs)
        block = jnp.where(row % (2 * step) == step, got, block)
        step //= 2
    return block


def shards(fronts, pivots, targets, ancestor):
    row = lax.axis_index("row")
    col = lax.axis_index("col")
    cols = lax.axis_size("col")
    blocks = fronts.shape[2] // B
    half = cols // 2
    groups = [list(range(half)), list(range(half, cols))]
    front = fronts[0]

    side = col // half
    block_col = col % half
    first = side * half
    piv = lax.dynamic_slice_in_dim(pivots, first, half)
    tgt = lax.dynamic_slice_in_dim(targets, first, half, axis=0)
    col_half = lax.dynamic_index_in_dim(tgt, block_col, 1, keepdims=False) // blocks
    row_half = lax.dynamic_index_in_dim(tgt, row, 1, keepdims=False) // blocks
    keep = (block_col >= piv) & (row >= piv)
    slots = jnp.where(keep, jnp.where(col_half == side, 0, 2) + row_half, 4).astype(jnp.int32)
    scalars = jnp.stack([pivots[col], row.astype(jnp.int32)])

    own, corner = lax.optimization_barrier((front[:, : STEPS * B], front[:, :B]))
    gathered = lax.all_gather(own, "row", axis=0, tiled=False)
    corner = broadcast_first(corner, row)
    low0, inv0 = factor_first(corner)
    f = lax.all_to_all(
        block_columns(front), "col", 0, 0, axis_index_groups=groups, tiled=True
    )

    low, inv, pan = factor_rest(gathered[1:STEPS].reshape((STEPS - 1) * B, STEPS * B), inv0)
    factor, u = solve_and_update(scalars, own, gathered, low0, inv0, low, inv, pan)
    u = lax.all_to_all(u, "col", 0, 0, axis_index_groups=groups, tiled=True)

    acc = sum_blocks(start_sum_kernel, slots, f, ancestor)
    acc = sum_blocks(end_sum_kernel, slots, u, acc)
    received = lax.ppermute(acc[2:4], "col", [(c, (c + half) % cols) for c in range(cols)])
    return factor[None], acc[0:2] + received


def solution(mesh):
    in_specs = (P("col", "row", None), P(), P(), P(None, "row", "col"))
    out_specs = (P("col", "row", None), P(None, "row", "col"))
    return jax.shard_map(shards, mesh=mesh, in_specs=in_specs, out_specs=out_specs, check_vma=False)
```

time: 958 us -> 240 us (0.25)
  the two profiles are of different devices: /device:TPU:215 before, /device:TPU:124 now
where the time goes in v2:
time: 240 us
  Pallas kernels  118 us (49%)
  waiting for transfers between devices  71.2 us (30%)
  starting transfers between devices  28.2 us (12%)
  between operations  14.3 us (6%)
  local copies, waits for them, and re-layouts  5.84 us (2%)
  other arithmetic  2.43 us (1%)
    pallas_call x1, Pallas kernels, block_columns(): pl.pallas_call(relayout_kernel, in_specs=[ANY], out_specs=ANY, out_shape=...  67.1 us
    all_to_all x1, waiting for transfers between devices, shards(): u = lax.all_to_all(u, 'col', 0, 0, axis_index_groups=groups, tiled=True)  35.8 us
    ppermute x4, waiting for transfers between devices, broadcast_first(): got = lax.ppermute(block, 'row', pairs)  22.6 us
    pallas_call x1, Pallas kernels, factor_rest(): pl.pallas_call(rest_kernel, in_specs=[VMEM, VMEM], out_specs=[VMEM, VMEM,...  20.5 us
    pallas_call x1, Pallas kernels, solve_and_update(): pl.pallas_call(update_kernel, in_specs=[pl.BlockSpec(memory_space=pltpu.S...  17 us
    ppermute x1, waiting for transfers between devices, shards(): lax.ppermute(acc[2:4], 'col', [(c, (c + half) % cols) for c in range(cols)])  12.8 us
    pallas_call x1, Pallas kernels, factor_first(): pl.pallas_call(first_kernel, in_specs=[VMEM], out_specs=[VMEM, VMEM], out...  9.43 us
    ppermute x1, starting transfers between devices, shards(): lax.ppermute(acc[2:4], 'col', [(c, (c + half) % cols) for c in range(cols)])  8.68 us
  transfers between devices with their start and end apart: 8, of which 3 were waited for; matrix products, arithmetic and copies ran while one was open for 1% of the time, Pallas kernels for 48%

profile of v2, /device:TPU:124, one launch (start us, length us, event | category | flops | bytes accessed | tf_op | source)
XLA Modules:
  0.0 239.8 jit_solution(12885641118496453258)
XLA Ops:
  7.2 0.0 all-gather.3.cloned.1.call-start
  7.2 0.9 slice.22
  8.1 1.8 slice.21.own_ref
  9.9 0.0 all-gather.3.cloned.1.call-update
  9.9 0.7 collective-permute-start
  10.6 0.0 collective-permute-done
  10.6 0.7 collective-permute-start.1
  11.3 0.0 collective-permute-done.1
  11.4 1.3 collective-permute-start.2
  12.7 22.6 %collective-permute-done.2 = bf16[256,256]{1,0:T(8,128)(2,1)S(1)} collective-permute-done((bf16[256,256]{1,0:T(8,128)(2,1)S(1)}, bf16[256,256]{1,0:T(8,128)(2,1)S(1)}, u32[]{:S(2)}, u32[]{:S(2)}) %collective-permute-start.2) | collective-permute-done | bytes 131104 | tf_op jit(solution)/shard_map/ppermute | solution.py:407
  35.3 1.3 collective-permute-start.3
  36.6 67.1 %shard_map.62 = bf16[16,256,256]{2,1,0:T(8,128)(2,1)} custom-call(bf16[256,4096]{1,0:T(8,128)(2,1)} %bitcast.26), custom_call_target="tpu_custom_call" | custom-call | bytes 4194304 | tf_op jit(solution)/shard_map/pallas_call | solution.py:343
  103.7 0.0 copy-start.3
  103.7 7.9 %all-to-all-start.1 = ((bf16[16,256,256]{2,1,0:T(8,128)(2,1)}), bf16[16,256,256]{2,1,0:T(8,128)(2,1)S(1)}, u32[]{:S(2)}, u32[]{:S(2)}) async-start(bf16[16,256,256]{2,1,0:T(8,128)(2,1)} %shard_map.62), calls=%async_computation.1 | async-start | bytes 4194304 | tf_op jit(solution)/shard_map/all_to_all | solution.py:437
  111.6 0.0 copy-done.3
  111.6 0.6 dynamic_slice.14
  112.2 0.7 pad_add_fusion.scalars
  112.9 0.0 collective-permute-done.3
  113.0 9.4 %shard_map.59 = (f32[1,256,256]{2,1,0:T(8,128)S(1)}, f32[1,256,256]{2,1,0:T(8,128)S(1)}) custom-call(bf16[256,256]{1,0:T(8,128)(2,1)S(1)} %broadcast_select_fusion.3.a_ref), custom_call_target="tpu_custom_call" | custom-call | flops 10000000000 | bytes 1048576 | tf_op jit(solution)/shard_map/pallas_call | solution.py:159
  122.4 0.0 all-gather.3.cloned.1.call-done
  122.4 1.2 slice.23.a_ref
  123.6 0.0 copy-start.1
  123.6 20.5 %shard_map.60 = (f32[2,256,256]{2,1,0:T(8,128)S(1)}, f32[2,256,256]{2,1,0:T(8,128)S(1)}, bf16[3,256,256]{2,1,0:T(8,128)(2,1)S(1)}) custom-call(bf16[512,768]{1,0:T(8,128)(2,1)S(1)} %slice.23.a_ref, f32[1,256,256]{2,1,0:T(8,128)S(1)} %get-tuple-element.14.inv0_ref), custom_call_target="tpu_custom_call" | custom-call | flops 20000000000 | bytes 4194304 | tf_op jit(solution)/shard_map/pallas_call | solution.py:192
  144.1 0.0 copy-done.1
  144.1 17.0 %shard_map.61 = (f32[256,768]{1,0:T(8,128)}, bf16[16,256,256]{2,1,0:T(8,128)(2,1)S(1)}) custom-call(s32[2]{0:T(128)S(1)} %pad_add_fusion.scalars, bf16[256,768]{1,0:T(8,128)(2,1)S(1)} %copy-done.1, bf16[16,256,768]{2,1,0:T(8,128)(2,1)} %bitcast.27, f32[1,256,256]{2,1,0:T(8,128)S(1)} %get-tuple-element.13.low0_ref, ...), custom_call_target="tpu_custom_call" | custom-call | flops 16000000000 | bytes 10485760 | tf_op jit(solution)/shard_map/pallas_call | solution.py:307
  161.1 0.0 copy-start
  161.1 1.3 copy-done
  162.4 0.0 all-to-all-done.1.x_ref
  162.4 0.0 copy-start.2
  162.4 7.7 %all-to-all-start = ((bf16[16,256,256]{2,1,0:T(8,128)(2,1)}), bf16[16,256,256]{2,1,0:T(8,128)(2,1)}, u32[]{:S(2)}, u32[]{:S(2)}) async-start(bf16[16,256,256]{2,1,0:T(8,128)(2,1)} %copy-done), calls=%async_computation | async-start | bytes 4194304 | tf_op jit(solution)/shard_map/all_to_all | solution.py:443
  170.1 0.8 and_select_fusion.2.slots
  170.9 0.0 copy-done.2
  170.9 1.2 shard_map.63.start_ref
  172.1 35.8 %all-to-all-done.x_ref = bf16[16,256,256]{2,1,0:T(8,128)(2,1)} async-done(((bf16[16,256,256]{2,1,0:T(8,128)(2,1)}), bf16[16,256,256]{2,1,0:T(8,128)(2,1)}, u32[]{:S(2)}, u32[]{:S(2)}) %all-to-all-start) | async-done | bytes 2097184 | tf_op jit(solution)/shard_map/all_to_all | solution.py:443
  207.9 2.6 %shard_map.64 = f32[4,256,256]{2,1,0:T(8,128)S(1)} custom-call(s32[16]{0:T(128)S(1)} %and_select_fusion.2.slots, bf16[16,256,256]{2,1,0:T(8,128)(2,1)} %all-to-all-done.x_ref, f32[4,256,256]{2,1,0:T(8,128)S(1)} %shard_map.63.start_ref), custom_call_target="tpu_custom_call" | custom-call | flops 4000000000 | bytes 4194304 | tf_op jit(solution)/shard_map/pallas_call | solution.py:385
  210.6 8.7 %collective-permute-start.4 = (f32[2,256,256]{2,1,0:T(8,128)S(1)}, f32[2,256,256]{2,1,0:T(8,128)S(1)}, u32[]{:S(2)}, u32[]{:S(2)}) collective-permute-start(f32[2,256,256]{2,1,0:T(8,128)S(1)} %slice.25), channel_id=1, source_target_pairs={{0,16},{1,17},{2,18},{3,19},{4,20},{5,21},{6,22},{7,23},{8,24},{9,... | collective-permute-start | bytes 1572872 | tf_op jit(solution)/shard_map/ppermute | solution.py:447
  219.3 12.8 %collective-permute-done.4 = f32[2,256,256]{2,1,0:T(8,128)S(1)} collective-permute-done((f32[2,256,256]{2,1,0:T(8,128)S(1)}, f32[2,256,256]{2,1,0:T(8,128)S(1)}, u32[]{:S(2)}, u32[]{:S(2)}) %collective-permute-start.4) | collective-permute-done | bytes 524320 | tf_op jit(solution)/shard_map/ppermute | solution.py:447
  232.1 0.9 slice_add_fusion
  (5 shorter events, 0.1 us)
Async XLA Ops:
  7.2 115.2 %all-gather.3.cloned.1.call-start = ((), (), s32[]{:S(2)}) async-start(), calls=%async_computation.2 | async-start | bytes 6684672 | tf_op jit(solution)/shard_map/all_gather | solution.py:434
  9.9 0.7 collective-permute-start
  10.6 0.7 collective-permute-start.1
  11.4 23.9 %collective-permute-start.2 = (bf16[256,256]{1,0:T(8,128)(2,1)S(1)}, bf16[256,256]{1,0:T(8,128)(2,1)S(1)}, u32[]{:S(2)}, u32[]{:S(2)}) collective-permute-start(bf16[256,256]{1,0:T(8,128)(2,1)S(1)} %broadcast_select_fusion.1), channel_id=1, source_target_pairs={{0,64},{128,192},{256,320},{384,448},{1,65},{129,193},{257,321},{3... | collective-permute-start | bytes 393224 | tf_op jit(solution)/shard_map/ppermute | solution.py:407
  35.3 77.6 %collective-permute-start.3 = (bf16[256,256]{1,0:T(8,128)(2,1)S(1)}, bf16[256,256]{1,0:T(8,128)(2,1)S(1)}, u32[]{:S(2)}, u32[]{:S(2)}) collective-permute-start(bf16[256,256]{1,0:T(8,128)(2,1)S(1)} %broadcast_select_fusion.2), channel_id=1, source_target_pairs={{0,32},{64,96},{128,160},{192,224},{256,288},{320,352},{384,416},{... | collective-permute-start | bytes 393224 | tf_op jit(solution)/shard_map/ppermute | solution.py:407
  103.7 7.9 %copy-start.3 = (s32[32]{0:T(128)S(1)}, s32[32]{0:T(128)}, u32[]{:S(2)}) copy-start(s32[32]{0:T(128)} %param.5) | copy-start | bytes 388
  103.7 58.7 %all-to-all-start.1 = ((bf16[16,256,256]{2,1,0:T(8,128)(2,1)}), bf16[16,256,256]{2,1,0:T(8,128)(2,1)S(1)}, u32[]{:S(2)}, u32[]{:S(2)}) async-start(bf16[16,256,256]{2,1,0:T(8,128)(2,1)} %shard_map.62), calls=%async_computation.1 | async-start | bytes 4194304 | tf_op jit(solution)/shard_map/all_to_all | solution.py:437
  123.6 20.5 %copy-start.1 = (bf16[256,768]{1,0:T(8,128)(2,1)S(1)}, bf16[256,768]{1,0:T(8,128)(2,1)}, u32[]{:S(2)}) copy-start(bf16[256,768]{1,0:T(8,128)(2,1)} %slice.21.own_ref) | copy-start | bytes 1179652
  161.1 1.3 copy-start
  162.4 8.5 %copy-start.2 = (bf16[2,256,256]{2,1,0:T(8,128)(2,1)S(1)}, bf16[2,256,256]{2,1,0:T(8,128)(2,1)}, u32[]{:S(2)}) copy-start(bf16[2,256,256]{2,1,0:T(8,128)(2,1)} %anc_ref.1) | copy-start | bytes 786436
  162.4 45.5 %all-to-all-start = ((bf16[16,256,256]{2,1,0:T(8,128)(2,1)}), bf16[16,256,256]{2,1,0:T(8,128)(2,1)}, u32[]{:S(2)}, u32[]{:S(2)}) async-start(bf16[16,256,256]{2,1,0:T(8,128)(2,1)} %copy-done), calls=%async_computation | async-start | bytes 4194304 | tf_op jit(solution)/shard_map/all_to_all | solution.py:443
  210.6 21.5 %collective-permute-start.4 = (f32[2,256,256]{2,1,0:T(8,128)S(1)}, f32[2,256,256]{2,1,0:T(8,128)S(1)}, u32[]{:S(2)}, u32[]{:S(2)}) collective-permute-start(f32[2,256,256]{2,1,0:T(8,128)S(1)} %slice.25), channel_id=1, source_target_pairs={{0,16},{1,17},{2,18},{3,19},{4,20},{5,21},{6,22},{7,23},{8,24},{9,... | collective-permute-start | bytes 1572872 | tf_op jit(solution)/shard_map/ppermute | solution.py:447
Sparse Core Ops, SparseCore 0:
  10.7 51.9 all-gather.2

commit v3 on v2

--- a/solution.py
+++ b/solution.py
@@ -327,25 +327,19 @@
     )(scalars, own, gathered, low0, inv0, low, inv, pan)
 
 
-def relayout_kernel(x_ref, y_ref, sems):
-    copies = [
-        pltpu.make_async_copy(x_ref.at[:, j * B : (j + 1) * B], y_ref.at[j], sems.at[j])
-        for j in range(y_ref.shape[0])
-    ]
-    for copy in copies:
-        copy.start()
-    for copy in copies:
-        copy.wait()
+def relayout_kernel(x_ref, y_ref):
+    for i in range(GROUP):
+        y_ref[i] = x_ref[:, i * B : (i + 1) * B]
 
 
 def block_columns(front):
     blocks = front.shape[1] // B
     return pl.pallas_call(
         relayout_kernel,
-        in_specs=[ANY],
-        out_specs=ANY,
+        grid=(blocks // GROUP,),
+        in_specs=[pl.BlockSpec((B, GROUP * B), lambda j: (0, j))],
+        out_specs=pl.BlockSpec((GROUP, B, B), lambda j: (j, 0, 0)),
         out_shape=jax.ShapeDtypeStruct((blocks, B, B), front.dtype),
-        scratch_shapes=[pltpu.SemaphoreType.DMA((blocks,))],
         cost_estimate=pl.CostEstimate(flops=0, bytes_accessed=4 << 20, transcendentals=0),
     )(front)
 

time: 240 us -> 201 us (0.84)
  the two profiles are of different devices: /device:TPU:124 before, /device:TPU:69 now
where the time goes in v3:
time: 201 us
  waiting for transfers between devices  98.1 us (49%)
  Pallas kernels  54.3 us (27%)
  starting transfers between devices  25.8 us (13%)
  between operations  14.2 us (7%)
  local copies, waits for them, and re-layouts  5.84 us (3%)
  other arithmetic  2.49 us (1%)
    all_to_all x1, waiting for transfers between devices, shards(): u = lax.all_to_all(u, 'col', 0, 0, axis_index_groups=groups, tiled=True)  45.6 us
    all_gather x1, waiting for transfers between devices, shards(): gathered = lax.all_gather(own, 'row', axis=0, tiled=False)  24.7 us
    ppermute x1, waiting for transfers between devices, shards(): lax.ppermute(acc[2:4], 'col', [(c, (c + half) % cols) for c in range(cols)])  24.6 us
    pallas_call x1, Pallas kernels, factor_rest(): pl.pallas_call(rest_kernel, in_specs=[VMEM, VMEM], out_specs=[VMEM, VMEM,...  20.5 us
    pallas_call x1, Pallas kernels, solve_and_update(): pl.pallas_call(update_kernel, in_specs=[pl.BlockSpec(memory_space=pltpu.S...  17 us
    pallas_call x1, Pallas kernels, factor_first(): pl.pallas_call(first_kernel, in_specs=[VMEM], out_specs=[VMEM, VMEM], out...  9.43 us
    all_to_all x1, starting transfers between devices, shards(): lax.all_to_all(block_columns(front), 'col', 0, 0, axis_index_groups=group...  8.91 us
    all_to_all x1, starting transfers between devices, shards(): u = lax.all_to_all(u, 'col', 0, 0, axis_index_groups=groups, tiled=True)  7.4 us
  transfers between devices with their start and end apart: 8, of which 4 were waited for; matrix products, arithmetic and copies ran while one was open for 2% of the time, Pallas kernels for 26%

profile of v3, /device:TPU:69, one launch (start us, length us, event | category | flops | bytes accessed | tf_op | source)
XLA Modules:
  0.0 200.8 jit_solution(11800901090796564167)
XLA Ops:
  7.2 0.0 all-gather.3.cloned.1.call-start
  7.2 0.9 slice.22
  8.1 1.8 slice.21.own_ref
  9.9 0.0 all-gather.3.cloned.1.call-update
  9.9 0.7 collective-permute-start
  10.6 0.0 collective-permute-done
  10.6 0.7 collective-permute-start.1
  11.3 0.0 collective-permute-done.1
  11.4 0.7 collective-permute-start.2
  12.1 0.0 collective-permute-done.2
  12.1 1.3 collective-permute-start.3
  13.4 3.8 %shard_map.62 = bf16[16,256,256]{2,1,0:T(8,128)(2,1)} custom-call(bf16[256,4096]{1,0:T(8,128)(2,1)} %bitcast.26), custom_call_target="tpu_custom_call" | custom-call | bytes 4194304 | tf_op jit(solution)/shard_map/pallas_call | solution.py:337
  17.2 0.0 copy-start.3
  17.2 8.9 %all-to-all-start.1 = ((bf16[16,256,256]{2,1,0:T(8,128)(2,1)}), bf16[16,256,256]{2,1,0:T(8,128)(2,1)S(1)}, u32[]{:S(2)}, u32[]{:S(2)}) async-start(bf16[16,256,256]{2,1,0:T(8,128)(2,1)} %shard_map.62), calls=%async_computation.1 | async-start | bytes 4194304 | tf_op jit(solution)/shard_map/all_to_all | solution.py:431
  26.1 0.0 copy-done.3
  26.2 0.6 dynamic_slice.14
  26.7 0.7 pad_add_fusion.scalars
  27.5 3.2 %collective-permute-done.3 = bf16[256,256]{1,0:T(8,128)(2,1)S(1)} collective-permute-done((bf16[256,256]{1,0:T(8,128)(2,1)S(1)}, bf16[256,256]{1,0:T(8,128)(2,1)S(1)}, u32[]{:S(2)}, u32[]{:S(2)}) %collective-permute-start.3) | collective-permute-done | bytes 131104 | tf_op jit(solution)/shard_map/ppermute | solution.py:401
  30.6 9.4 %shard_map.59 = (f32[1,256,256]{2,1,0:T(8,128)S(1)}, f32[1,256,256]{2,1,0:T(8,128)S(1)}) custom-call(bf16[256,256]{1,0:T(8,128)(2,1)S(1)} %broadcast_select_fusion.3.a_ref), custom_call_target="tpu_custom_call" | custom-call | flops 10000000000 | bytes 1048576 | tf_op jit(solution)/shard_map/pallas_call | solution.py:159
  40.1 24.7 %all-gather.3.cloned.1.call-done = bf16[4096,768]{1,0:T(8,128)(2,1)} async-done(((bf16[256,768]{1,0:T(8,128)(2,1)}), bf16[4096,768]{1,0:T(8,128)(2,1)}) %all-gather.3.cloned.1.call-update) | async-done | bytes 6291472 | tf_op jit(solution)/shard_map/all_gather | solution.py:428
  64.7 1.2 slice.23.a_ref
  65.9 0.0 copy-start.1
  65.9 20.5 %shard_map.60 = (f32[2,256,256]{2,1,0:T(8,128)S(1)}, f32[2,256,256]{2,1,0:T(8,128)S(1)}, bf16[3,256,256]{2,1,0:T(8,128)(2,1)S(1)}) custom-call(bf16[512,768]{1,0:T(8,128)(2,1)S(1)} %slice.23.a_ref, f32[1,256,256]{2,1,0:T(8,128)S(1)} %get-tuple-element.14.inv0_ref), custom_call_target="tpu_custom_call" | custom-call | flops 20000000000 | bytes 4194304 | tf_op jit(solution)/shard_map/pallas_call | solution.py:192
  86.4 0.0 copy-done.1
  86.4 17.0 %shard_map.61 = (f32[256,768]{1,0:T(8,128)}, bf16[16,256,256]{2,1,0:T(8,128)(2,1)S(1)}) custom-call(s32[2]{0:T(128)S(1)} %pad_add_fusion.scalars, bf16[256,768]{1,0:T(8,128)(2,1)S(1)} %copy-done.1, bf16[16,256,768]{2,1,0:T(8,128)(2,1)} %bitcast.27, f32[1,256,256]{2,1,0:T(8,128)S(1)} %get-tuple-element.13.low0_ref, ...), custom_call_target="tpu_custom_call" | custom-call | flops 16000000000 | bytes 10485760 | tf_op jit(solution)/shard_map/pallas_call | solution.py:307
  103.4 0.0 copy-start
  103.4 1.3 copy-done
  104.7 0.0 all-to-all-done.1.x_ref
  104.7 0.0 copy-start.2
  104.7 7.4 %all-to-all-start = ((bf16[16,256,256]{2,1,0:T(8,128)(2,1)}), bf16[16,256,256]{2,1,0:T(8,128)(2,1)}, u32[]{:S(2)}, u32[]{:S(2)}) async-start(bf16[16,256,256]{2,1,0:T(8,128)(2,1)} %copy-done), calls=%async_computation | async-start | bytes 4194304 | tf_op jit(solution)/shard_map/all_to_all | solution.py:437
  112.2 0.8 and_select_fusion.2.slots
  113.0 0.0 copy-done.2
  113.0 1.0 shard_map.63.start_ref
  114.1 45.6 %all-to-all-done.x_ref = bf16[16,256,256]{2,1,0:T(8,128)(2,1)} async-done(((bf16[16,256,256]{2,1,0:T(8,128)(2,1)}), bf16[16,256,256]{2,1,0:T(8,128)(2,1)}, u32[]{:S(2)}, u32[]{:S(2)}) %all-to-all-start) | async-done | bytes 2097184 | tf_op jit(solution)/shard_map/all_to_all | solution.py:437
  159.7 2.6 %shard_map.64 = f32[4,256,256]{2,1,0:T(8,128)S(1)} custom-call(s32[16]{0:T(128)S(1)} %and_select_fusion.2.slots, bf16[16,256,256]{2,1,0:T(8,128)(2,1)} %all-to-all-done.x_ref, f32[4,256,256]{2,1,0:T(8,128)S(1)} %shard_map.63.start_ref), custom_call_target="tpu_custom_call" | custom-call | flops 4000000000 | bytes 4194304 | tf_op jit(solution)/shard_map/pallas_call | solution.py:379
  162.3 6.2 %collective-permute-start.4 = (f32[2,256,256]{2,1,0:T(8,128)S(1)}, f32[2,256,256]{2,1,0:T(8,128)S(1)}, u32[]{:S(2)}, u32[]{:S(2)}) collective-permute-start(f32[2,256,256]{2,1,0:T(8,128)S(1)} %slice.25), channel_id=1, source_target_pairs={{0,16},{1,17},{2,18},{3,19},{4,20},{5,21},{6,22},{7,23},{8,24},{9,... | collective-permute-start | bytes 1572872 | tf_op jit(solution)/shard_map/ppermute | solution.py:441
  168.4 24.6 %collective-permute-done.4 = f32[2,256,256]{2,1,0:T(8,128)S(1)} collective-permute-done((f32[2,256,256]{2,1,0:T(8,128)S(1)}, f32[2,256,256]{2,1,0:T(8,128)S(1)}, u32[]{:S(2)}, u32[]{:S(2)}) %collective-permute-start.4) | collective-permute-done | bytes 524320 | tf_op jit(solution)/shard_map/ppermute | solution.py:441
  193.0 0.9 slice_add_fusion
  (5 shorter events, 0.1 us)
Async XLA Ops:
  7.2 57.6 %all-gather.3.cloned.1.call-start = ((), (), s32[]{:S(2)}) async-start(), calls=%async_computation.2 | async-start | bytes 6684672 | tf_op jit(solution)/shard_map/all_gather | solution.py:428
  9.9 0.7 collective-permute-start
  10.6 0.7 collective-permute-start.1
  11.4 0.7 collective-permute-start.2
  12.1 18.5 %collective-permute-start.3 = (bf16[256,256]{1,0:T(8,128)(2,1)S(1)}, bf16[256,256]{1,0:T(8,128)(2,1)S(1)}, u32[]{:S(2)}, u32[]{:S(2)}) collective-permute-start(bf16[256,256]{1,0:T(8,128)(2,1)S(1)} %broadcast_select_fusion.2), channel_id=1, source_target_pairs={{0,32},{64,96},{128,160},{192,224},{256,288},{320,352},{384,416},{... | collective-permute-start | bytes 393224 | tf_op jit(solution)/shard_map/ppermute | solution.py:401
  17.2 8.9 %copy-start.3 = (s32[32]{0:T(128)S(1)}, s32[32]{0:T(128)}, u32[]{:S(2)}) copy-start(s32[32]{0:T(128)} %param.5) | copy-start | bytes 388
  17.2 87.5 %all-to-all-start.1 = ((bf16[16,256,256]{2,1,0:T(8,128)(2,1)}), bf16[16,256,256]{2,1,0:T(8,128)(2,1)S(1)}, u32[]{:S(2)}, u32[]{:S(2)}) async-start(bf16[16,256,256]{2,1,0:T(8,128)(2,1)} %shard_map.62), calls=%async_computation.1 | async-start | bytes 4194304 | tf_op jit(solution)/shard_map/all_to_all | solution.py:431
  65.9 20.5 %copy-start.1 = (bf16[256,768]{1,0:T(8,128)(2,1)S(1)}, bf16[256,768]{1,0:T(8,128)(2,1)}, u32[]{:S(2)}) copy-start(bf16[256,768]{1,0:T(8,128)(2,1)} %slice.21.own_ref) | copy-start | bytes 1179652
  103.4 1.3 copy-start
  104.7 8.3 %copy-start.2 = (bf16[2,256,256]{2,1,0:T(8,128)(2,1)S(1)}, bf16[2,256,256]{2,1,0:T(8,128)(2,1)}, u32[]{:S(2)}) copy-start(bf16[2,256,256]{2,1,0:T(8,128)(2,1)} %anc_ref.1) | copy-start | bytes 786436
  104.7 54.9 %all-to-all-start = ((bf16[16,256,256]{2,1,0:T(8,128)(2,1)}), bf16[16,256,256]{2,1,0:T(8,128)(2,1)}, u32[]{:S(2)}, u32[]{:S(2)}) async-start(bf16[16,256,256]{2,1,0:T(8,128)(2,1)} %copy-done), calls=%async_computation | async-start | bytes 4194304 | tf_op jit(solution)/shard_map/all_to_all | solution.py:437
  162.3 30.8 %collective-permute-start.4 = (f32[2,256,256]{2,1,0:T(8,128)S(1)}, f32[2,256,256]{2,1,0:T(8,128)S(1)}, u32[]{:S(2)}, u32[]{:S(2)}) collective-permute-start(f32[2,256,256]{2,1,0:T(8,128)S(1)} %slice.25), channel_id=1, source_target_pairs={{0,16},{1,17},{2,18},{3,19},{4,20},{5,21},{6,22},{7,23},{8,24},{9,... | collective-permute-start | bytes 1572872 | tf_op jit(solution)/shard_map/ppermute | solution.py:441
Sparse Core Ops, SparseCore 0:
  10.7 53.9 all-gather.2

commit v4 on v3

--- a/solution.py
+++ b/solution.py
@@ -10,6 +10,8 @@
 SUB = 8
 PANEL = 32
 GROUP = 4
+H = B // 2
+EXTRA = 16
 VMEM = pl.BlockSpec(memory_space=pltpu.VMEM)
 ANY = pl.BlockSpec(memory_space=pl.ANY)
 F32 = jnp.float32
@@ -241,6 +243,30 @@
     return panels
 
 
+def half_update(row, j, mine_ref, other, out_ref):
+    @pl.when(row < j)
+    def _():
+        out_ref[j, :H] = dot_nt(mine_ref[:H, :], other).astype(BF16)
+        out_ref[j, H:] = jnp.zeros((EXTRA, B), BF16)
+
+    @pl.when(row > j)
+    def _():
+        out_ref[j, :H] = dot_nt(other[H:], mine_ref[...]).astype(BF16)
+        out_ref[j, H:] = jnp.zeros((EXTRA, B), BF16)
+
+    @pl.when(row == j)
+    def _():
+        top = dot_nt(mine_ref[:H, :], mine_ref[...])
+        last = dot_nt(mine_ref[H:, :], mine_ref[H:, :])
+        ri = lax.broadcasted_iota(jnp.int32, (H, H), 0)
+        ci = lax.broadcasted_iota(jnp.int32, (H, H), 1)
+        first = jnp.where(ri >= ci, top[:, :H], last)
+        out_ref[j, :H] = jnp.concatenate([first, top[:, H:]], axis=1).astype(BF16)
+        diagonal = jnp.sum(jnp.where(ri == ci, last, 0.0), axis=0, keepdims=True)
+        diagonal = jnp.concatenate([diagonal, jnp.zeros((1, H), F32)], axis=1)
+        out_ref[j, H:] = jnp.broadcast_to(diagonal, (EXTRA, B)).astype(BF16)
+
+
 def update_kernel(
     scalars,
     own_ref,
@@ -291,9 +317,7 @@
             [jnp.where(t < pivots, panels[t], 0.0).astype(BF16) for t in range(STEPS)], axis=1
         )
         for k in range(GROUP):
-            out_ref[i * GROUP + k] = dot_nt(
-                mine_ref[...], other[k * B : (k + 1) * B]
-            ).astype(BF16)
+            half_update(row, i * GROUP + k, mine_ref, other[k * B : (k + 1) * B], out_ref)
         send(i).start()
         return carry
 
@@ -310,13 +334,13 @@
         out_specs=[VMEM, ANY],
         out_shape=[
             jax.ShapeDtypeStruct((B, STEPS * B), F32),
-            jax.ShapeDtypeStruct((blocks, B, B), BF16),
+            jax.ShapeDtypeStruct((blocks, H + EXTRA, B), BF16),
         ],
         scratch_shapes=[
             pltpu.VMEM((B, STEPS * B), BF16),
             pltpu.VMEM((STEPS, 2, B, B), BF16),
             pltpu.VMEM((blocks, B, STEPS * B), BF16),
-            pltpu.VMEM((blocks, B, B), BF16),
+            pltpu.VMEM((blocks, H + EXTRA, B), BF16),
             pltpu.SemaphoreType.DMA((blocks // GROUP,)),
             pltpu.SemaphoreType.DMA((blocks // GROUP,)),
         ],
@@ -360,29 +384,14 @@
             acc_ref[slot] += x_ref[i].astype(F32)
 
 
-def end_sum_kernel(slots, x_ref, start_ref, acc_ref):
-    k = pl.program_id(0)
-
-    @pl.when(k == 0)
-    def _():
-        acc_ref[...] = start_ref[...]
-
-    for i in range(GROUP):
-        slot = slots[k * GROUP + i]
-
-        @pl.when(slot < 4)
-        def _(i=i, slot=slot):
-            acc_ref[slot] -= x_ref[i].astype(F32)
-
-
-def sum_blocks(kernel, slots, x, start):
-    return pl.pallas_call(
-        kernel,
+def sum_fronts(slots, x, ancestor):
+    return pl.pallas_call(
+        start_sum_kernel,
         grid=(x.shape[0] // GROUP,),
         in_specs=[
             pl.BlockSpec(memory_space=pltpu.SMEM),
             pl.BlockSpec((GROUP, B, B), lambda k: (k, 0, 0)),
-            pl.BlockSpec(start.shape, lambda k: (0, 0, 0)),
+            pl.BlockSpec(ancestor.shape, lambda k: (0, 0, 0)),
         ],
         out_specs=pl.BlockSpec((4, B, B), lambda k: (0, 0, 0)),
         out_shape=jax.ShapeDtypeStruct((4, B, B), F32),
@@ -390,7 +399,106 @@
         cost_estimate=pl.CostEstimate(
             flops=4_000_000_000, bytes_accessed=4 << 20, transcendentals=0
         ),
-    )(slots, x, start)
+    )(slots, x, ancestor)
+
+
+def update_sum_kernel(slots, side_ref, x_ref, own_ref, far_ref, near_mirror, far_mirror, acc_ref):
+    k = pl.program_id(0)
+
+    @pl.when(k == 0)
+    def _():
+        acc_ref[...] = jnp.zeros_like(acc_ref)
+
+    for i in range(GROUP):
+        slot = slots[k * GROUP + i]
+
+        @pl.when(slot < 4)
+        def _(i=i, slot=slot):
+            acc_ref[slot] += x_ref[i].astype(F32)
+
+    @pl.when(k == pl.num_programs(0) - 1)
+    def _():
+        side = side_ref[0]
+        for h in range(2):
+            own_ref[h] = acc_ref[2 * side + h]
+            far_ref[h] = acc_ref[2 * (1 - side) + h].astype(BF16)
+            near_mirror[h] = acc_ref[2 * h + side][:H].astype(BF16)
+            far_mirror[h] = acc_ref[2 * h + 1 - side][:H].astype(BF16)
+
+
+def sum_updates(slots, side, x):
+    rows = x.shape[1]
+    whole = lambda k: (0, 0, 0)
+    return pl.pallas_call(
+        update_sum_kernel,
+        grid=(x.shape[0] // GROUP,),
+        in_specs=[
+            pl.BlockSpec(memory_space=pltpu.SMEM),
+            pl.BlockSpec(memory_space=pltpu.SMEM),
+            pl.BlockSpec((GROUP, rows, B), lambda k: (k, 0, 0)),
+        ],
+        out_specs=[
+            pl.BlockSpec((2, rows, B), whole),
+            pl.BlockSpec((2, rows, B), whole),
+            pl.BlockSpec((2, H, B), whole),
+            pl.BlockSpec((2, H, B), whole),
+        ],
+        out_shape=[
+            jax.ShapeDtypeStruct((2, rows, B), F32),
+            jax.ShapeDtypeStruct((2, rows, B), BF16),
+            jax.ShapeDtypeStruct((2, H, B), BF16),
+            jax.ShapeDtypeStruct((2, H, B), BF16),
+        ],
+        scratch_shapes=[pltpu.VMEM((4, rows, B), F32)],
+        compiler_params=pltpu.CompilerParams(vmem_limit_bytes=40 << 20),
+        cost_estimate=pl.CostEstimate(
+            flops=2_000_000, bytes_accessed=3 << 20, transcendentals=0
+        ),
+    )(slots, side, x)
+
+
+def finish_kernel(place, start_ref, far_start, own_ref, far_ref, mirror_a, mirror_b, out_ref):
+    row = place[0]
+    block_col = place[1]
+    for h in range(2):
+        start = start_ref[h] + far_start[h]
+        mine = own_ref[h] + far_ref[h].astype(F32)
+        mirror = mirror_a[h].astype(F32) + mirror_b[h].astype(F32)
+
+        @pl.when(row < block_col)
+        def _(h=h, start=start, mine=mine, mirror=mirror):
+            out_ref[h] = start - jnp.concatenate([mine[:H], mirror], axis=0)
+
+        @pl.when(row > block_col)
+        def _(h=h, start=start, mine=mine, mirror=mirror):
+            out_ref[h] = start - jnp.concatenate([mirror, mine[:H]], axis=0).T
+
+        @pl.when(row == block_col)
+        def _(h=h, start=start, mine=mine):
+            ri = lax.broadcasted_iota(jnp.int32, (H, H), 0)
+            ci = lax.broadcasted_iota(jnp.int32, (H, H), 1)
+            packed = mine[:H, :H]
+            turned = packed.T
+            side = mine[:H, H:]
+            first = jnp.where(ri >= ci, packed, turned)
+            diagonal = jnp.broadcast_to(mine[H : H + 1, :H], (H, H))
+            last = jnp.where(ri < ci, packed, jnp.where(ri > ci, turned, diagonal))
+            top = jnp.concatenate([first, side], axis=1)
+            bottom = jnp.concatenate([side.T, last], axis=1)
+            out_ref[h] = start - jnp.concatenate([top, bottom], axis=0)
+
+
+def finish(place, *arrays):
+    return pl.pallas_call(
+        finish_kernel,
+        in_specs=[pl.BlockSpec(memory_space=pltpu.SMEM)] + [VMEM] * len(arrays),
+        out_specs=VMEM,
+        out_shape=jax.ShapeDtypeStruct((2, B, B), F32),
+        compiler_params=pltpu.CompilerParams(vmem_limit_bytes=40 << 20),
+        cost_estimate=pl.CostEstimate(
+            flops=2_000_000, bytes_accessed=3 << 20, transcendentals=0
+        ),
+    )(place, *arrays)
 
 
 def broadcast_first(block, row):
@@ -422,6 +530,18 @@
     row_half = lax.dynamic_index_in_dim(tgt, row, 1, keepdims=False) // blocks
     keep = (block_col >= piv) & (row >= piv)
     slots = jnp.where(keep, jnp.where(col_half == side, 0, 2) + row_half, 4).astype(jnp.int32)
+    update_slots = jnp.where(keep, 2 * col_half + row_half, 4).astype(jnp.int32)
+    place = jnp.stack([row, block_col]).astype(jnp.int32)
+    far = [(c, (c + half) % cols) for c in range(cols)]
+    mirror = [
+        [
+            ((i * 2 + z) * half + j, (j * 2 + (z + turn) % 2) * half + i)
+            for i in range(blocks)
+            for z in range(2)
+            for j in range(half)
+        ]
+        for turn in range(2)
+    ]
     scalars = jnp.stack([pivots[col], row.astype(jnp.int32)])
 
     own, corner = lax.optimization_barrier((front[:, : STEPS * B], front[:, :B]))
@@ -433,13 +553,20 @@
     )
 
     low, inv, pan = factor_rest(gathered[1:STEPS].reshape((STEPS - 1) * B, STEPS * B), inv0)
+    start = sum_fronts(slots, f, ancestor)
+    far_start, inv = lax.optimization_barrier((start[2:4], inv))
+    far_start = lax.ppermute(far_start, "col", far)
     factor, u = solve_and_update(scalars, own, gathered, low0, inv0, low, inv, pan)
     u = lax.all_to_all(u, "col", 0, 0, axis_index_groups=groups, tiled=True)
 
-    acc = sum_blocks(start_sum_kernel, slots, f, ancestor)
-    acc = sum_blocks(end_sum_kernel, slots, u, acc)
-    received = lax.ppermute(acc[2:4], "col", [(c, (c + half) % cols) for c in range(cols)])
-    return factor[None], acc[0:2] + received
+    own_sum, far_sum, mirror_a, mirror_b = sum_updates(
+        update_slots, side.astype(jnp.int32)[None], u
+    )
+    far_sum = lax.ppermute(far_sum, "col", far)
+    mirror_a = lax.ppermute(mirror_a, ("row", "col"), mirror[0])
+    mirror_b = lax.ppermute(mirror_b, ("row", "col"), mirror[1])
+    out = finish(place, start[0:2], far_start, own_sum, far_sum, mirror_a, mirror_b)
+    return factor[None], out
 
 
 def solution(mesh):

time: 201 us -> 226 us (1.12)
  the two profiles are of different devices: /device:TPU:69 before, /device:TPU:57 now
where the time goes in v4:
time: 226 us; the launch traced here: 225 us
  waiting for transfers between devices  84.6 us (37%)
  starting transfers between devices  62.9 us (28%)
  Pallas kernels  56.5 us (25%)
  between operations  14.3 us (6%)
  local copies, waits for them, and re-layouts  5.33 us (2%)
    all_to_all x1, waiting for transfers between devices, shards(): u = lax.all_to_all(u, 'col', 0, 0, axis_index_groups=groups, tiled=True)  29.1 us
    ppermute x4, waiting for transfers between devices, broadcast_first(): got = lax.ppermute(block, 'row', pairs)  26.2 us
    ppermute x1, waiting for transfers between devices, shards(): mirror_a = lax.ppermute(mirror_a, ('row', 'col'), mirror[0])  25.6 us
    pallas_call x1, Pallas kernels, factor_rest(): pl.pallas_call(rest_kernel, in_specs=[VMEM, VMEM], out_specs=[VMEM, VMEM,...  20.5 us
    ppermute x1, starting transfers between devices, shards(): mirror_a = lax.ppermute(mirror_a, ('row', 'col'), mirror[0])  20.5 us
    pallas_call x1, Pallas kernels, solve_and_update(): pl.pallas_call(update_kernel, in_specs=[pl.BlockSpec(memory_space=pltpu.S...  19.1 us
    all_to_all x1, starting transfers between devices, shards(): u = lax.all_to_all(u, 'col', 0, 0, axis_index_groups=groups, tiled=True)  11.3 us
    all_to_all x1, starting transfers between devices, shards(): lax.all_to_all(block_columns(front), 'col', 0, 0, axis_index_groups=group...  9.68 us
  transfers between devices with their start and end apart: 11, of which 5 were waited for; matrix products, arithmetic and copies ran while one was open for 1% of the time, Pallas kernels for 7%

profile of v4, /device:TPU:57, one launch (start us, length us, event | category | flops | bytes accessed | tf_op | source)
XLA Modules:
  0.0 225.4 jit_solution(6487975804274669479)
XLA Ops:
  7.2 0.0 all-gather.3.cloned.1.call-start
  7.2 1.8 slice.21.own_ref
  9.0 0.9 slice.22
  9.9 0.0 all-gather.3.cloned.1.call-update
  9.9 3.8 %shard_map.61 = bf16[16,256,256]{2,1,0:T(8,128)(2,1)} custom-call(bf16[256,4096]{1,0:T(8,128)(2,1)} %bitcast.26), custom_call_target="tpu_custom_call" | custom-call | bytes 4194304 | tf_op jit(solution)/shard_map/pallas_call | solution.py:361
  13.8 0.0 copy-start.2
  13.8 9.7 %all-to-all-start = ((bf16[16,256,256]{2,1,0:T(8,128)(2,1)}), bf16[16,256,256]{2,1,0:T(8,128)(2,1)S(1)}, u32[]{:S(2)}, u32[]{:S(2)}) async-start(bf16[16,256,256]{2,1,0:T(8,128)(2,1)} %shard_map.61), calls=%async_computation | async-start | bytes 4194304 | tf_op jit(solution)/shard_map/all_to_all | solution.py:551
  23.4 0.7 collective-permute-start
  24.1 0.0 collective-permute-done
  24.2 0.7 collective-permute-start.1
  24.9 0.0 collective-permute-done.1
  24.9 0.7 collective-permute-start.2
  25.6 0.0 copy-done.2
  25.6 0.8 add_select_fusion
  26.4 0.0 collective-permute-done.2
  26.5 1.3 collective-permute-start.3
  27.8 0.6 dynamic_slice.14
  28.4 0.7 pad_add_fusion.scalars
  29.1 26.2 %collective-permute-done.3 = bf16[256,256]{1,0:T(8,128)(2,1)S(1)} collective-permute-done((bf16[256,256]{1,0:T(8,128)(2,1)S(1)}, bf16[256,256]{1,0:T(8,128)(2,1)S(1)}, u32[]{:S(2)}, u32[]{:S(2)}) %collective-permute-start.3) | collective-permute-done | bytes 131104 | tf_op jit(solution)/shard_map/ppermute | solution.py:509
  55.3 0.0 copy-start.1
  55.3 9.4 %shard_map.59 = (f32[1,256,256]{2,1,0:T(8,128)S(1)}, f32[1,256,256]{2,1,0:T(8,128)S(1)}) custom-call(bf16[256,256]{1,0:T(8,128)(2,1)S(1)} %broadcast_select_fusion.3.a_ref), custom_call_target="tpu_custom_call" | custom-call | flops 10000000000 | bytes 1048576 | tf_op jit(solution)/shard_map/pallas_call | solution.py:161
  64.8 0.2 all-to-all-done.x_ref
  64.9 0.0 copy-done.1
  64.9 1.0 shard_map.62
  65.9 0.9 fusion.2
  66.8 0.0 all-gather.3.cloned.1.call-done
  66.8 1.2 slice.23.a_ref
  68.0 0.0 copy-start
  68.0 20.5 %shard_map.60 = (f32[2,256,256]{2,1,0:T(8,128)S(1)}, f32[2,256,256]{2,1,0:T(8,128)S(1)}, bf16[3,256,256]{2,1,0:T(8,128)(2,1)S(1)}) custom-call(bf16[512,768]{1,0:T(8,128)(2,1)S(1)} %slice.23.a_ref, f32[1,256,256]{2,1,0:T(8,128)S(1)} %get-tuple-element.20.inv0_ref), custom_call_target="tpu_custom_call" | custom-call | flops 20000000000 | bytes 4194304 | tf_op jit(solution)/shard_map/pallas_call | solution.py:194
  88.5 0.0 copy-done
  88.5 19.1 %shard_map.63 = (f32[256,768]{1,0:T(8,128)}, bf16[16,144,256]{2,1,0:T(8,128)(2,1)}) custom-call(s32[2]{0:T(128)S(1)} %pad_add_fusion.scalars, bf16[256,768]{1,0:T(8,128)(2,1)S(1)} %copy-done, bf16[16,256,768]{2,1,0:T(8,128)(2,1)} %bitcast.27, f32[1,256,256]{2,1,0:T(8,128)S(1)} %get-tuple-element.19.low0_ref, f32[1,256,256]{2,1,0:T(8,128)S(1)} %get-tuple-element.20.inv0_ref, ...), custom_call_target="tpu_custom_call" | custom-call | flops 16000000000 | bytes 10485760 | tf_op jit(solution)/shard_map/pallas_call | solution.py:331
  107.7 11.3 %all-to-all-start.1 = ((bf16[16,144,256]{2,1,0:T(8,128)(2,1)}), bf16[16,144,256]{2,1,0:T(8,128)(2,1)S(1)}, u32[]{:S(2)}, u32[]{:S(2)}) async-start(bf16[16,144,256]{2,1,0:T(8,128)(2,1)} %get-tuple-element.27), calls=%async_computation.1 | async-start | bytes 2359296 | tf_op jit(solution)/shard_map/all_to_all | solution.py:560
  119.0 7.9 %collective-permute-start.4 = (f32[2,256,256]{2,1,0:T(8,128)}, f32[2,256,256]{2,1,0:T(8,128)S(1)}, u32[]{:S(2)}, u32[]{:S(2)}) collective-permute-start(f32[2,256,256]{2,1,0:T(8,128)} %get-tuple-element.26), channel_id=1, source_target_pairs={{0,16},{1,17},{2,18},{3,19},{4,20},{5,21},{6,22},{7,23},{8,24},{9,... | collective-permute-start | bytes 1572872 | tf_op jit(solution)/shard_map/ppermute | solution.py:558
  126.9 29.1 %all-to-all-done.1.x_ref = bf16[16,144,256]{2,1,0:T(8,128)(2,1)S(1)} async-done(((bf16[16,144,256]{2,1,0:T(8,128)(2,1)}), bf16[16,144,256]{2,1,0:T(8,128)(2,1)S(1)}, u32[]{:S(2)}, u32[]{:S(2)}) %all-to-all-start.1) | async-done | bytes 1179680 | tf_op jit(solution)/shard_map/all_to_all | solution.py:560
  156.0 0.9 shard_map.64
  156.9 8.2 %collective-permute-start.5 = (bf16[2,144,256]{2,1,0:T(8,128)(2,1)S(1)}, bf16[2,144,256]{2,1,0:T(8,128)(2,1)S(1)}, u32[]{:S(2)}, u32[]{:S(2)}) collective-permute-start(bf16[2,144,256]{2,1,0:T(8,128)(2,1)S(1)} %get-tuple-element.29), channel_id=1, source_target_pairs={{0,16},{1,17},{2,18},{3,19},{4,20},{5,21},{6,22},{7,23},{8,24},{9,... | collective-permute-start | bytes 442376 | tf_op jit(solution)/shard_map/ppermute | solution.py:565
  165.1 20.5 %collective-permute-start.6 = (bf16[2,128,256]{2,1,0:T(8,128)(2,1)S(1)}, bf16[2,128,256]{2,1,0:T(8,128)(2,1)S(1)}, u32[]{:S(2)}, u32[]{:S(2)}) collective-permute-start(bf16[2,128,256]{2,1,0:T(8,128)(2,1)S(1)} %get-tuple-element.30), channel_id=1, source_target_pairs={{0,0},{1,32},{2,64},{3,96},{4,128},{5,160},{6,192},{7,224},{8,256}... | collective-permute-start | bytes 393224 | tf_op jit(solution)/shard_map/ppermute | solution.py:566
  185.7 1.9 collective-permute-start.7
  187.6 0.1 pad_add_fusion.1.place
  187.7 0.0 collective-permute-done.4.far_start
  187.7 25.6 %collective-permute-done.6.mirror_a = bf16[2,128,256]{2,1,0:T(8,128)(2,1)S(1)} collective-permute-done((bf16[2,128,256]{2,1,0:T(8,128)(2,1)S(1)}, bf16[2,128,256]{2,1,0:T(8,128)(2,1)S(1)}, u32[]{:S(2)}, u32[]{:S(2)}) %collective-permute-start.6) | collective-permute-done | bytes 131104 | tf_op jit(solution)/shard_map/ppermute | solution.py:566
  213.3 3.5 %collective-permute-done.7.mirror_b = bf16[2,128,256]{2,1,0:T(8,128)(2,1)S(1)} collective-permute-done((bf16[2,128,256]{2,1,0:T(8,128)(2,1)S(1)}, bf16[2,128,256]{2,1,0:T(8,128)(2,1)S(1)}, u32[]{:S(2)}, u32[]{:S(2)}) %collective-permute-start.7) | collective-permute-done | bytes 131104 | tf_op jit(solution)/shard_map/ppermute | solution.py:567
  216.8 0.0 collective-permute-done.5.far_ref
  216.8 1.7 shard_map.65
  (5 shorter events, 0.1 us)
Async XLA Ops:
  7.2 59.6 %all-gather.3.cloned.1.call-start = ((), (), s32[]{:S(2)}) async-start(), calls=%async_computation.2 | async-start | bytes 6684672 | tf_op jit(solution)/shard_map/all_gather | solution.py:548
  13.8 11.9 %copy-start.2 = (s32[32]{0:T(128)S(1)}, s32[32]{0:T(128)}, u32[]{:S(2)}) copy-start(s32[32]{0:T(128)} %param.5) | copy-start | bytes 388
  13.8 51.2 %all-to-all-start = ((bf16[16,256,256]{2,1,0:T(8,128)(2,1)}), bf16[16,256,256]{2,1,0:T(8,128)(2,1)S(1)}, u32[]{:S(2)}, u32[]{:S(2)}) async-start(bf16[16,256,256]{2,1,0:T(8,128)(2,1)} %shard_map.61), calls=%async_computation | async-start | bytes 4194304 | tf_op jit(solution)/shard_map/all_to_all | solution.py:551
  23.4 0.7 collective-permute-start
  24.2 0.7 collective-permute-start.1
  24.9 1.5 collective-permute-start.2
  26.5 28.8 %collective-permute-start.3 = (bf16[256,256]{1,0:T(8,128)(2,1)S(1)}, bf16[256,256]{1,0:T(8,128)(2,1)S(1)}, u32[]{:S(2)}, u32[]{:S(2)}) collective-permute-start(bf16[256,256]{1,0:T(8,128)(2,1)S(1)} %broadcast_select_fusion.2), channel_id=1, source_target_pairs={{0,32},{64,96},{128,160},{192,224},{256,288},{320,352},{384,416},{... | collective-permute-start | bytes 393224 | tf_op jit(solution)/shard_map/ppermute | solution.py:509
  55.3 9.6 %copy-start.1 = (bf16[2,256,256]{2,1,0:T(8,128)(2,1)S(1)}, bf16[2,256,256]{2,1,0:T(8,128)(2,1)}, u32[]{:S(2)}) copy-start(bf16[2,256,256]{2,1,0:T(8,128)(2,1)} %anc_ref.1) | copy-start | bytes 786436
  68.0 20.6 %copy-start = (bf16[256,768]{1,0:T(8,128)(2,1)S(1)}, bf16[256,768]{1,0:T(8,128)(2,1)}, u32[]{:S(2)}) copy-start(bf16[256,768]{1,0:T(8,128)(2,1)} %slice.21.own_ref) | copy-start | bytes 1179652
  107.7 48.3 %all-to-all-start.1 = ((bf16[16,144,256]{2,1,0:T(8,128)(2,1)}), bf16[16,144,256]{2,1,0:T(8,128)(2,1)S(1)}, u32[]{:S(2)}, u32[]{:S(2)}) async-start(bf16[16,144,256]{2,1,0:T(8,128)(2,1)} %get-tuple-element.27), calls=%async_computation.1 | async-start | bytes 2359296 | tf_op jit(solution)/shard_map/all_to_all | solution.py:560
  119.0 68.7 %collective-permute-start.4 = (f32[2,256,256]{2,1,0:T(8,128)}, f32[2,256,256]{2,1,0:T(8,128)S(1)}, u32[]{:S(2)}, u32[]{:S(2)}) collective-permute-start(f32[2,256,256]{2,1,0:T(8,128)} %get-tuple-element.26), channel_id=1, source_target_pairs={{0,16},{1,17},{2,18},{3,19},{4,20},{5,21},{6,22},{7,23},{8,24},{9,... | collective-permute-start | bytes 1572872 | tf_op jit(solution)/shard_map/ppermute | solution.py:558
  156.9 59.9 %collective-permute-start.5 = (bf16[2,144,256]{2,1,0:T(8,128)(2,1)S(1)}, bf16[2,144,256]{2,1,0:T(8,128)(2,1)S(1)}, u32[]{:S(2)}, u32[]{:S(2)}) collective-permute-start(bf16[2,144,256]{2,1,0:T(8,128)(2,1)S(1)} %get-tuple-element.29), channel_id=1, source_target_pairs={{0,16},{1,17},{2,18},{3,19},{4,20},{5,21},{6,22},{7,23},{8,24},{9,... | collective-permute-start | bytes 442376 | tf_op jit(solution)/shard_map/ppermute | solution.py:565
  165.1 48.2 %collective-permute-start.6 = (bf16[2,128,256]{2,1,0:T(8,128)(2,1)S(1)}, bf16[2,128,256]{2,1,0:T(8,128)(2,1)S(1)}, u32[]{:S(2)}, u32[]{:S(2)}) collective-permute-start(bf16[2,128,256]{2,1,0:T(8,128)(2,1)S(1)} %get-tuple-element.30), channel_id=1, source_target_pairs={{0,0},{1,32},{2,64},{3,96},{4,128},{5,160},{6,192},{7,224},{8,256}... | collective-permute-start | bytes 393224 | tf_op jit(solution)/shard_map/ppermute | solution.py:566
  185.7 31.1 %collective-permute-start.7 = (bf16[2,128,256]{2,1,0:T(8,128)(2,1)S(1)}, bf16[2,128,256]{2,1,0:T(8,128)(2,1)S(1)}, u32[]{:S(2)}, u32[]{:S(2)}) collective-permute-start(bf16[2,128,256]{2,1,0:T(8,128)(2,1)S(1)} %get-tuple-element.31), channel_id=1, source_target_pairs={{0,16},{1,48},{2,80},{3,112},{4,144},{5,176},{6,208},{7,240},{8,27... | collective-permute-start | bytes 393224 | tf_op jit(solution)/shard_map/ppermute | solution.py:567
Sparse Core Ops, SparseCore 0:
  10.7 54.5 all-gather.2

commit v5 on v3

--- a/solution.py
+++ b/solution.py
@@ -113,11 +113,12 @@
     return keep, update
 
 
-def cholesky_in_place(t_ref):
+def cholesky_in_place(t_ref, beside):
     count = PANEL // SUB
     tiles = [t_ref[SUB * i : SUB * (i + 1), :] for i in range(count)]
     for b0 in range(0, B, PANEL):
         b1 = b0 + PANEL
+        beside(b0 // PANEL)
         keep, update = factor_tiles(tiles, b0)
         for i in range(count):
             t_ref[b0 + SUB * i : b0 + SUB * (i + 1), :] = keep[i]
@@ -139,20 +140,19 @@
             t_ref[b1 + PANEL :, :] = below(b1 + PANEL, B)
 
 
-def factor_block(d, t_ref, low_ref, inv_ref, s):
+def factor_block(d, t_ref, beside=lambda q: None):
     t_ref[...] = 0.5 * (d + d.T)
-    cholesky_in_place(t_ref)
+    cholesky_in_place(t_ref, beside)
     t = t_ref[...]
     ri = lax.broadcasted_iota(jnp.int32, (B, B), 0)
     ci = lax.broadcasted_iota(jnp.int32, (B, B), 1)
     inv = jnp.where(ci <= ri, t, 0.0)
-    inv_ref[s] = inv
-    low_ref[s] = jnp.where(ci > ri, t, jnp.where(ci == ri, 1.0 / t, 0.0)).T
-    return inv
+    low = jnp.where(ci > ri, t, jnp.where(ci == ri, 1.0 / t, 0.0)).T
+    return low, inv
 
 
 def first_kernel(a_ref, low_ref, inv_ref, t_ref):
-    factor_block(a_ref[...].astype(F32), t_ref, low_ref, inv_ref, 0)
+    low_ref[...], inv_ref[...] = factor_block(a_ref[...].astype(F32), t_ref)
 
 
 def factor_first(block):
@@ -160,7 +160,7 @@
         first_kernel,
         in_specs=[VMEM],
         out_specs=[VMEM, VMEM],
-        out_shape=[jax.ShapeDtypeStruct((1, B, B), F32)] * 2,
+        out_shape=[jax.ShapeDtypeStruct((B, B), F32)] * 2,
         scratch_shapes=[pltpu.VMEM((B, B), F32)],
         compiler_params=pltpu.CompilerParams(vmem_limit_bytes=40 << 20),
         cost_estimate=pl.CostEstimate(
@@ -169,97 +169,39 @@
     )(block)
 
 
-def rest_kernel(a_ref, inv0_ref, low_ref, inv_ref, pan_ref, w_ref, t_ref):
-    inv = inv0_ref[0]
-    w_ref[...] = a_ref[...].astype(F32)
-    for s in range(STEPS - 1):
-        panels = []
-        for r in range(s + 1, STEPS):
-            w = w_ref[(r - 1) * B : r * B, s * B : (s + 1) * B]
-            panel = dot_nt(w, inv, HIGHEST).astype(BF16)
-            panels.append(panel)
-            pan_ref[s + r - 1] = panel
-        for r in range(s + 1, STEPS):
-            for c in range(s + 1, r + 1):
-                w_ref[(r - 1) * B : r * B, c * B : (c + 1) * B] -= dot_nt(
-                    panels[r - s - 1], panels[c - s - 1]
-                )
-        d = w_ref[s * B : (s + 1) * B, (s + 1) * B : (s + 2) * B]
-        inv = factor_block(d, t_ref, low_ref, inv_ref, s)
-
-
-def factor_rest(rows, inv0):
-    return pl.pallas_call(
-        rest_kernel,
-        in_specs=[VMEM, VMEM],
-        out_specs=[VMEM, VMEM, VMEM],
-        out_shape=[
-            jax.ShapeDtypeStruct((STEPS - 1, B, B), F32),
-            jax.ShapeDtypeStruct((STEPS - 1, B, B), F32),
-            jax.ShapeDtypeStruct((STEPS, B, B), BF16),
-        ],
-        scratch_shapes=[pltpu.VMEM(((STEPS - 1) * B, STEPS * B), F32), pltpu.VMEM((B, B), F32)],
-        compiler_params=pltpu.CompilerParams(vmem_limit_bytes=40 << 20),
-        cost_estimate=pl.CostEstimate(
-            flops=20_000_000_000, bytes_accessed=4 << 20, transcendentals=0
-        ),
-    )(rows, inv0)
-
-
 def split(x):
     high = x.astype(BF16)
     return high, (x - high.astype(F32)).astype(BF16)
 
 
-def solve_own(a, invs, pan_ref):
-    solved = []
-    panels = []
-    for t in range(STEPS):
-        w = a[:, t * B : (t + 1) * B].astype(F32)
-        for s in range(t):
-            w = w - dot_nt(panels[s], pan_ref[t + s - 1])
-        x = dot_nt(w, invs[t], HIGHEST)
-        solved.append(x)
-        panels.append(x.astype(BF16))
-    return solved, panels
-
-
-def solve_panels(a, parts_ref, pan_ref):
-    panels = []
-    for t in range(STEPS):
-        w = a[:, t * B : (t + 1) * B]
-        high, low = parts_ref[t, 0], parts_ref[t, 1]
-        if t == 0:
-            x = dot_nt(w, high) + dot_nt(w, low)
-        else:
-            w = w.astype(F32)
-            for s in range(t):
-                w = w - dot_nt(panels[s], pan_ref[t + s - 1])
-            wh, wl = split(w)
-            x = dot_nt(wh, high) + (dot_nt(wl, high) + dot_nt(wh, low))
-        panels.append(x.astype(BF16))
-    return panels
-
-
-def update_kernel(
+def rest_kernel(
     scalars,
     own_ref,
     all_ref,
     low0_ref,
     inv0_ref,
-    low_ref,
-    inv_ref,
-    pan_ref,
     factor_ref,
     u_ref,
+    rows_ref,
+    corner_ref,
+    t_ref,
     mine_ref,
+    mine_rest,
     parts_ref,
-    rows_ref,
+    pan_ref,
+    p_ref,
+    high_ref,
+    low_part_ref,
+    sum_ref,
     out_ref,
     in_sems,
     out_sems,
 ):
-    groups = u_ref.shape[0] // GROUP
+    blocks = u_ref.shape[0]
+    groups = blocks // GROUP
+    per_panel = blocks // (B // PANEL)
+    pivots = scalars[0]
+    row = scalars[1]
 
     def fetch(i):
         part = pl.ds(i * GROUP, GROUP)
@@ -269,62 +211,125 @@
         part = pl.ds(i * GROUP, GROUP)
         return pltpu.make_async_copy(out_ref.at[part], u_ref.at[part], out_sems.at[i])
 
+    def cols(t):
+        return slice(t * B, (t + 1) * B)
+
+    def take_inverse(t, inv):
+        parts_ref[t, 0], parts_ref[t, 1] = split(inv)
+
+    def own_step(t, w, low, inv):
+        solved = dot_nt(w, inv, HIGHEST)
+        block = jnp.where(row > t, solved, jnp.where(row == t, low, 0.0))
+        factor_ref[:, cols(t)] = jnp.where(t < pivots, block, 0.0)
+        panel = solved.astype(BF16)
+        mine_ref[:, cols(t)] = jnp.where(t < pivots, panel, 0.0).astype(BF16)
+        return panel
+
+    def other_step(t, j):
+        high, low = parts_ref[t, 0], parts_ref[t, 1]
+        if t == 0:
+            a = rows_ref[j, :, cols(0)]
+            x = dot_nt(a, high) + dot_nt(a, low)
+        else:
+            wh, wl = high_ref[j], low_part_ref[j]
+            x = dot_nt(wh, high) + (dot_nt(wl, high) + dot_nt(wh, low))
+        return x.astype(BF16)
+
     for i in range(groups):
         fetch(i).start()
-    pivots = scalars[0]
-    row = scalars[1]
-    lows = [low0_ref[0], low_ref[0], low_ref[1]]
-    invs = [inv0_ref[0], inv_ref[0], inv_ref[1]]
-    solved, panels = solve_own(own_ref[...], invs, pan_ref)
-    for t in range(STEPS):
-        active = t < pivots
-        block = jnp.where(row > t, solved[t], jnp.where(row == t, lows[t], 0.0))
-        factor_ref[:, t * B : (t + 1) * B] = jnp.where(active, block, 0.0)
-        mine_ref[:, t * B : (t + 1) * B] = jnp.where(active, panels[t], 0.0).astype(BF16)
-        parts_ref[t, 0], parts_ref[t, 1] = split(invs[t])
-
-    def group(i, carry):
-        fetch(i).wait()
-        a = rows_ref[pl.ds(i * GROUP, GROUP)].reshape(GROUP * B, STEPS * B)
-        panels = solve_panels(a, parts_ref, pan_ref)
-        other = jnp.concatenate(
-            [jnp.where(t < pivots, panels[t], 0.0).astype(BF16) for t in range(STEPS)], axis=1
-        )
+    inv0 = inv0_ref[...]
+    take_inverse(0, inv0)
+    fetch(0).wait()
+
+    p1 = dot_nt(rows_ref[1, :, cols(0)].astype(F32), inv0, HIGHEST).astype(BF16)
+    p2 = dot_nt(rows_ref[2, :, cols(0)].astype(F32), inv0, HIGHEST).astype(BF16)
+    pan_ref[0] = p1
+    pan_ref[1] = p2
+    d = rows_ref[1, :, cols(1)].astype(F32) - dot_nt(p1, p1)
+    corner_ref[0] = rows_ref[2, :, cols(1)].astype(F32) - dot_nt(p2, p1)
+    corner_ref[1] = rows_ref[2, :, cols(2)].astype(F32) - dot_nt(p2, p2)
+
+    def beside_first(q):
+        if q == 0:
+            panel = own_step(0, own_ref[:, cols(0)].astype(F32), low0_ref[...], inv0)
+            mine_rest[0] = own_ref[:, cols(1)].astype(F32) - dot_nt(panel, pan_ref[0])
+            mine_rest[1] = own_ref[:, cols(2)].astype(F32) - dot_nt(panel, pan_ref[1])
+        for j in range(q * per_panel, (q + 1) * per_panel):
+            if j and j % GROUP == 0:
+                fetch(j // GROUP).wait()
+            p = other_step(0, j)
+            p_ref[j] = p
+            w = rows_ref[j, :, cols(1)].astype(F32) - dot_nt(p, pan_ref[0])
+            high_ref[j], low_part_ref[j] = split(w)
+
+    low1, inv1 = factor_block(d, t_ref, beside_first)
+    take_inverse(1, inv1)
+
+    p21 = dot_nt(corner_ref[0], inv1, HIGHEST).astype(BF16)
+    pan_ref[2] = p21
+    d = corner_ref[1] - dot_nt(p21, p21)
+
+    def beside_second(q):
+        if q == 0:
+            panel = own_step(1, mine_rest[0], low1, inv1)
+            mine_rest[1] = mine_rest[1] - dot_nt(panel, pan_ref[2])
+        for j in range(q * per_panel, (q + 1) * per_panel):
+            p0 = p_ref[j]
+            p1 = other_step(1, j)
+            w = rows_ref[j, :, cols(2)].astype(F32)
+            w = w - dot_nt(p0, pan_ref[1]) - dot_nt(p1, pan_ref[2])
+            high_ref[j], low_part_ref[j] = split(w)
+            p1 = jnp.where(1 < pivots, p1, 0.0).astype(BF16)
+            sum_ref[j] = dot_nt(mine_ref[:, cols(0)], p0) + dot_nt(mine_ref[:, cols(1)], p1)
+
+    low2, inv2 = factor_block(d, t_ref, beside_second)
+    take_inverse(2, inv2)
+    own_step(2, mine_rest[1], low2, inv2)
+
+    def last(i, carry):
         for k in range(GROUP):
-            out_ref[i * GROUP + k] = dot_nt(
-                mine_ref[...], other[k * B : (k + 1) * B]
-            ).astype(BF16)
+            j = i * GROUP + k
+            p2 = jnp.where(2 < pivots, other_step(2, j), 0.0).astype(BF16)
+            out_ref[j] = (sum_ref[j] + dot_nt(mine_ref[:, cols(2)], p2)).astype(BF16)
         send(i).start()
         return carry
 
-    lax.fori_loop(0, groups, group, 0)
+    lax.fori_loop(0, groups, last, 0)
     for i in range(groups):
         send(i).wait()
 
 
-def solve_and_update(scalars, own, gathered, low0, inv0, low, inv, pan):
+def factor_and_update(scalars, own, gathered, low0, inv0):
     blocks = gathered.shape[0]
     return pl.pallas_call(
-        update_kernel,
-        in_specs=[pl.BlockSpec(memory_space=pltpu.SMEM), VMEM, ANY] + [VMEM] * 5,
-        out_specs=[VMEM, ANY],
+        rest_kernel,
+        in_specs=[pl.BlockSpec(memory_space=pltpu.SMEM), VMEM, ANY, VMEM, VMEM],
+        out_specs=[VMEM, pl.BlockSpec(memory_space=pltpu.HBM)],
         out_shape=[
             jax.ShapeDtypeStruct((B, STEPS * B), F32),
             jax.ShapeDtypeStruct((blocks, B, B), BF16),
         ],
         scratch_shapes=[
+            pltpu.VMEM((blocks, B, STEPS * B), BF16),
+            pltpu.VMEM((2, B, B), F32),
+            pltpu.VMEM((B, B), F32),
             pltpu.VMEM((B, STEPS * B), BF16),
+            pltpu.VMEM((2, B, B), F32),
             pltpu.VMEM((STEPS, 2, B, B), BF16),
-            pltpu.VMEM((blocks, B, STEPS * B), BF16),
+            pltpu.VMEM((STEPS, B, B), BF16),
+            pltpu.VMEM((blocks, B, B), BF16),
+            pltpu.VMEM((blocks, B, B), BF16),
+            pltpu.VMEM((blocks, B, B), BF16),
+            pltpu.VMEM((blocks, B, B), F32),
             pltpu.VMEM((blocks, B, B), BF16),
             pltpu.SemaphoreType.DMA((blocks // GROUP,)),
             pltpu.SemaphoreType.DMA((blocks // GROUP,)),
         ],
         compiler_params=pltpu.CompilerParams(vmem_limit_bytes=48 << 20),
         cost_estimate=pl.CostEstimate(
-            flops=16_000_000_000, bytes_accessed=10 << 20, transcendentals=0
+            flops=30_000_000_000, bytes_accessed=10 << 20, transcendentals=0
         ),
-    )(scalars, own, gathered, low0, inv0, low, inv, pan)
+    )(scalars, own, gathered, low0, inv0)
 
 
 def relayout_kernel(x_ref, y_ref):
@@ -360,12 +365,13 @@
             acc_ref[slot] += x_ref[i].astype(F32)
 
 
-def end_sum_kernel(slots, x_ref, start_ref, acc_ref):
+def end_sum_kernel(slots, x_ref, start_ref, far_ref, own_ref, send_ref, acc_ref):
     k = pl.program_id(0)
 
     @pl.when(k == 0)
     def _():
-        acc_ref[...] = start_ref[...]
+        acc_ref[0:2] = start_ref[0:2] + far_ref[...]
+        acc_ref[2:4] = jnp.zeros((2, B, B), F32)
 
     for i in range(GROUP):
         slot = slots[k * GROUP + i]
@@ -374,23 +380,51 @@
         def _(i=i, slot=slot):
             acc_ref[slot] -= x_ref[i].astype(F32)
 
-
-def sum_blocks(kernel, slots, x, start):
+    @pl.when(k == pl.num_programs(0) - 1)
+    def _():
+        own_ref[...] = acc_ref[0:2]
+        send_ref[...] = acc_ref[2:4].astype(BF16)
+
+
+def sum_fronts(slots, x, ancestor):
     return pl.pallas_call(
-        kernel,
+        start_sum_kernel,
         grid=(x.shape[0] // GROUP,),
         in_specs=[
             pl.BlockSpec(memory_space=pltpu.SMEM),
             pl.BlockSpec((GROUP, B, B), lambda k: (k, 0, 0)),
-            pl.BlockSpec(start.shape, lambda k: (0, 0, 0)),
+            pl.BlockSpec((2, B, B), lambda k: (0, 0, 0)),
         ],
         out_specs=pl.BlockSpec((4, B, B), lambda k: (0, 0, 0)),
         out_shape=jax.ShapeDtypeStruct((4, B, B), F32),
         compiler_params=pltpu.CompilerParams(vmem_limit_bytes=40 << 20),
         cost_estimate=pl.CostEstimate(
-            flops=4_000_000_000, bytes_accessed=4 << 20, transcendentals=0
+            flops=4_000_000, bytes_accessed=4 << 20, transcendentals=0
         ),
-    )(slots, x, start)
+    )(slots, x, ancestor)
+
+
+def sum_updates(slots, x, start, far):
+    return pl.pallas_call(
+        end_sum_kernel,
+        grid=(x.shape[0] // GROUP,),
+        in_specs=[
+            pl.BlockSpec(memory_space=pltpu.SMEM),
+            pl.BlockSpec((GROUP, B, B), lambda k: (k, 0, 0)),
+            pl.BlockSpec((4, B, B), lambda k: (0, 0, 0)),
+            pl.BlockSpec((2, B, B), lambda k: (0, 0, 0)),
+        ],
+        out_specs=[pl.BlockSpec((2, B, B), lambda k: (0, 0, 0))] * 2,
+        out_shape=[
+            jax.ShapeDtypeStruct((2, B, B), F32),
+            jax.ShapeDtypeStruct((2, B, B), BF16),
+        ],
+        scratch_shapes=[pltpu.VMEM((4, B, B), F32)],
+        compiler_params=pltpu.CompilerParams(vmem_limit_bytes=40 << 20),
+        cost_estimate=pl.CostEstimate(
+            flops=4_000_000, bytes_accessed=4 << 20, transcendentals=0
+        ),
+    )(slots, x, start, far)
 
 
 def broadcast_first(block, row):
@@ -432,14 +466,17 @@
         block_columns(front), "col", 0, 0, axis_index_groups=groups, tiled=True
     )
 
-    low, inv, pan = factor_rest(gathered[1:STEPS].reshape((STEPS - 1) * B, STEPS * B), inv0)
-    factor, u = solve_and_update(scalars, own, gathered, low0, inv0, low, inv, pan)
+    far = [(c, (c + half) % cols) for c in range(cols)]
+    start = sum_fronts(slots, f, ancestor)
+    sent, gathered = lax.optimization_barrier((start[2:4], gathered))
+    received = lax.ppermute(sent, "col", far)
+    factor, u = factor_and_update(scalars, own, gathered, low0, inv0)
+    received, u = lax.optimization_barrier((received, u))
     u = lax.all_to_all(u, "col", 0, 0, axis_index_groups=groups, tiled=True)
 
-    acc = sum_blocks(start_sum_kernel, slots, f, ancestor)
-    acc = sum_blocks(end_sum_kernel, slots, u, acc)
-    received = lax.ppermute(acc[2:4], "col", [(c, (c + half) % cols) for c in range(cols)])
-    return factor[None], acc[0:2] + received
+    mine, sent = sum_updates(slots, u, start, received)
+    received = lax.ppermute(sent, "col", far)
+    return factor[None], mine + received.astype(F32)
 
 
 def solution(mesh):

time: 201 us -> 196 us (0.975)
  the two profiles are of different devices: /device:TPU:69 before, /device:TPU:48 now
where the time goes in v5:
time: 196 us
  blocking collectives  58.5 us (30%)
  Pallas kernels  47.3 us (24%)
  waiting for transfers between devices  40.4 us (21%)
  starting transfers between devices  25.2 us (13%)
  between operations  14.3 us (7%)
  local copies, waits for them, and re-layouts  7.64 us (4%)
  other arithmetic  2.39 us (1%)
    all_to_all x1, blocking collectives, shards(): u = lax.all_to_all(u, 'col', 0, 0, axis_index_groups=groups, tiled=True)  58.5 us
    pallas_call x1, Pallas kernels, factor_and_update(): pl.pallas_call(rest_kernel, in_specs=[pl.BlockSpec(memory_space=pltpu.SME...  32.3 us
    ppermute x4, waiting for transfers between devices, broadcast_first(): got = lax.ppermute(block, 'row', pairs)  22.9 us
    ppermute x2, waiting for transfers between devices, shards(): received = lax.ppermute(sent, 'col', far)  15 us
    ppermute x2, starting transfers between devices, shards(): received = lax.ppermute(sent, 'col', far)  10.6 us
    all_to_all x1, starting transfers between devices, shards(): lax.all_to_all(block_columns(front), 'col', 0, 0, axis_index_groups=group...  9.96 us
    pallas_call x1, Pallas kernels, factor_first(): pl.pallas_call(first_kernel, in_specs=[VMEM], out_specs=[VMEM, VMEM], out...  9.42 us
    ppermute x4, starting transfers between devices, broadcast_first(): got = lax.ppermute(block, 'row', pairs)  4.56 us
  transfers between devices with their start and end apart: 8, of which 4 were waited for; matrix products, arithmetic and copies ran while one was open for 1% of the time, Pallas kernels for 24%

profile of v5, /device:TPU:48, one launch (start us, length us, event | category | flops | bytes accessed | tf_op | source)
XLA Modules:
  0.0 195.7 jit_solution(5456634415807870277)
XLA Ops:
  7.2 0.0 all-gather.3.cloned.1.call-start
  7.2 0.9 slice.13
  8.1 1.8 slice.12.own_ref
  9.9 0.0 all-gather.3.cloned.1.call-update
  9.9 3.8 %shard_map.59 = bf16[16,256,256]{2,1,0:T(8,128)(2,1)} custom-call(bf16[256,4096]{1,0:T(8,128)(2,1)} %bitcast.26), custom_call_target="tpu_custom_call" | custom-call | bytes 4194304 | tf_op jit(solution)/shard_map/pallas_call | solution.py:342
  13.7 0.0 copy-start.6
  13.7 10.0 %all-to-all-start = ((bf16[16,256,256]{2,1,0:T(8,128)(2,1)}), bf16[16,256,256]{2,1,0:T(8,128)(2,1)S(1)}, u32[]{:S(2)}, u32[]{:S(2)}) async-start(bf16[16,256,256]{2,1,0:T(8,128)(2,1)} %shard_map.59), calls=%async_computation | async-start | bytes 4194304 | tf_op jit(solution)/shard_map/all_to_all | solution.py:465
  23.7 0.7 collective-permute-start
  24.4 0.0 collective-permute-done
  24.4 1.3 collective-permute-start.1
  25.8 18.7 %collective-permute-done.1 = bf16[256,256]{1,0:T(8,128)(2,1)S(1)} collective-permute-done((bf16[256,256]{1,0:T(8,128)(2,1)S(1)}, bf16[256,256]{1,0:T(8,128)(2,1)S(1)}, u32[]{:S(2)}, u32[]{:S(2)}) %collective-permute-start.1) | collective-permute-done | bytes 131104 | tf_op jit(solution)/shard_map/ppermute | solution.py:435
  44.5 1.3 collective-permute-start.2
  45.8 0.0 copy-done.6
  45.8 0.7 dynamic_slice.14
  46.5 4.2 %collective-permute-done.2 = bf16[256,256]{1,0:T(8,128)(2,1)S(1)} collective-permute-done((bf16[256,256]{1,0:T(8,128)(2,1)S(1)}, bf16[256,256]{1,0:T(8,128)(2,1)S(1)}, u32[]{:S(2)}, u32[]{:S(2)}) %collective-permute-start.2) | collective-permute-done | bytes 131104 | tf_op jit(solution)/shard_map/ppermute | solution.py:435
  50.7 1.3 collective-permute-start.3
  52.0 0.7 pad_add_fusion.scalars
  52.7 0.8 and_select_fusion.2.slots
  53.5 0.0 collective-permute-done.3
  53.5 9.4 %shard_map.61 = (f32[256,256]{1,0:T(8,128)S(1)}, f32[256,256]{1,0:T(8,128)S(1)}) custom-call(bf16[256,256]{1,0:T(8,128)(2,1)S(1)} %broadcast_select_fusion.3.a_ref), custom_call_target="tpu_custom_call" | custom-call | flops 10000000000 | bytes 1048576 | tf_op jit(solution)/shard_map/pallas_call | solution.py:159
  63.0 0.0 copy-start.2
  63.0 0.7 copy-done.2
  63.7 0.0 copy-start.4
  63.7 0.7 copy-done.4
  64.4 0.0 copy-start
  64.4 2.4 %all-to-all-done.x_ref = bf16[16,256,256]{2,1,0:T(8,128)(2,1)S(1)} async-done(((bf16[16,256,256]{2,1,0:T(8,128)(2,1)}), bf16[16,256,256]{2,1,0:T(8,128)(2,1)S(1)}, u32[]{:S(2)}, u32[]{:S(2)}) %all-to-all-start) | async-done | bytes 2097184 | tf_op jit(solution)/shard_map/all_to_all | solution.py:465
  66.7 0.0 copy-start.1
  66.7 0.9 copy-done.1
  67.7 0.8 shard_map.60.start_ref
  68.6 0.0 all-gather.3.cloned.1.call-done
  68.6 8.4 %collective-permute-start.4 = (f32[2,256,256]{2,1,0:T(8,128)S(1)}, f32[2,256,256]{2,1,0:T(8,128)S(1)}, u32[]{:S(2)}, u32[]{:S(2)}) collective-permute-start(f32[2,256,256]{2,1,0:T(8,128)S(1)} %slice.14), channel_id=1, source_target_pairs={{0,16},{1,17},{2,18},{3,19},{4,20},{5,21},{6,22},{7,23},{8,24},{9,... | collective-permute-start | bytes 1572872 | tf_op jit(solution)/shard_map/ppermute | solution.py:472
  77.0 0.0 copy-done
  77.0 0.0 copy-start.3
  77.0 0.9 copy-done.3
  77.9 0.0 copy-start.5
  77.9 0.9 copy-done.5
  78.9 32.3 %shard_map.62 = (f32[256,768]{1,0:T(8,128)}, bf16[16,256,256]{2,1,0:T(8,128)(2,1)S(1)}) custom-call(s32[2]{0:T(128)S(1)} %pad_add_fusion.scalars, bf16[256,768]{1,0:T(8,128)(2,1)S(1)} %copy-done, bf16[16,256,768]{2,1,0:T(8,128)(2,1)} %bitcast.27, f32[256,256]{1,0:T(8,128)S(1)} %copy-done.3, f32[256,256]{1,0:T(8,128)S(1)} %copy-done.5), custom_call_target="tpu_custom_call" | custom-call | flops 30000001024 | bytes 10485760 | tf_op jit(solution)/shard_map/pallas_call | solution.py:304
  111.2 0.0 collective-permute-done.4.far_ref
  111.2 58.5 %all_to_all.10.x_ref = bf16[16,256,256]{2,1,0:T(8,128)(2,1)S(1)} all-to-all(bf16[16,256,256]{2,1,0:T(8,128)(2,1)S(1)} %get-tuple-element.22), channel_id=1, replica_groups={{0,1,2,3,4,5,6,7,8,9,10,11,12,13,14,15},{16,17,18,19,20,21,22,23,24,25,..., dimensions={0} | all-to-all | bytes 4194304 | tf_op jit(solution)/shard_map/all_to_all | solution.py:475
  169.7 0.9 shard_map.63
  170.7 2.3 %collective-permute-start.5 = (bf16[2,256,256]{2,1,0:T(8,128)(2,1)S(1)}, bf16[2,256,256]{2,1,0:T(8,128)(2,1)S(1)}, u32[]{:S(2)}, u32[]{:S(2)}) collective-permute-start(bf16[2,256,256]{2,1,0:T(8,128)(2,1)S(1)} %get-tuple-element.25), channel_id=1, source_target_pairs={{0,16},{1,17},{2,18},{3,19},{4,20},{5,21},{6,22},{7,23},{8,24},{9,... | collective-permute-start | bytes 786440 | tf_op jit(solution)/shard_map/ppermute | solution.py:478
  173.0 15.0 %collective-permute-done.5 = bf16[2,256,256]{2,1,0:T(8,128)(2,1)S(1)} collective-permute-done((bf16[2,256,256]{2,1,0:T(8,128)(2,1)S(1)}, bf16[2,256,256]{2,1,0:T(8,128)(2,1)S(1)}, u32[]{:S(2)}, u32[]{:S(2)}) %collective-permute-start.5) | collective-permute-done | bytes 262176 | tf_op jit(solution)/shard_map/ppermute | solution.py:478
  188.0 0.8 convert_add_fusion
  (5 shorter events, 0.1 us)
Async XLA Ops:
  7.2 61.4 %all-gather.3.cloned.1.call-start = ((), (), s32[]{:S(2)}) async-start(), calls=%async_computation.2 | async-start | bytes 6684672 | tf_op jit(solution)/shard_map/all_gather | solution.py:462
  13.7 32.1 %copy-start.6 = (s32[32]{0:T(128)S(1)}, s32[32]{0:T(128)}, u32[]{:S(2)}) copy-start(s32[32]{0:T(128)} %param.5) | copy-start | bytes 388
  13.7 53.0 %all-to-all-start = ((bf16[16,256,256]{2,1,0:T(8,128)(2,1)}), bf16[16,256,256]{2,1,0:T(8,128)(2,1)S(1)}, u32[]{:S(2)}, u32[]{:S(2)}) async-start(bf16[16,256,256]{2,1,0:T(8,128)(2,1)} %shard_map.59), calls=%async_computation | async-start | bytes 4194304 | tf_op jit(solution)/shard_map/all_to_all | solution.py:465
  23.7 0.7 collective-permute-start
  24.4 20.0 %collective-permute-start.1 = (bf16[256,256]{1,0:T(8,128)(2,1)S(1)}, bf16[256,256]{1,0:T(8,128)(2,1)S(1)}, u32[]{:S(2)}, u32[]{:S(2)}) collective-permute-start(bf16[256,256]{1,0:T(8,128)(2,1)S(1)} %broadcast_select_fusion), channel_id=1, source_target_pairs={{0,128},{256,384},{1,129},{257,385},{2,130},{258,386},{3,131},{259... | collective-permute-start | bytes 393224 | tf_op jit(solution)/shard_map/ppermute | solution.py:435
  44.5 6.2 %collective-permute-start.2 = (bf16[256,256]{1,0:T(8,128)(2,1)S(1)}, bf16[256,256]{1,0:T(8,128)(2,1)S(1)}, u32[]{:S(2)}, u32[]{:S(2)}) collective-permute-start(bf16[256,256]{1,0:T(8,128)(2,1)S(1)} %broadcast_select_fusion.1), channel_id=1, source_target_pairs={{0,64},{128,192},{256,320},{384,448},{1,65},{129,193},{257,321},{3... | collective-permute-start | bytes 393224 | tf_op jit(solution)/shard_map/ppermute | solution.py:435
  50.7 2.8 %collective-permute-start.3 = (bf16[256,256]{1,0:T(8,128)(2,1)S(1)}, bf16[256,256]{1,0:T(8,128)(2,1)S(1)}, u32[]{:S(2)}, u32[]{:S(2)}) collective-permute-start(bf16[256,256]{1,0:T(8,128)(2,1)S(1)} %broadcast_select_fusion.2), channel_id=1, source_target_pairs={{0,32},{64,96},{128,160},{192,224},{256,288},{320,352},{384,416},{... | collective-permute-start | bytes 393224 | tf_op jit(solution)/shard_map/ppermute | solution.py:435
  63.0 0.7 copy-start.2
  63.7 0.7 copy-start.4
  64.4 12.6 %copy-start = (bf16[256,768]{1,0:T(8,128)(2,1)S(1)}, bf16[256,768]{1,0:T(8,128)(2,1)}, u32[]{:S(2)}) copy-start(bf16[256,768]{1,0:T(8,128)(2,1)} %slice.12.own_ref) | copy-start | bytes 1179652
  66.7 1.0 copy-start.1
  68.6 42.6 %collective-permute-start.4 = (f32[2,256,256]{2,1,0:T(8,128)S(1)}, f32[2,256,256]{2,1,0:T(8,128)S(1)}, u32[]{:S(2)}, u32[]{:S(2)}) collective-permute-start(f32[2,256,256]{2,1,0:T(8,128)S(1)} %slice.14), channel_id=1, source_target_pairs={{0,16},{1,17},{2,18},{3,19},{4,20},{5,21},{6,22},{7,23},{8,24},{9,... | collective-permute-start | bytes 1572872 | tf_op jit(solution)/shard_map/ppermute | solution.py:472
  77.0 1.0 copy-start.3
  77.9 0.9 copy-start.5
  170.7 17.3 %collective-permute-start.5 = (bf16[2,256,256]{2,1,0:T(8,128)(2,1)S(1)}, bf16[2,256,256]{2,1,0:T(8,128)(2,1)S(1)}, u32[]{:S(2)}, u32[]{:S(2)}) collective-permute-start(bf16[2,256,256]{2,1,0:T(8,128)(2,1)S(1)} %get-tuple-element.25), channel_id=1, source_target_pairs={{0,16},{1,17},{2,18},{3,19},{4,20},{5,21},{6,22},{7,23},{8,24},{9,... | collective-permute-start | bytes 786440 | tf_op jit(solution)/shard_map/ppermute | solution.py:478
Sparse Core Ops, SparseCore 0:
  10.7 54.4 all-gather.2

commit v6 on v5

--- a/solution.py
+++ b/solution.py
@@ -10,6 +10,7 @@
 SUB = 8
 PANEL = 32
 GROUP = 4
+H = B // 2
 VMEM = pl.BlockSpec(memory_space=pltpu.VMEM)
 ANY = pl.BlockSpec(memory_space=pl.ANY)
 F32 = jnp.float32
@@ -181,7 +182,8 @@
     low0_ref,
     inv0_ref,
     factor_ref,
-    u_ref,
+    top_ref,
+    bottom_ref,
     rows_ref,
     corner_ref,
     t_ref,
@@ -197,7 +199,7 @@
     in_sems,
     out_sems,
 ):
-    blocks = u_ref.shape[0]
+    blocks = top_ref.shape[0]
     groups = blocks // GROUP
     per_panel = blocks // (B // PANEL)
     pivots = scalars[0]
@@ -207,9 +209,12 @@
         part = pl.ds(i * GROUP, GROUP)
         return pltpu.make_async_copy(all_ref.at[part], rows_ref.at[part], in_sems.at[i])
 
-    def send(i):
+    def send(i, half):
         part = pl.ds(i * GROUP, GROUP)
-        return pltpu.make_async_copy(out_ref.at[part], u_ref.at[part], out_sems.at[i])
+        target = bottom_ref if half else top_ref
+        return pltpu.make_async_copy(
+            out_ref.at[half, part], target.at[part], out_sems.at[half, i]
+        )
 
     def cols(t):
         return slice(t * B, (t + 1) * B)
@@ -287,16 +292,26 @@
     own_step(2, mine_rest[1], low2, inv2)
 
     def last(i, carry):
+        part = pl.ds(i * GROUP, GROUP)
+        wh = high_ref[part].reshape(GROUP * B, B)
+        wl = low_part_ref[part].reshape(GROUP * B, B)
+        high, low = parts_ref[2, 0], parts_ref[2, 1]
+        x = dot_nt(wh, high) + (dot_nt(wl, high) + dot_nt(wh, low))
+        p2 = jnp.where(2 < pivots, x.astype(BF16), 0.0).astype(BF16)
         for k in range(GROUP):
             j = i * GROUP + k
-            p2 = jnp.where(2 < pivots, other_step(2, j), 0.0).astype(BF16)
-            out_ref[j] = (sum_ref[j] + dot_nt(mine_ref[:, cols(2)], p2)).astype(BF16)
-        send(i).start()
+            product = dot_nt(mine_ref[:, cols(2)], p2[k * B : (k + 1) * B])
+            u = (sum_ref[j] + product).astype(BF16)
+            out_ref[0, j] = u[:H]
+            out_ref[1, j] = u[H:]
+        send(i, 0).start()
+        send(i, 1).start()
         return carry
 
     lax.fori_loop(0, groups, last, 0)
     for i in range(groups):
-        send(i).wait()
+        send(i, 0).wait()
+        send(i, 1).wait()
 
 
 def factor_and_update(scalars, own, gathered, low0, inv0):
@@ -304,10 +319,11 @@
     return pl.pallas_call(
         rest_kernel,
         in_specs=[pl.BlockSpec(memory_space=pltpu.SMEM), VMEM, ANY, VMEM, VMEM],
-        out_specs=[VMEM, pl.BlockSpec(memory_space=pltpu.HBM)],
+        out_specs=[VMEM] + [pl.BlockSpec(memory_space=pltpu.HBM)] * 2,
         out_shape=[
             jax.ShapeDtypeStruct((B, STEPS * B), F32),
-            jax.ShapeDtypeStruct((blocks, B, B), BF16),
+            jax.ShapeDtypeStruct((blocks, H, B), BF16),
+            jax.ShapeDtypeStruct((blocks, H, B), BF16),
         ],
         scratch_shapes=[
             pltpu.VMEM((blocks, B, STEPS * B), BF16),
@@ -321,9 +337,9 @@
             pltpu.VMEM((blocks, B, B), BF16),
             pltpu.VMEM((blocks, B, B), BF16),
             pltpu.VMEM((blocks, B, B), F32),
-            pltpu.VMEM((blocks, B, B), BF16),
+            pltpu.VMEM((2, blocks, H, B), BF16),
             pltpu.SemaphoreType.DMA((blocks // GROUP,)),
-            pltpu.SemaphoreType.DMA((blocks // GROUP,)),
+            pltpu.SemaphoreType.DMA((2, blocks // GROUP)),
         ],
         compiler_params=pltpu.CompilerParams(vmem_limit_bytes=48 << 20),
         cost_estimate=pl.CostEstimate(
@@ -365,13 +381,12 @@
             acc_ref[slot] += x_ref[i].astype(F32)
 
 
-def end_sum_kernel(slots, x_ref, start_ref, far_ref, own_ref, send_ref, acc_ref):
+def end_sum_kernel(slots, x_ref, start_ref, own_ref, send_ref, acc_ref):
     k = pl.program_id(0)
 
     @pl.when(k == 0)
     def _():
-        acc_ref[0:2] = start_ref[0:2] + far_ref[...]
-        acc_ref[2:4] = jnp.zeros((2, B, B), F32)
+        acc_ref[...] = start_ref[...]
 
     for i in range(GROUP):
         slot = slots[k * GROUP + i]
@@ -383,7 +398,7 @@
     @pl.when(k == pl.num_programs(0) - 1)
     def _():
         own_ref[...] = acc_ref[0:2]
-        send_ref[...] = acc_ref[2:4].astype(BF16)
+        send_ref[...] = acc_ref[2:4]
 
 
 def sum_fronts(slots, x, ancestor):
@@ -404,27 +419,23 @@
     )(slots, x, ancestor)
 
 
-def sum_updates(slots, x, start, far):
+def sum_updates(slots, x, start, half):
     return pl.pallas_call(
         end_sum_kernel,
         grid=(x.shape[0] // GROUP,),
         in_specs=[
             pl.BlockSpec(memory_space=pltpu.SMEM),
-            pl.BlockSpec((GROUP, B, B), lambda k: (k, 0, 0)),
-            pl.BlockSpec((4, B, B), lambda k: (0, 0, 0)),
-            pl.BlockSpec((2, B, B), lambda k: (0, 0, 0)),
+            pl.BlockSpec((GROUP, H, B), lambda k: (k, 0, 0)),
+            pl.BlockSpec((4, H, B), lambda k: (0, half, 0)),
         ],
-        out_specs=[pl.BlockSpec((2, B, B), lambda k: (0, 0, 0))] * 2,
-        out_shape=[
-            jax.ShapeDtypeStruct((2, B, B), F32),
-            jax.ShapeDtypeStruct((2, B, B), BF16),
-        ],
-        scratch_shapes=[pltpu.VMEM((4, B, B), F32)],
+        out_specs=[pl.BlockSpec((2, H, B), lambda k: (0, 0, 0))] * 2,
+        out_shape=[jax.ShapeDtypeStruct((2, H, B), F32)] * 2,
+        scratch_shapes=[pltpu.VMEM((4, H, B), F32)],
         compiler_params=pltpu.CompilerParams(vmem_limit_bytes=40 << 20),
         cost_estimate=pl.CostEstimate(
-            flops=4_000_000, bytes_accessed=4 << 20, transcendentals=0
+            flops=4_000_000, bytes_accessed=2 << 20, transcendentals=0
         ),
-    )(slots, x, start, far)
+    )(slots, x, start)
 
 
 def broadcast_first(block, row):
@@ -444,39 +455,48 @@
     cols = lax.axis_size("col")
     blocks = fronts.shape[2] // B
     half = cols // 2
-    groups = [list(range(half)), list(range(half, cols))]
+    quarter = half // 2
+    lines = [list(range(half)), list(range(half, cols))]
+    shifted = [
+        list(range(quarter)) + list(range(half + quarter, cols)),
+        list(range(half, half + quarter)) + list(range(quarter, half)),
+    ]
     front = fronts[0]
 
     side = col // half
     block_col = col % half
-    first = side * half
-    piv = lax.dynamic_slice_in_dim(pivots, first, half)
-    tgt = lax.dynamic_slice_in_dim(targets, first, half, axis=0)
-    col_half = lax.dynamic_index_in_dim(tgt, block_col, 1, keepdims=False) // blocks
-    row_half = lax.dynamic_index_in_dim(tgt, row, 1, keepdims=False) // blocks
-    keep = (block_col >= piv) & (row >= piv)
-    slots = jnp.where(keep, jnp.where(col_half == side, 0, 2) + row_half, 4).astype(jnp.int32)
+    classes = jnp.arange(half, dtype=jnp.int32)
+
+    def slots_of(upper):
+        piv = jnp.where(upper, pivots[half:], pivots[:half])
+        tgt = jnp.where(upper[:, None], targets[half:], targets[:half])
+        col_half = lax.dynamic_index_in_dim(tgt, block_col, 1, keepdims=False) // blocks
+        row_half = lax.dynamic_index_in_dim(tgt, row, 1, keepdims=False) // blocks
+        keep = (block_col >= piv) & (row >= piv)
+        return jnp.where(keep, jnp.where(col_half == side, 0, 2) + row_half, 4).astype(jnp.int32)
+
+    line_slots = slots_of(jnp.broadcast_to(side == 1, (half,)))
+    first_shifted = (col < quarter) | (col >= half + quarter)
+    shifted_slots = slots_of((classes >= quarter) == first_shifted)
     scalars = jnp.stack([pivots[col], row.astype(jnp.int32)])
 
     own, corner = lax.optimization_barrier((front[:, : STEPS * B], front[:, :B]))
     gathered = lax.all_gather(own, "row", axis=0, tiled=False)
     corner = broadcast_first(corner, row)
     low0, inv0 = factor_first(corner)
-    f = lax.all_to_all(
-        block_columns(front), "col", 0, 0, axis_index_groups=groups, tiled=True
-    )
+    f = lax.all_to_all(block_columns(front), "col", 0, 0, axis_index_groups=lines, tiled=True)
+    start = sum_fronts(line_slots, f, ancestor)
+
+    factor, top, bottom = factor_and_update(scalars, own, gathered, low0, inv0)
+    top = lax.all_to_all(top, "col", 0, 0, axis_index_groups=lines, tiled=True)
+    bottom = lax.all_to_all(bottom, "col", 0, 0, axis_index_groups=shifted, tiled=True)
 
     far = [(c, (c + half) % cols) for c in range(cols)]
-    start = sum_fronts(slots, f, ancestor)
-    sent, gathered = lax.optimization_barrier((start[2:4], gathered))
-    received = lax.ppermute(sent, "col", far)
-    factor, u = factor_and_update(scalars, own, gathered, low0, inv0)
-    received, u = lax.optimization_barrier((received, u))
-    u = lax.all_to_all(u, "col", 0, 0, axis_index_groups=groups, tiled=True)
-
-    mine, sent = sum_updates(slots, u, start, received)
-    received = lax.ppermute(sent, "col", far)
-    return factor[None], mine + received.astype(F32)
+    top, top_sent = sum_updates(line_slots, top, start, 0)
+    bottom, bottom_sent = sum_updates(shifted_slots, bottom, start, 1)
+    top = top + lax.ppermute(top_sent, "col", far)
+    bottom = bottom + lax.ppermute(bottom_sent, "col", far)
+    return factor[None], jnp.concatenate([top, bottom], axis=1)
 
 
 def solution(mesh):

time: 196 us -> 202 us (1.031)
  the two profiles are of different devices: /device:TPU:48 before, /device:TPU:65 now
where the time goes in v6:
time: 202 us
  waiting for transfers between devices  72.4 us (36%)
  Pallas kernels  47.4 us (23%)
  blocking collectives  34.8 us (17%)
  starting transfers between devices  25.4 us (13%)
  between operations  14.3 us (7%)
  local copies, waits for them, and re-layouts  5.49 us (3%)
    all_to_all x1, blocking collectives, shards(): lax.all_to_all(bottom, 'col', 0, 0, axis_index_groups=shifted, tiled=True)  34.8 us
    pallas_call x1, Pallas kernels, factor_and_update(): pl.pallas_call(rest_kernel, in_specs=[pl.BlockSpec(memory_space=pltpu.SME...  29.8 us
    all_to_all x1, waiting for transfers between devices, shards(): top = lax.all_to_all(top, 'col', 0, 0, axis_index_groups=lines, tiled=True)  29 us
    all_gather x1, waiting for transfers between devices, shards(): gathered = lax.all_gather(own, 'row', axis=0, tiled=False)  24.6 us
    ppermute x1, waiting for transfers between devices, shards(): top = top + lax.ppermute(top_sent, 'col', far)  15.7 us
    pallas_call x1, Pallas kernels, factor_first(): pl.pallas_call(first_kernel, in_specs=[VMEM], out_specs=[VMEM, VMEM], out...  9.42 us
    all_to_all x1, starting transfers between devices, shards(): lax.all_to_all(block_columns(front), 'col', 0, 0, axis_index_groups=lines...  8.96 us
    all_to_all x1, starting transfers between devices, shards(): top = lax.all_to_all(top, 'col', 0, 0, axis_index_groups=lines, tiled=True)  6.07 us
  transfers between devices with their start and end apart: 9, of which 4 were waited for; matrix products, arithmetic and copies ran while one was open for 1% of the time, Pallas kernels for 24%

profile of v6, /device:TPU:65, one launch (start us, length us, event | category | flops | bytes accessed | tf_op | source)
XLA Modules:
  0.0 201.5 jit_solution(12207069962119718545)
XLA Ops:
  7.2 0.0 all-gather.3.cloned.1.call-start
  7.2 0.9 slice.29
  8.1 1.8 slice.28.own_ref
  9.9 0.0 all-gather.3.cloned.1.call-update
  9.9 0.7 collective-permute-start
  10.6 0.0 collective-permute-done
  10.6 0.7 collective-permute-start.1
  11.3 0.0 collective-permute-done.1
  11.4 0.7 collective-permute-start.2
  12.1 0.0 collective-permute-done.2
  12.1 1.3 collective-permute-start.3
  13.4 3.8 %shard_map.61 = bf16[16,256,256]{2,1,0:T(8,128)(2,1)} custom-call(bf16[256,4096]{1,0:T(8,128)(2,1)} %bitcast.22), custom_call_target="tpu_custom_call" | custom-call | bytes 4194304 | tf_op jit(solution)/shard_map/pallas_call | solution.py:358
  17.2 0.0 copy-start.5
  17.2 9.0 %all-to-all-start.1 = ((bf16[16,256,256]{2,1,0:T(8,128)(2,1)}), bf16[16,256,256]{2,1,0:T(8,128)(2,1)S(1)}, u32[]{:S(2)}, u32[]{:S(2)}) async-start(bf16[16,256,256]{2,1,0:T(8,128)(2,1)} %shard_map.61), calls=%async_computation.1 | async-start | bytes 4194304 | tf_op jit(solution)/shard_map/all_to_all | solution.py:487
  26.2 0.0 copy-done.5
  26.2 0.6 dynamic_slice.16
  26.8 0.7 pad_add_fusion.scalars
  27.5 3.1 %collective-permute-done.3 = bf16[256,256]{1,0:T(8,128)(2,1)S(1)} collective-permute-done((bf16[256,256]{1,0:T(8,128)(2,1)S(1)}, bf16[256,256]{1,0:T(8,128)(2,1)S(1)}, u32[]{:S(2)}, u32[]{:S(2)}) %collective-permute-start.3) | collective-permute-done | bytes 131104 | tf_op jit(solution)/shard_map/ppermute | solution.py:446
  30.6 0.0 copy-start.1
  30.6 9.4 %shard_map.59 = (f32[256,256]{1,0:T(8,128)S(1)}, f32[256,256]{1,0:T(8,128)S(1)}) custom-call(bf16[256,256]{1,0:T(8,128)(2,1)S(1)} %broadcast_select_fusion.3.a_ref), custom_call_target="tpu_custom_call" | custom-call | flops 10000000000 | bytes 1048576 | tf_op jit(solution)/shard_map/pallas_call | solution.py:160
  40.1 24.6 %all-gather.3.cloned.1.call-done = bf16[4096,768]{1,0:T(8,128)(2,1)} async-done(((bf16[256,768]{1,0:T(8,128)(2,1)}), bf16[4096,768]{1,0:T(8,128)(2,1)}) %all-gather.3.cloned.1.call-update) | async-done | bytes 6291472 | tf_op jit(solution)/shard_map/all_gather | solution.py:484
  64.7 0.0 copy-done.1
  64.7 29.8 %shard_map.60 = (f32[256,768]{1,0:T(8,128)}, bf16[16,128,256]{2,1,0:T(8,128)(2,1)}, bf16[16,128,256]{2,1,0:T(8,128)(2,1)S(1)}) custom-call(s32[2]{0:T(128)S(1)} %pad_add_fusion.scalars, bf16[256,768]{1,0:T(8,128)(2,1)S(1)} %copy-done.1, bf16[16,256,768]{2,1,0:T(8,128)(2,1)} %bitcast.23, f32[256,256]{1,0:T(8,128)S(1)} %get-tuple-element.15.low0_ref, ...), custom_call_target="tpu_custom_call" | custom-call | flops 30000001024 | bytes 10485760 | tf_op jit(solution)/shard_map/pallas_call | solution.py:319
  94.5 0.0 copy-start.2
  94.6 1.0 copy-done.2
  95.5 0.0 all-to-all-done.1.x_ref
  95.5 0.0 copy-start.4
  95.5 0.0 copy-start.3
  95.5 34.8 %all_to_all.15.x_ref = bf16[16,128,256]{2,1,0:T(8,128)(2,1)} all-to-all(bf16[16,128,256]{2,1,0:T(8,128)(2,1)} %copy-done.2), channel_id=1, replica_groups={{0,1,2,3,4,5,6,7,24,25,26,27,28,29,30,31},{16,17,18,19,20,21,22,23,8,9,..., dimensions={0} | all-to-all | bytes 2097152 | tf_op jit(solution)/shard_map/all_to_all | solution.py:492
  130.3 6.1 %all-to-all-start = ((bf16[16,128,256]{2,1,0:T(8,128)(2,1)}), bf16[16,128,256]{2,1,0:T(8,128)(2,1)}, u32[]{:S(2)}, u32[]{:S(2)}) async-start(bf16[16,128,256]{2,1,0:T(8,128)(2,1)} %get-tuple-element.18), calls=%async_computation | async-start | bytes 2097152 | tf_op jit(solution)/shard_map/all_to_all | solution.py:491
  136.4 0.0 copy-done.4
  136.4 0.1 slice_select_fusion.1
  136.5 0.1 and_select_fusion.5
  136.5 0.0 copy-done.3
  136.5 1.1 shard_map.62.start_ref
  137.6 0.0 copy-start
  137.6 1.2 copy-done
  138.8 0.9 shard_map.64
  139.8 3.5 %collective-permute-start.5 = (f32[2,128,256]{2,1,0:T(8,128)S(1)}, f32[2,128,256]{2,1,0:T(8,128)S(1)}, u32[]{:S(2)}, u32[]{:S(2)}) collective-permute-start(f32[2,128,256]{2,1,0:T(8,128)S(1)} %get-tuple-element.23), channel_id=1, source_target_pairs={{0,16},{1,17},{2,18},{3,19},{4,20},{5,21},{6,22},{7,23},{8,24},{9,... | collective-permute-start | bytes 786440 | tf_op jit(solution)/shard_map/ppermute | solution.py:498
  143.3 29.0 %all-to-all-done.x_ref = bf16[16,128,256]{2,1,0:T(8,128)(2,1)} async-done(((bf16[16,128,256]{2,1,0:T(8,128)(2,1)}), bf16[16,128,256]{2,1,0:T(8,128)(2,1)}, u32[]{:S(2)}, u32[]{:S(2)}) %all-to-all-start) | async-done | bytes 1048608 | tf_op jit(solution)/shard_map/all_to_all | solution.py:491
  172.3 2.3 %shard_map.63 = (f32[2,128,256]{2,1,0:T(8,128)S(1)}, f32[2,128,256]{2,1,0:T(8,128)S(1)}) custom-call(s32[16]{0:T(128)S(1)} %get-tuple-element.26.slots, bf16[16,128,256]{2,1,0:T(8,128)(2,1)} %all-to-all-done.x_ref, f32[4,256,256]{2,1,0:T(8,128)S(1)} %shard_map.62.start_ref), custom_call_target="tpu_custom_call" | custom-call | flops 4000000 | bytes 2097152 | tf_op jit(solution)/shard_map/pallas_call | solution.py:423
  174.6 3.5 %collective-permute-start.4 = (f32[2,128,256]{2,1,0:T(8,128)S(1)}, f32[2,128,256]{2,1,0:T(8,128)S(1)}, u32[]{:S(2)}, u32[]{:S(2)}) collective-permute-start(f32[2,128,256]{2,1,0:T(8,128)S(1)} %get-tuple-element.20), channel_id=1, source_target_pairs={{0,16},{1,17},{2,18},{3,19},{4,20},{5,21},{6,22},{7,23},{8,24},{9,... | collective-permute-start | bytes 786440 | tf_op jit(solution)/shard_map/ppermute | solution.py:497
  178.1 0.0 collective-permute-done.5
  178.1 15.7 %collective-permute-done.4 = f32[2,128,256]{2,1,0:T(8,128)S(1)} collective-permute-done((f32[2,128,256]{2,1,0:T(8,128)S(1)}, f32[2,128,256]{2,1,0:T(8,128)S(1)}, u32[]{:S(2)}, u32[]{:S(2)}) %collective-permute-start.4) | collective-permute-done | bytes 262176 | tf_op jit(solution)/shard_map/ppermute | solution.py:497
  193.9 0.8 pad_maximum_fusion
  (7 shorter events, 0.1 us)
Async XLA Ops:
  7.2 57.5 %all-gather.3.cloned.1.call-start = ((), (), s32[]{:S(2)}) async-start(), calls=%async_computation.3 | async-start | bytes 6684672 | tf_op jit(solution)/shard_map/all_gather | solution.py:484
  9.9 0.7 collective-permute-start
  10.6 0.7 collective-permute-start.1
  11.4 0.7 collective-permute-start.2
  12.1 18.5 %collective-permute-start.3 = (bf16[256,256]{1,0:T(8,128)(2,1)S(1)}, bf16[256,256]{1,0:T(8,128)(2,1)S(1)}, u32[]{:S(2)}, u32[]{:S(2)}) collective-permute-start(bf16[256,256]{1,0:T(8,128)(2,1)S(1)} %broadcast_select_fusion.2), channel_id=1, source_target_pairs={{0,32},{64,96},{128,160},{192,224},{256,288},{320,352},{384,416},{... | collective-permute-start | bytes 393224 | tf_op jit(solution)/shard_map/ppermute | solution.py:446
  17.2 9.0 %copy-start.5 = (s32[32]{0:T(128)S(1)}, s32[32]{0:T(128)}, u32[]{:S(2)}) copy-start(s32[32]{0:T(128)} %param.5) | copy-start | bytes 388
  17.2 78.3 %all-to-all-start.1 = ((bf16[16,256,256]{2,1,0:T(8,128)(2,1)}), bf16[16,256,256]{2,1,0:T(8,128)(2,1)S(1)}, u32[]{:S(2)}, u32[]{:S(2)}) async-start(bf16[16,256,256]{2,1,0:T(8,128)(2,1)} %shard_map.61), calls=%async_computation.1 | async-start | bytes 4194304 | tf_op jit(solution)/shard_map/all_to_all | solution.py:487
  30.6 34.1 %copy-start.1 = (bf16[256,768]{1,0:T(8,128)(2,1)S(1)}, bf16[256,768]{1,0:T(8,128)(2,1)}, u32[]{:S(2)}) copy-start(bf16[256,768]{1,0:T(8,128)(2,1)} %slice.28.own_ref) | copy-start | bytes 1179652
  94.5 1.0 copy-start.2
  95.5 40.8 %copy-start.4 = (s32[32,16]{0,1:T(8,128)S(1)}, s32[32,16]{0,1:T(8,128)}, u32[]{:S(2)}) copy-start(s32[32,16]{0,1:T(8,128)} %param.6) | copy-start | bytes 6148
  95.5 41.0 %copy-start.3 = (bf16[2,256,256]{2,1,0:T(8,128)(2,1)S(1)}, bf16[2,256,256]{2,1,0:T(8,128)(2,1)}, u32[]{:S(2)}) copy-start(bf16[2,256,256]{2,1,0:T(8,128)(2,1)} %anc_ref.1) | copy-start | bytes 786436
  130.3 42.0 %all-to-all-start = ((bf16[16,128,256]{2,1,0:T(8,128)(2,1)}), bf16[16,128,256]{2,1,0:T(8,128)(2,1)}, u32[]{:S(2)}, u32[]{:S(2)}) async-start(bf16[16,128,256]{2,1,0:T(8,128)(2,1)} %get-tuple-element.18), calls=%async_computation | async-start | bytes 2097152 | tf_op jit(solution)/shard_map/all_to_all | solution.py:491
  137.6 1.2 copy-start
  139.8 38.3 %collective-permute-start.5 = (f32[2,128,256]{2,1,0:T(8,128)S(1)}, f32[2,128,256]{2,1,0:T(8,128)S(1)}, u32[]{:S(2)}, u32[]{:S(2)}) collective-permute-start(f32[2,128,256]{2,1,0:T(8,128)S(1)} %get-tuple-element.23), channel_id=1, source_target_pairs={{0,16},{1,17},{2,18},{3,19},{4,20},{5,21},{6,22},{7,23},{8,24},{9,... | collective-permute-start | bytes 786440 | tf_op jit(solution)/shard_map/ppermute | solution.py:498
  174.6 19.3 %collective-permute-start.4 = (f32[2,128,256]{2,1,0:T(8,128)S(1)}, f32[2,128,256]{2,1,0:T(8,128)S(1)}, u32[]{:S(2)}, u32[]{:S(2)}) collective-permute-start(f32[2,128,256]{2,1,0:T(8,128)S(1)} %get-tuple-element.20), channel_id=1, source_target_pairs={{0,16},{1,17},{2,18},{3,19},{4,20},{5,21},{6,22},{7,23},{8,24},{9,... | collective-permute-start | bytes 786440 | tf_op jit(solution)/shard_map/ppermute | solution.py:497
Sparse Core Ops, SparseCore 0:
  10.7 53.9 all-gather.2

commit v7 on v5

--- a/solution.py
+++ b/solution.py
@@ -287,10 +287,16 @@
     own_step(2, mine_rest[1], low2, inv2)
 
     def last(i, carry):
+        part = pl.ds(i * GROUP, GROUP)
+        wh = high_ref[part].reshape(GROUP * B, B)
+        wl = low_part_ref[part].reshape(GROUP * B, B)
+        high, low = parts_ref[2, 0], parts_ref[2, 1]
+        x = dot_nt(wh, high) + (dot_nt(wl, high) + dot_nt(wh, low))
+        p2 = jnp.where(2 < pivots, x.astype(BF16), 0.0).astype(BF16)
         for k in range(GROUP):
             j = i * GROUP + k
-            p2 = jnp.where(2 < pivots, other_step(2, j), 0.0).astype(BF16)
-            out_ref[j] = (sum_ref[j] + dot_nt(mine_ref[:, cols(2)], p2)).astype(BF16)
+            product = dot_nt(mine_ref[:, cols(2)], p2[k * B : (k + 1) * B])
+            out_ref[j] = (sum_ref[j] + product).astype(BF16)
         send(i).start()
         return carry
 
@@ -365,13 +371,12 @@
             acc_ref[slot] += x_ref[i].astype(F32)
 
 
-def end_sum_kernel(slots, x_ref, start_ref, far_ref, own_ref, send_ref, acc_ref):
+def end_sum_kernel(slots, x_ref, start_ref, own_ref, send_ref, acc_ref):
     k = pl.program_id(0)
 
     @pl.when(k == 0)
     def _():
-        acc_ref[0:2] = start_ref[0:2] + far_ref[...]
-        acc_ref[2:4] = jnp.zeros((2, B, B), F32)
+        acc_ref[...] = start_ref[...]
 
     for i in range(GROUP):
         slot = slots[k * GROUP + i]
@@ -383,7 +388,7 @@
     @pl.when(k == pl.num_programs(0) - 1)
     def _():
         own_ref[...] = acc_ref[0:2]
-        send_ref[...] = acc_ref[2:4].astype(BF16)
+        send_ref[...] = acc_ref[2:4]
 
 
 def sum_fronts(slots, x, ancestor):
@@ -404,7 +409,7 @@
     )(slots, x, ancestor)
 
 
-def sum_updates(slots, x, start, far):
+def sum_updates(slots, x, start):
     return pl.pallas_call(
         end_sum_kernel,
         grid=(x.shape[0] // GROUP,),
@@ -412,19 +417,15 @@
             pl.BlockSpec(memory_space=pltpu.SMEM),
             pl.BlockSpec((GROUP, B, B), lambda k: (k, 0, 0)),
             pl.BlockSpec((4, B, B), lambda k: (0, 0, 0)),
-            pl.BlockSpec((2, B, B), lambda k: (0, 0, 0)),
         ],
         out_specs=[pl.BlockSpec((2, B, B), lambda k: (0, 0, 0))] * 2,
-        out_shape=[
-            jax.ShapeDtypeStruct((2, B, B), F32),
-            jax.ShapeDtypeStruct((2, B, B), BF16),
-        ],
+        out_shape=[jax.ShapeDtypeStruct((2, B, B), F32)] * 2,
         scratch_shapes=[pltpu.VMEM((4, B, B), F32)],
         compiler_params=pltpu.CompilerParams(vmem_limit_bytes=40 << 20),
         cost_estimate=pl.CostEstimate(
             flops=4_000_000, bytes_accessed=4 << 20, transcendentals=0
         ),
-    )(slots, x, start, far)
+    )(slots, x, start)
 
 
 def broadcast_first(block, row):
@@ -466,17 +467,12 @@
         block_columns(front), "col", 0, 0, axis_index_groups=groups, tiled=True
     )
 
-    far = [(c, (c + half) % cols) for c in range(cols)]
     start = sum_fronts(slots, f, ancestor)
-    sent, gathered = lax.optimization_barrier((start[2:4], gathered))
-    received = lax.ppermute(sent, "col", far)
     factor, u = factor_and_update(scalars, own, gathered, low0, inv0)
-    received, u = lax.optimization_barrier((received, u))
     u = lax.all_to_all(u, "col", 0, 0, axis_index_groups=groups, tiled=True)
-
-    mine, sent = sum_updates(slots, u, start, received)
-    received = lax.ppermute(sent, "col", far)
-    return factor[None], mine + received.astype(F32)
+    mine, sent = sum_updates(slots, u, start)
+    received = lax.ppermute(sent, "col", [(c, (c + half) % cols) for c in range(cols)])
+    return factor[None], mine + received
 
 
 def solution(mesh):

time: 196 us -> 192 us (0.980)
  the two profiles are of different devices: /device:TPU:48 before, /device:TPU:69 now
where the time goes in v7:
time: 192 us; the launch traced here: 191 us
  waiting for transfers between devices  98 us (51%)
  Pallas kernels  45.8 us (24%)
  starting transfers between devices  25.9 us (13%)
  between operations  14.2 us (7%)
  local copies, waits for them, and re-layouts  4.62 us (2%)
  other arithmetic  2.49 us (1%)
    all_to_all x1, waiting for transfers between devices, shards(): u = lax.all_to_all(u, 'col', 0, 0, axis_index_groups=groups, tiled=True)  45.7 us
    pallas_call x1, Pallas kernels, factor_and_update(): pl.pallas_call(rest_kernel, in_specs=[pl.BlockSpec(memory_space=pltpu.SME...  29 us
    all_gather x1, waiting for transfers between devices, shards(): gathered = lax.all_gather(own, 'row', axis=0, tiled=False)  24.6 us
    ppermute x1, waiting for transfers between devices, shards(): lax.ppermute(sent, 'col', [(c, (c + half) % cols) for c in range(cols)])  24.6 us
    pallas_call x1, Pallas kernels, factor_first(): pl.pallas_call(first_kernel, in_specs=[VMEM], out_specs=[VMEM, VMEM], out...  9.42 us
    all_to_all x1, starting transfers between devices, shards(): lax.all_to_all(block_columns(front), 'col', 0, 0, axis_index_groups=group...  8.91 us
    all_to_all x1, starting transfers between devices, shards(): u = lax.all_to_all(u, 'col', 0, 0, axis_index_groups=groups, tiled=True)  7.48 us
    ppermute x1, starting transfers between devices, shards(): lax.ppermute(sent, 'col', [(c, (c + half) % cols) for c in range(cols)])  6.22 us
  transfers between devices with their start and end apart: 8, of which 4 were waited for; matrix products, arithmetic and copies ran while one was open for 1% of the time, Pallas kernels for 23%

profile of v7, /device:TPU:69, one launch (start us, length us, event | category | flops | bytes accessed | tf_op | source)
XLA Modules:
  0.0 191.1 jit_solution(9961580301034771700)
XLA Ops:
  7.2 0.0 all-gather.3.cloned.1.call-start
  7.2 0.9 slice.9
  8.1 1.8 slice.8.own_ref
  9.9 0.0 all-gather.3.cloned.1.call-update
  9.9 0.7 collective-permute-start
  10.6 0.0 collective-permute-done
  10.6 0.7 collective-permute-start.1
  11.3 0.0 collective-permute-done.1
  11.4 0.7 collective-permute-start.2
  12.1 0.0 collective-permute-done.2
  12.1 1.3 collective-permute-start.3
  13.4 3.8 %shard_map.61 = bf16[16,256,256]{2,1,0:T(8,128)(2,1)} custom-call(bf16[256,4096]{1,0:T(8,128)(2,1)} %bitcast.26), custom_call_target="tpu_custom_call" | custom-call | bytes 4194304 | tf_op jit(solution)/shard_map/pallas_call | solution.py:348
  17.2 0.0 copy-start.3
  17.2 8.9 %all-to-all-start.1 = ((bf16[16,256,256]{2,1,0:T(8,128)(2,1)}), bf16[16,256,256]{2,1,0:T(8,128)(2,1)S(1)}, u32[]{:S(2)}, u32[]{:S(2)}) async-start(bf16[16,256,256]{2,1,0:T(8,128)(2,1)} %shard_map.61), calls=%async_computation.1 | async-start | bytes 4194304 | tf_op jit(solution)/shard_map/all_to_all | solution.py:466
  26.1 0.0 copy-done.3
  26.2 0.6 dynamic_slice.14
  26.7 0.7 pad_add_fusion.scalars
  27.5 3.2 %collective-permute-done.3 = bf16[256,256]{1,0:T(8,128)(2,1)S(1)} collective-permute-done((bf16[256,256]{1,0:T(8,128)(2,1)S(1)}, bf16[256,256]{1,0:T(8,128)(2,1)S(1)}, u32[]{:S(2)}, u32[]{:S(2)}) %collective-permute-start.3) | collective-permute-done | bytes 131104 | tf_op jit(solution)/shard_map/ppermute | solution.py:436
  30.6 0.0 copy-start.1
  30.6 9.4 %shard_map.59 = (f32[256,256]{1,0:T(8,128)S(1)}, f32[256,256]{1,0:T(8,128)S(1)}) custom-call(bf16[256,256]{1,0:T(8,128)(2,1)S(1)} %broadcast_select_fusion.3.a_ref), custom_call_target="tpu_custom_call" | custom-call | flops 10000000000 | bytes 1048576 | tf_op jit(solution)/shard_map/pallas_call | solution.py:159
  40.1 24.6 %all-gather.3.cloned.1.call-done = bf16[4096,768]{1,0:T(8,128)(2,1)} async-done(((bf16[256,768]{1,0:T(8,128)(2,1)}), bf16[4096,768]{1,0:T(8,128)(2,1)}) %all-gather.3.cloned.1.call-update) | async-done | bytes 6291472 | tf_op jit(solution)/shard_map/all_gather | solution.py:463
  64.6 0.0 copy-done.1
  64.7 29.0 %shard_map.60 = (f32[256,768]{1,0:T(8,128)}, bf16[16,256,256]{2,1,0:T(8,128)(2,1)S(1)}) custom-call(s32[2]{0:T(128)S(1)} %pad_add_fusion.scalars, bf16[256,768]{1,0:T(8,128)(2,1)S(1)} %copy-done.1, bf16[16,256,768]{2,1,0:T(8,128)(2,1)} %bitcast.27, f32[256,256]{1,0:T(8,128)S(1)} %get-tuple-element.12.low0_ref, f32[256,256]{1,0:T(8,128)S(1)} %get-tuple-element.13.inv0_ref), custom_call_target="tpu_custom_call" | custom-call | flops 30000001024 | bytes 10485760 | tf_op jit(solution)/shard_map/pallas_call | solution.py:310
  93.7 0.0 copy-start
  93.7 1.3 copy-done
  95.0 0.0 all-to-all-done.1.x_ref
  95.0 0.0 copy-start.2
  95.0 7.5 %all-to-all-start = ((bf16[16,256,256]{2,1,0:T(8,128)(2,1)}), bf16[16,256,256]{2,1,0:T(8,128)(2,1)}, u32[]{:S(2)}, u32[]{:S(2)}) async-start(bf16[16,256,256]{2,1,0:T(8,128)(2,1)} %copy-done), calls=%async_computation | async-start | bytes 4194304 | tf_op jit(solution)/shard_map/all_to_all | solution.py:472
  102.5 0.8 and_select_fusion.2.slots
  103.3 0.0 copy-done.2
  103.4 1.0 shard_map.62.start_ref
  104.3 45.7 %all-to-all-done.x_ref = bf16[16,256,256]{2,1,0:T(8,128)(2,1)} async-done(((bf16[16,256,256]{2,1,0:T(8,128)(2,1)}), bf16[16,256,256]{2,1,0:T(8,128)(2,1)}, u32[]{:S(2)}, u32[]{:S(2)}) %all-to-all-start) | async-done | bytes 2097184 | tf_op jit(solution)/shard_map/all_to_all | solution.py:472
  150.0 2.6 %shard_map.63 = (f32[2,256,256]{2,1,0:T(8,128)S(1)}, f32[2,256,256]{2,1,0:T(8,128)S(1)}) custom-call(s32[16]{0:T(128)S(1)} %and_select_fusion.2.slots, bf16[16,256,256]{2,1,0:T(8,128)(2,1)} %all-to-all-done.x_ref, f32[4,256,256]{2,1,0:T(8,128)S(1)} %shard_map.62.start_ref), custom_call_target="tpu_custom_call" | custom-call | flops 4000000 | bytes 4194304 | tf_op jit(solution)/shard_map/pallas_call | solution.py:413
  152.6 6.2 %collective-permute-start.4 = (f32[2,256,256]{2,1,0:T(8,128)S(1)}, f32[2,256,256]{2,1,0:T(8,128)S(1)}, u32[]{:S(2)}, u32[]{:S(2)}) collective-permute-start(f32[2,256,256]{2,1,0:T(8,128)S(1)} %get-tuple-element.17), channel_id=1, source_target_pairs={{0,16},{1,17},{2,18},{3,19},{4,20},{5,21},{6,22},{7,23},{8,24},{9,... | collective-permute-start | bytes 1572872 | tf_op jit(solution)/shard_map/ppermute | solution.py:474
  158.8 24.6 %collective-permute-done.4 = f32[2,256,256]{2,1,0:T(8,128)S(1)} collective-permute-done((f32[2,256,256]{2,1,0:T(8,128)S(1)}, f32[2,256,256]{2,1,0:T(8,128)S(1)}, u32[]{:S(2)}, u32[]{:S(2)}) %collective-permute-start.4) | collective-permute-done | bytes 524320 | tf_op jit(solution)/shard_map/ppermute | solution.py:474
  183.4 0.9 add.53
  (4 shorter events, 0.1 us)
Async XLA Ops:
  7.2 57.5 %all-gather.3.cloned.1.call-start = ((), (), s32[]{:S(2)}) async-start(), calls=%async_computation.2 | async-start | bytes 6684672 | tf_op jit(solution)/shard_map/all_gather | solution.py:463
  9.9 0.7 collective-permute-start
  10.6 0.7 collective-permute-start.1
  11.4 0.7 collective-permute-start.2
  12.1 18.5 %collective-permute-start.3 = (bf16[256,256]{1,0:T(8,128)(2,1)S(1)}, bf16[256,256]{1,0:T(8,128)(2,1)S(1)}, u32[]{:S(2)}, u32[]{:S(2)}) collective-permute-start(bf16[256,256]{1,0:T(8,128)(2,1)S(1)} %broadcast_select_fusion.2), channel_id=1, source_target_pairs={{0,32},{64,96},{128,160},{192,224},{256,288},{320,352},{384,416},{... | collective-permute-start | bytes 393224 | tf_op jit(solution)/shard_map/ppermute | solution.py:436
  17.2 8.9 %copy-start.3 = (s32[32]{0:T(128)S(1)}, s32[32]{0:T(128)}, u32[]{:S(2)}) copy-start(s32[32]{0:T(128)} %param.5) | copy-start | bytes 388
  17.2 77.8 %all-to-all-start.1 = ((bf16[16,256,256]{2,1,0:T(8,128)(2,1)}), bf16[16,256,256]{2,1,0:T(8,128)(2,1)S(1)}, u32[]{:S(2)}, u32[]{:S(2)}) async-start(bf16[16,256,256]{2,1,0:T(8,128)(2,1)} %shard_map.61), calls=%async_computation.1 | async-start | bytes 4194304 | tf_op jit(solution)/shard_map/all_to_all | solution.py:466
  30.6 34.0 %copy-start.1 = (bf16[256,768]{1,0:T(8,128)(2,1)S(1)}, bf16[256,768]{1,0:T(8,128)(2,1)}, u32[]{:S(2)}) copy-start(bf16[256,768]{1,0:T(8,128)(2,1)} %slice.8.own_ref) | copy-start | bytes 1179652
  93.7 1.3 copy-start
  95.0 8.3 %copy-start.2 = (bf16[2,256,256]{2,1,0:T(8,128)(2,1)S(1)}, bf16[2,256,256]{2,1,0:T(8,128)(2,1)}, u32[]{:S(2)}) copy-start(bf16[2,256,256]{2,1,0:T(8,128)(2,1)} %anc_ref.1) | copy-start | bytes 786436
  95.0 55.0 %all-to-all-start = ((bf16[16,256,256]{2,1,0:T(8,128)(2,1)}), bf16[16,256,256]{2,1,0:T(8,128)(2,1)}, u32[]{:S(2)}, u32[]{:S(2)}) async-start(bf16[16,256,256]{2,1,0:T(8,128)(2,1)} %copy-done), calls=%async_computation | async-start | bytes 4194304 | tf_op jit(solution)/shard_map/all_to_all | solution.py:472
  152.6 30.8 %collective-permute-start.4 = (f32[2,256,256]{2,1,0:T(8,128)S(1)}, f32[2,256,256]{2,1,0:T(8,128)S(1)}, u32[]{:S(2)}, u32[]{:S(2)}) collective-permute-start(f32[2,256,256]{2,1,0:T(8,128)S(1)} %get-tuple-element.17), channel_id=1, source_target_pairs={{0,16},{1,17},{2,18},{3,19},{4,20},{5,21},{6,22},{7,23},{8,24},{9,... | collective-permute-start | bytes 1572872 | tf_op jit(solution)/shard_map/ppermute | solution.py:474
Sparse Core Ops, SparseCore 0:
  10.7 53.9 all-gather.2

commit v8 on v7

--- a/solution.py
+++ b/solution.py
@@ -371,24 +371,26 @@
             acc_ref[slot] += x_ref[i].astype(F32)
 
 
-def end_sum_kernel(slots, x_ref, start_ref, own_ref, send_ref, acc_ref):
-    k = pl.program_id(0)
-
-    @pl.when(k == 0)
-    def _():
-        acc_ref[...] = start_ref[...]
-
-    for i in range(GROUP):
-        slot = slots[k * GROUP + i]
+def end_sum_kernel(slots, x_ref, start_ref, own_ref, up_ref, down_ref, acc_ref, block_ref, sems):
+    count = x_ref.shape[0]
+
+    def fetch(k):
+        return pltpu.make_async_copy(x_ref.at[k], block_ref.at[k], sems.at[k])
+
+    for k in range(count):
+        fetch(k).start()
+    acc_ref[...] = start_ref[...]
+    for k in range(count):
+        fetch(k).wait()
+        slot = slots[k]
 
         @pl.when(slot < 4)
-        def _(i=i, slot=slot):
-            acc_ref[slot] -= x_ref[i].astype(F32)
-
-    @pl.when(k == pl.num_programs(0) - 1)
-    def _():
-        own_ref[...] = acc_ref[0:2]
-        send_ref[...] = acc_ref[2:4]
+        def _(k=k, slot=slot):
+            acc_ref[slot] -= block_ref[k].astype(F32)
+
+    own_ref[...] = acc_ref[0:2]
+    up_ref[...] = acc_ref[2]
+    down_ref[...] = acc_ref[3]
 
 
 def sum_fronts(slots, x, ancestor):
@@ -410,17 +412,21 @@
 
 
 def sum_updates(slots, x, start):
+    count = x.shape[0]
     return pl.pallas_call(
         end_sum_kernel,
-        grid=(x.shape[0] // GROUP,),
-        in_specs=[
-            pl.BlockSpec(memory_space=pltpu.SMEM),
-            pl.BlockSpec((GROUP, B, B), lambda k: (k, 0, 0)),
-            pl.BlockSpec((4, B, B), lambda k: (0, 0, 0)),
+        in_specs=[pl.BlockSpec(memory_space=pltpu.SMEM), ANY, VMEM],
+        out_specs=[VMEM, VMEM, VMEM],
+        out_shape=[
+            jax.ShapeDtypeStruct((2, B, B), F32),
+            jax.ShapeDtypeStruct((B, B), F32),
+            jax.ShapeDtypeStruct((B, B), F32),
         ],
-        out_specs=[pl.BlockSpec((2, B, B), lambda k: (0, 0, 0))] * 2,
-        out_shape=[jax.ShapeDtypeStruct((2, B, B), F32)] * 2,
-        scratch_shapes=[pltpu.VMEM((4, B, B), F32)],
+        scratch_shapes=[
+            pltpu.VMEM((4, B, B), F32),
+            pltpu.VMEM((count, B, B), BF16),
+            pltpu.SemaphoreType.DMA((count,)),
+        ],
         compiler_params=pltpu.CompilerParams(vmem_limit_bytes=40 << 20),
         cost_estimate=pl.CostEstimate(
             flops=4_000_000, bytes_accessed=4 << 20, transcendentals=0
@@ -470,9 +476,12 @@
     start = sum_fronts(slots, f, ancestor)
     factor, u = factor_and_update(scalars, own, gathered, low0, inv0)
     u = lax.all_to_all(u, "col", 0, 0, axis_index_groups=groups, tiled=True)
-    mine, sent = sum_updates(slots, u, start)
-    received = lax.ppermute(sent, "col", [(c, (c + half) % cols) for c in range(cols)])
-    return factor[None], mine + received
+    mine, up, down = sum_updates(slots, u, start)
+    step = half // 2
+    for _ in range(2):
+        up = lax.ppermute(up, "col", [(c, (c + step) % cols) for c in range(cols)])
+        down = lax.ppermute(down, "col", [(c, (c - step) % cols) for c in range(cols)])
+    return factor[None], mine + jnp.stack([up, down])
 
 
 def solution(mesh):

time: 192 us -> 196 us (1.021)
  the two profiles are of different devices: /device:TPU:69 before, /device:TPU:64 now
where the time goes in v8:
time: 196 us
  waiting for transfers between devices  78.9 us (40%)
  starting transfers between devices  49.9 us (25%)
  Pallas kernels  45.7 us (23%)
  between operations  14.2 us (7%)
  local copies, waits for them, and re-layouts  4.61 us (2%)
  other arithmetic  2.49 us (1%)
    all_to_all x1, waiting for transfers between devices, shards(): u = lax.all_to_all(u, 'col', 0, 0, axis_index_groups=groups, tiled=True)  46 us
    pallas_call x1, Pallas kernels, factor_and_update(): pl.pallas_call(rest_kernel, in_specs=[pl.BlockSpec(memory_space=pltpu.SME...  29.2 us
    ppermute x4, starting transfers between devices, broadcast_first(): got = lax.ppermute(block, 'row', pairs)  11.6 us
    ppermute x2, starting transfers between devices, shards(): up = lax.ppermute(up, 'col', [(c, (c + step) % cols) for c in range(cols)])  11.4 us
    all_to_all x1, starting transfers between devices, shards(): lax.all_to_all(block_columns(front), 'col', 0, 0, axis_index_groups=group...  11 us
    ppermute x2, waiting for transfers between devices, shards(): up = lax.ppermute(up, 'col', [(c, (c + step) % cols) for c in range(cols)])  10.1 us
    all_gather x1, waiting for transfers between devices, shards(): gathered = lax.all_gather(own, 'row', axis=0, tiled=False)  9.56 us
    pallas_call x1, Pallas kernels, factor_first(): pl.pallas_call(first_kernel, in_specs=[VMEM], out_specs=[VMEM, VMEM], out...  9.43 us
  transfers between devices with their start and end apart: 11, of which 8 were waited for; matrix products, arithmetic and copies ran while one was open for 1% of the time, Pallas kernels for 22%

profile of v8, /device:TPU:64, one launch (start us, length us, event | category | flops | bytes accessed | tf_op | source)
XLA Modules:
  0.0 195.9 jit_solution(6557892891933804313)
XLA Ops:
  7.2 0.0 all-gather.3.cloned.1.call-start
  7.2 0.9 slice.9
  8.1 1.8 slice.8.own_ref
  9.9 0.0 all-gather.3.cloned.1.call-update
  9.9 7.7 %collective-permute-start = (bf16[256,256]{1,0:T(8,128)(2,1)S(1)}, bf16[256,256]{1,0:T(8,128)(2,1)S(1)}, u32[]{:S(2)}, u32[]{:S(2)}) collective-permute-start(bf16[256,256]{1,0:T(8,128)(2,1)S(1)} %slice.9), channel_id=1, source_target_pairs={{0,256},{1,257},{2,258},{3,259},{4,260},{5,261},{6,262},{7,263},{8... | collective-permute-start | bytes 393224 | tf_op jit(solution)/shard_map/ppermute | solution.py:442
  17.7 2.5 %collective-permute-done = bf16[256,256]{1,0:T(8,128)(2,1)S(1)} collective-permute-done((bf16[256,256]{1,0:T(8,128)(2,1)S(1)}, bf16[256,256]{1,0:T(8,128)(2,1)S(1)}, u32[]{:S(2)}, u32[]{:S(2)}) %collective-permute-start) | collective-permute-done | bytes 131104 | tf_op jit(solution)/shard_map/ppermute | solution.py:442
  20.2 1.3 collective-permute-start.1
  21.5 2.5 %collective-permute-done.1 = bf16[256,256]{1,0:T(8,128)(2,1)S(1)} collective-permute-done((bf16[256,256]{1,0:T(8,128)(2,1)S(1)}, bf16[256,256]{1,0:T(8,128)(2,1)S(1)}, u32[]{:S(2)}, u32[]{:S(2)}) %collective-permute-start.1) | collective-permute-done | bytes 131104 | tf_op jit(solution)/shard_map/ppermute | solution.py:442
  24.0 1.3 collective-permute-start.2
  25.3 2.5 %collective-permute-done.2 = bf16[256,256]{1,0:T(8,128)(2,1)S(1)} collective-permute-done((bf16[256,256]{1,0:T(8,128)(2,1)S(1)}, bf16[256,256]{1,0:T(8,128)(2,1)S(1)}, u32[]{:S(2)}, u32[]{:S(2)}) %collective-permute-start.2) | collective-permute-done | bytes 131104 | tf_op jit(solution)/shard_map/ppermute | solution.py:442
  27.8 1.3 collective-permute-start.3
  29.1 3.8 %shard_map.61 = bf16[16,256,256]{2,1,0:T(8,128)(2,1)} custom-call(bf16[256,4096]{1,0:T(8,128)(2,1)} %bitcast.28), custom_call_target="tpu_custom_call" | custom-call | bytes 4194304 | tf_op jit(solution)/shard_map/pallas_call | solution.py:348
  33.0 0.0 copy-start.3
  33.0 11.0 %all-to-all-start.1 = ((bf16[16,256,256]{2,1,0:T(8,128)(2,1)}), bf16[16,256,256]{2,1,0:T(8,128)(2,1)S(1)}, u32[]{:S(2)}, u32[]{:S(2)}) async-start(bf16[16,256,256]{2,1,0:T(8,128)(2,1)} %shard_map.61), calls=%async_computation.1 | async-start | bytes 4194304 | tf_op jit(solution)/shard_map/all_to_all | solution.py:472
  43.9 0.0 copy-done.3
  43.9 0.6 dynamic_slice.14
  44.5 0.7 pad_add_fusion.scalars
  45.2 0.0 collective-permute-done.3
  45.3 0.0 copy-start.1
  45.3 9.4 %shard_map.59 = (f32[256,256]{1,0:T(8,128)S(1)}, f32[256,256]{1,0:T(8,128)S(1)}) custom-call(bf16[256,256]{1,0:T(8,128)(2,1)S(1)} %broadcast_select_fusion.3.a_ref), custom_call_target="tpu_custom_call" | custom-call | flops 10000000000 | bytes 1048576 | tf_op jit(solution)/shard_map/pallas_call | solution.py:159
  54.7 9.6 %all-gather.3.cloned.1.call-done = bf16[4096,768]{1,0:T(8,128)(2,1)} async-done(((bf16[256,768]{1,0:T(8,128)(2,1)}), bf16[4096,768]{1,0:T(8,128)(2,1)}) %all-gather.3.cloned.1.call-update) | async-done | bytes 6291472 | tf_op jit(solution)/shard_map/all_gather | solution.py:469
  64.3 0.0 copy-done.1
  64.3 29.2 %shard_map.60 = (f32[256,768]{1,0:T(8,128)}, bf16[16,256,256]{2,1,0:T(8,128)(2,1)S(1)}) custom-call(s32[2]{0:T(128)S(1)} %pad_add_fusion.scalars, bf16[256,768]{1,0:T(8,128)(2,1)S(1)} %copy-done.1, bf16[16,256,768]{2,1,0:T(8,128)(2,1)} %bitcast.31, f32[256,256]{1,0:T(8,128)S(1)} %get-tuple-element.13.low0_ref, f32[256,256]{1,0:T(8,128)S(1)} %get-tuple-element.14.inv0_ref), custom_call_target="tpu_custom_call" | custom-call | flops 30000001024 | bytes 10485760 | tf_op jit(solution)/shard_map/pallas_call | solution.py:310
  93.5 0.0 copy-start
  93.5 1.3 copy-done
  94.9 0.0 all-to-all-done.1.x_ref
  94.9 0.0 copy-start.2
  94.9 8.0 %all-to-all-start = ((bf16[16,256,256]{2,1,0:T(8,128)(2,1)}), bf16[16,256,256]{2,1,0:T(8,128)(2,1)}, u32[]{:S(2)}, u32[]{:S(2)}) async-start(bf16[16,256,256]{2,1,0:T(8,128)(2,1)} %copy-done), calls=%async_computation | async-start | bytes 4194304 | tf_op jit(solution)/shard_map/all_to_all | solution.py:478
  102.9 0.8 and_select_fusion.2.slots
  103.8 0.0 copy-done.2
  103.8 0.9 shard_map.62.start_ref
  104.6 46.0 %all-to-all-done.x_ref = bf16[16,256,256]{2,1,0:T(8,128)(2,1)} async-done(((bf16[16,256,256]{2,1,0:T(8,128)(2,1)}), bf16[16,256,256]{2,1,0:T(8,128)(2,1)}, u32[]{:S(2)}, u32[]{:S(2)}) %all-to-all-start) | async-done | bytes 2097184 | tf_op jit(solution)/shard_map/all_to_all | solution.py:478
  150.6 2.3 %shard_map.63 = (f32[2,256,256]{2,1,0:T(8,128)S(1)}, f32[256,256]{1,0:T(8,128)S(1)}, f32[256,256]{1,0:T(8,128)S(1)}) custom-call(s32[16]{0:T(128)S(1)} %and_select_fusion.2.slots, bf16[16,256,256]{2,1,0:T(8,128)(2,1)} %all-to-all-done.x_ref, f32[4,256,256]{2,1,0:T(8,128)S(1)} %shard_map.62.start_ref), custom_call_target="tpu_custom_call" | custom-call | flops 4000000 | bytes 4194304 | tf_op jit(solution)/shard_map/pallas_call | solution.py:416
  152.9 2.1 %collective-permute-start.4 = (f32[256,256]{1,0:T(8,128)S(1)}, f32[256,256]{1,0:T(8,128)S(1)}, u32[]{:S(2)}, u32[]{:S(2)}) collective-permute-start(f32[256,256]{1,0:T(8,128)S(1)} %get-tuple-element.18), channel_id=1, source_target_pairs={{0,8},{1,9},{2,10},{3,11},{4,12},{5,13},{6,14},{7,15},{8,16},{9,17... | collective-permute-start | bytes 786440 | tf_op jit(solution)/shard_map/ppermute | solution.py:482
  155.0 5.9 %collective-permute-start.6 = (f32[256,256]{1,0:T(8,128)S(1)}, f32[256,256]{1,0:T(8,128)S(1)}, u32[]{:S(2)}, u32[]{:S(2)}) collective-permute-start(f32[256,256]{1,0:T(8,128)S(1)} %get-tuple-element.19), channel_id=1, source_target_pairs={{0,24},{1,25},{2,26},{3,27},{4,28},{5,29},{6,30},{7,31},{8,0},{9,1... | collective-permute-start | bytes 786440 | tf_op jit(solution)/shard_map/ppermute | solution.py:483
  160.9 2.6 %collective-permute-done.4 = f32[256,256]{1,0:T(8,128)S(1)} collective-permute-done((f32[256,256]{1,0:T(8,128)S(1)}, f32[256,256]{1,0:T(8,128)S(1)}, u32[]{:S(2)}, u32[]{:S(2)}) %collective-permute-start.4) | collective-permute-done | bytes 262176 | tf_op jit(solution)/shard_map/ppermute | solution.py:482
  163.5 9.4 %collective-permute-start.5 = (f32[256,256]{1,0:T(8,128)S(1)}, f32[256,256]{1,0:T(8,128)S(1)}, u32[]{:S(2)}, u32[]{:S(2)}) collective-permute-start(f32[256,256]{1,0:T(8,128)S(1)} %collective-permute-done.4), channel_id=1, source_target_pairs={{0,8},{1,9},{2,10},{3,11},{4,12},{5,13},{6,14},{7,15},{8,16},{9,17... | collective-permute-start | bytes 786440 | tf_op jit(solution)/shard_map/ppermute | solution.py:482
  172.9 0.0 collective-permute-done.6
  172.9 1.9 collective-permute-start.7
  174.8 7.5 %collective-permute-done.5 = f32[256,256]{1,0:T(8,128)S(1)} collective-permute-done((f32[256,256]{1,0:T(8,128)S(1)}, f32[256,256]{1,0:T(8,128)S(1)}, u32[]{:S(2)}, u32[]{:S(2)}) %collective-permute-start.5) | collective-permute-done | bytes 262176 | tf_op jit(solution)/shard_map/ppermute | solution.py:482
  182.4 5.8 %collective-permute-done.7 = f32[256,256]{1,0:T(8,128)S(1)} collective-permute-done((f32[256,256]{1,0:T(8,128)S(1)}, f32[256,256]{1,0:T(8,128)S(1)}, u32[]{:S(2)}, u32[]{:S(2)}) %collective-permute-start.7) | collective-permute-done | bytes 262176 | tf_op jit(solution)/shard_map/ppermute | solution.py:483
  188.2 0.9 maximum_add_fusion
  (4 shorter events, 0.1 us)
Async XLA Ops:
  7.2 57.1 %all-gather.3.cloned.1.call-start = ((), (), s32[]{:S(2)}) async-start(), calls=%async_computation.2 | async-start | bytes 6684672 | tf_op jit(solution)/shard_map/all_gather | solution.py:469
  9.9 10.2 %collective-permute-start = (bf16[256,256]{1,0:T(8,128)(2,1)S(1)}, bf16[256,256]{1,0:T(8,128)(2,1)S(1)}, u32[]{:S(2)}, u32[]{:S(2)}) collective-permute-start(bf16[256,256]{1,0:T(8,128)(2,1)S(1)} %slice.9), channel_id=1, source_target_pairs={{0,256},{1,257},{2,258},{3,259},{4,260},{5,261},{6,262},{7,263},{8... | collective-permute-start | bytes 393224 | tf_op jit(solution)/shard_map/ppermute | solution.py:442
  20.2 3.8 %collective-permute-start.1 = (bf16[256,256]{1,0:T(8,128)(2,1)S(1)}, bf16[256,256]{1,0:T(8,128)(2,1)S(1)}, u32[]{:S(2)}, u32[]{:S(2)}) collective-permute-start(bf16[256,256]{1,0:T(8,128)(2,1)S(1)} %broadcast_select_fusion), channel_id=1, source_target_pairs={{0,128},{256,384},{1,129},{257,385},{2,130},{258,386},{3,131},{259... | collective-permute-start | bytes 393224 | tf_op jit(solution)/shard_map/ppermute | solution.py:442
  24.0 3.8 %collective-permute-start.2 = (bf16[256,256]{1,0:T(8,128)(2,1)S(1)}, bf16[256,256]{1,0:T(8,128)(2,1)S(1)}, u32[]{:S(2)}, u32[]{:S(2)}) collective-permute-start(bf16[256,256]{1,0:T(8,128)(2,1)S(1)} %broadcast_select_fusion.1), channel_id=1, source_target_pairs={{0,64},{128,192},{256,320},{384,448},{1,65},{129,193},{257,321},{3... | collective-permute-start | bytes 393224 | tf_op jit(solution)/shard_map/ppermute | solution.py:442
  27.8 17.4 %collective-permute-start.3 = (bf16[256,256]{1,0:T(8,128)(2,1)S(1)}, bf16[256,256]{1,0:T(8,128)(2,1)S(1)}, u32[]{:S(2)}, u32[]{:S(2)}) collective-permute-start(bf16[256,256]{1,0:T(8,128)(2,1)S(1)} %broadcast_select_fusion.2), channel_id=1, source_target_pairs={{0,32},{64,96},{128,160},{192,224},{256,288},{320,352},{384,416},{... | collective-permute-start | bytes 393224 | tf_op jit(solution)/shard_map/ppermute | solution.py:442
  33.0 11.0 %copy-start.3 = (s32[32]{0:T(128)S(1)}, s32[32]{0:T(128)}, u32[]{:S(2)}) copy-start(s32[32]{0:T(128)} %param.5) | copy-start | bytes 388
  33.0 61.9 %all-to-all-start.1 = ((bf16[16,256,256]{2,1,0:T(8,128)(2,1)}), bf16[16,256,256]{2,1,0:T(8,128)(2,1)S(1)}, u32[]{:S(2)}, u32[]{:S(2)}) async-start(bf16[16,256,256]{2,1,0:T(8,128)(2,1)} %shard_map.61), calls=%async_computation.1 | async-start | bytes 4194304 | tf_op jit(solution)/shard_map/all_to_all | solution.py:472
  45.3 19.0 %copy-start.1 = (bf16[256,768]{1,0:T(8,128)(2,1)S(1)}, bf16[256,768]{1,0:T(8,128)(2,1)}, u32[]{:S(2)}) copy-start(bf16[256,768]{1,0:T(8,128)(2,1)} %slice.8.own_ref) | copy-start | bytes 1179652
  93.5 1.3 copy-start
  94.9 8.9 %copy-start.2 = (bf16[2,256,256]{2,1,0:T(8,128)(2,1)S(1)}, bf16[2,256,256]{2,1,0:T(8,128)(2,1)}, u32[]{:S(2)}) copy-start(bf16[2,256,256]{2,1,0:T(8,128)(2,1)} %anc_ref.1) | copy-start | bytes 786436
  94.9 55.7 %all-to-all-start = ((bf16[16,256,256]{2,1,0:T(8,128)(2,1)}), bf16[16,256,256]{2,1,0:T(8,128)(2,1)}, u32[]{:S(2)}, u32[]{:S(2)}) async-start(bf16[16,256,256]{2,1,0:T(8,128)(2,1)} %copy-done), calls=%async_computation | async-start | bytes 4194304 | tf_op jit(solution)/shard_map/all_to_all | solution.py:478
  152.9 10.6 %collective-permute-start.4 = (f32[256,256]{1,0:T(8,128)S(1)}, f32[256,256]{1,0:T(8,128)S(1)}, u32[]{:S(2)}, u32[]{:S(2)}) collective-permute-start(f32[256,256]{1,0:T(8,128)S(1)} %get-tuple-element.18), channel_id=1, source_target_pairs={{0,8},{1,9},{2,10},{3,11},{4,12},{5,13},{6,14},{7,15},{8,16},{9,17... | collective-permute-start | bytes 786440 | tf_op jit(solution)/shard_map/ppermute | solution.py:482
  155.0 17.9 %collective-permute-start.6 = (f32[256,256]{1,0:T(8,128)S(1)}, f32[256,256]{1,0:T(8,128)S(1)}, u32[]{:S(2)}, u32[]{:S(2)}) collective-permute-start(f32[256,256]{1,0:T(8,128)S(1)} %get-tuple-element.19), channel_id=1, source_target_pairs={{0,24},{1,25},{2,26},{3,27},{4,28},{5,29},{6,30},{7,31},{8,0},{9,1... | collective-permute-start | bytes 786440 | tf_op jit(solution)/shard_map/ppermute | solution.py:483
  163.5 18.8 %collective-permute-start.5 = (f32[256,256]{1,0:T(8,128)S(1)}, f32[256,256]{1,0:T(8,128)S(1)}, u32[]{:S(2)}, u32[]{:S(2)}) collective-permute-start(f32[256,256]{1,0:T(8,128)S(1)} %collective-permute-done.4), channel_id=1, source_target_pairs={{0,8},{1,9},{2,10},{3,11},{4,12},{5,13},{6,14},{7,15},{8,16},{9,17... | collective-permute-start | bytes 786440 | tf_op jit(solution)/shard_map/ppermute | solution.py:482
  172.9 15.3 %collective-permute-start.7 = (f32[256,256]{1,0:T(8,128)S(1)}, f32[256,256]{1,0:T(8,128)S(1)}, u32[]{:S(2)}, u32[]{:S(2)}) collective-permute-start(f32[256,256]{1,0:T(8,128)S(1)} %collective-permute-done.6), channel_id=1, source_target_pairs={{0,24},{1,25},{2,26},{3,27},{4,28},{5,29},{6,30},{7,31},{8,0},{9,1... | collective-permute-start | bytes 786440 | tf_op jit(solution)/shard_map/ppermute | solution.py:483
Sparse Core Ops, SparseCore 0:
  10.7 53.5 all-gather.2

commit v9 on v7

--- a/solution.py
+++ b/solution.py
@@ -10,6 +10,7 @@
 SUB = 8
 PANEL = 32
 GROUP = 4
+H = B // 2
 VMEM = pl.BlockSpec(memory_space=pltpu.VMEM)
 ANY = pl.BlockSpec(memory_space=pl.ANY)
 F32 = jnp.float32
@@ -331,7 +332,7 @@
             pltpu.SemaphoreType.DMA((blocks // GROUP,)),
             pltpu.SemaphoreType.DMA((blocks // GROUP,)),
         ],
-        compiler_params=pltpu.CompilerParams(vmem_limit_bytes=48 << 20),
+        compiler_params=pltpu.CompilerParams(vmem_limit_bytes=62 << 20),
         cost_estimate=pl.CostEstimate(
             flops=30_000_000_000, bytes_accessed=10 << 20, transcendentals=0
         ),
@@ -409,21 +410,21 @@
     )(slots, x, ancestor)
 
 
-def sum_updates(slots, x, start):
+def sum_updates(slots, x, start, half):
     return pl.pallas_call(
         end_sum_kernel,
         grid=(x.shape[0] // GROUP,),
         in_specs=[
             pl.BlockSpec(memory_space=pltpu.SMEM),
-            pl.BlockSpec((GROUP, B, B), lambda k: (k, 0, 0)),
-            pl.BlockSpec((4, B, B), lambda k: (0, 0, 0)),
+            pl.BlockSpec((GROUP, H, B), lambda k: (k, half, 0)),
+            pl.BlockSpec((4, H, B), lambda k: (0, half, 0)),
         ],
-        out_specs=[pl.BlockSpec((2, B, B), lambda k: (0, 0, 0))] * 2,
-        out_shape=[jax.ShapeDtypeStruct((2, B, B), F32)] * 2,
-        scratch_shapes=[pltpu.VMEM((4, B, B), F32)],
+        out_specs=[pl.BlockSpec((2, H, B), lambda k: (0, 0, 0))] * 2,
+        out_shape=[jax.ShapeDtypeStruct((2, H, B), F32)] * 2,
+        scratch_shapes=[pltpu.VMEM((4, H, B), F32)],
         compiler_params=pltpu.CompilerParams(vmem_limit_bytes=40 << 20),
         cost_estimate=pl.CostEstimate(
-            flops=4_000_000, bytes_accessed=4 << 20, transcendentals=0
+            flops=4_000_000, bytes_accessed=2 << 20, transcendentals=0
         ),
     )(slots, x, start)
 
@@ -470,9 +471,12 @@
     start = sum_fronts(slots, f, ancestor)
     factor, u = factor_and_update(scalars, own, gathered, low0, inv0)
     u = lax.all_to_all(u, "col", 0, 0, axis_index_groups=groups, tiled=True)
-    mine, sent = sum_updates(slots, u, start)
-    received = lax.ppermute(sent, "col", [(c, (c + half) % cols) for c in range(cols)])
-    return factor[None], mine + received
+    far = [(c, (c + half) % cols) for c in range(cols)]
+    top, top_sent = sum_updates(slots, u, start, 0)
+    top_got = lax.ppermute(top_sent, "col", far)
+    bottom, bottom_sent = sum_updates(slots, u, start, 1)
+    bottom_got = lax.ppermute(bottom_sent, "col", far)
+    return factor[None], jnp.concatenate([top + top_got, bottom + bottom_got], axis=1)
 
 
 def solution(mesh):

time: 192 us -> 189 us (0.984)
  the two profiles are of different devices: /device:TPU:69 before, /device:TPU:70 now
where the time goes in v9:
time: 189 us
  waiting for transfers between devices  78.6 us (42%)
  Pallas kernels  48 us (25%)
  starting transfers between devices  40.3 us (21%)
  between operations  14.2 us (8%)
  local copies, waits for them, and re-layouts  4.73 us (3%)
  other arithmetic  3.05 us (2%)
    all_to_all x1, waiting for transfers between devices, shards(): u = lax.all_to_all(u, 'col', 0, 0, axis_index_groups=groups, tiled=True)  44.3 us
    pallas_call x1, Pallas kernels, factor_and_update(): pl.pallas_call(rest_kernel, in_specs=[pl.BlockSpec(memory_space=pltpu.SME...  30.3 us
    ppermute x1, waiting for transfers between devices, shards(): bottom_got = lax.ppermute(bottom_sent, 'col', far)  14.3 us
    ppermute x4, starting transfers between devices, broadcast_first(): got = lax.ppermute(block, 'row', pairs)  11.6 us
    all_to_all x1, starting transfers between devices, shards(): lax.all_to_all(block_columns(front), 'col', 0, 0, axis_index_groups=group...  10.9 us
    pallas_call x1, Pallas kernels, factor_first(): pl.pallas_call(first_kernel, in_specs=[VMEM], out_specs=[VMEM, VMEM], out...  9.42 us
    all_to_all x1, starting transfers between devices, shards(): u = lax.all_to_all(u, 'col', 0, 0, axis_index_groups=groups, tiled=True)  8.04 us
    all_gather x1, waiting for transfers between devices, shards(): gathered = lax.all_gather(own, 'row', axis=0, tiled=False)  7.57 us
  transfers between devices with their start and end apart: 9, of which 7 were waited for; matrix products, arithmetic and copies ran while one was open for 1% of the time, Pallas kernels for 25%

profile of v9, /device:TPU:70, one launch (start us, length us, event | category | flops | bytes accessed | tf_op | source)
XLA Modules:
  0.0 188.9 jit_solution(7846487348356401923)
XLA Ops:
  7.2 0.0 all-gather.3.cloned.1.call-start
  7.2 0.9 slice.9
  8.1 1.8 slice.8.own_ref
  9.9 0.0 all-gather.3.cloned.1.call-update
  9.9 7.7 %collective-permute-start = (bf16[256,256]{1,0:T(8,128)(2,1)S(1)}, bf16[256,256]{1,0:T(8,128)(2,1)S(1)}, u32[]{:S(2)}, u32[]{:S(2)}) collective-permute-start(bf16[256,256]{1,0:T(8,128)(2,1)S(1)} %slice.9), channel_id=1, source_target_pairs={{0,256},{1,257},{2,258},{3,259},{4,260},{5,261},{6,262},{7,263},{8... | collective-permute-start | bytes 393224 | tf_op jit(solution)/shard_map/ppermute | solution.py:437
  17.7 2.5 %collective-permute-done = bf16[256,256]{1,0:T(8,128)(2,1)S(1)} collective-permute-done((bf16[256,256]{1,0:T(8,128)(2,1)S(1)}, bf16[256,256]{1,0:T(8,128)(2,1)S(1)}, u32[]{:S(2)}, u32[]{:S(2)}) %collective-permute-start) | collective-permute-done | bytes 131104 | tf_op jit(solution)/shard_map/ppermute | solution.py:437
  20.2 1.3 collective-permute-start.1
  21.5 2.5 %collective-permute-done.1 = bf16[256,256]{1,0:T(8,128)(2,1)S(1)} collective-permute-done((bf16[256,256]{1,0:T(8,128)(2,1)S(1)}, bf16[256,256]{1,0:T(8,128)(2,1)S(1)}, u32[]{:S(2)}, u32[]{:S(2)}) %collective-permute-start.1) | collective-permute-done | bytes 131104 | tf_op jit(solution)/shard_map/ppermute | solution.py:437
  24.0 1.3 collective-permute-start.2
  25.3 2.5 %collective-permute-done.2 = bf16[256,256]{1,0:T(8,128)(2,1)S(1)} collective-permute-done((bf16[256,256]{1,0:T(8,128)(2,1)S(1)}, bf16[256,256]{1,0:T(8,128)(2,1)S(1)}, u32[]{:S(2)}, u32[]{:S(2)}) %collective-permute-start.2) | collective-permute-done | bytes 131104 | tf_op jit(solution)/shard_map/ppermute | solution.py:437
  27.8 1.3 collective-permute-start.3
  29.1 3.9 %shard_map.61 = bf16[16,256,256]{2,1,0:T(8,128)(2,1)} custom-call(bf16[256,4096]{1,0:T(8,128)(2,1)} %bitcast.26), custom_call_target="tpu_custom_call" | custom-call | bytes 4194304 | tf_op jit(solution)/shard_map/pallas_call | solution.py:349
  33.0 0.0 copy-start.3
  33.0 10.9 %all-to-all-start.1 = ((bf16[16,256,256]{2,1,0:T(8,128)(2,1)}), bf16[16,256,256]{2,1,0:T(8,128)(2,1)}, u32[]{:S(2)}, u32[]{:S(2)}) async-start(bf16[16,256,256]{2,1,0:T(8,128)(2,1)} %shard_map.61), calls=%async_computation.1 | async-start | bytes 4194304 | tf_op jit(solution)/shard_map/all_to_all | solution.py:467
  43.9 0.0 copy-done.3
  43.9 0.6 dynamic_slice.14
  44.5 1.2 pad_add_fusion.scalars
  45.7 0.0 collective-permute-done.3
  45.8 9.4 %shard_map.59 = (f32[256,256]{1,0:T(8,128)S(1)}, f32[256,256]{1,0:T(8,128)S(1)}) custom-call(bf16[256,256]{1,0:T(8,128)(2,1)S(1)} %broadcast_select_fusion.3.a_ref), custom_call_target="tpu_custom_call" | custom-call | flops 10000000000 | bytes 1048576 | tf_op jit(solution)/shard_map/pallas_call | solution.py:160
  55.2 0.0 copy-start.1
  55.2 0.7 copy-done.1
  55.9 0.0 copy-start.2
  55.9 0.7 copy-done.2
  56.6 7.6 %all-gather.3.cloned.1.call-done = bf16[4096,768]{1,0:T(8,128)(2,1)} async-done(((bf16[256,768]{1,0:T(8,128)(2,1)}), bf16[4096,768]{1,0:T(8,128)(2,1)}) %all-gather.3.cloned.1.call-update) | async-done | bytes 6291472 | tf_op jit(solution)/shard_map/all_gather | solution.py:464
  64.2 30.3 %shard_map.60 = (f32[256,768]{1,0:T(8,128)}, bf16[16,256,256]{2,1,0:T(8,128)(2,1)}) custom-call(s32[2]{0:T(128)} %pad_add_fusion.scalars, bf16[256,768]{1,0:T(8,128)(2,1)} %slice.8.own_ref, bf16[16,256,768]{2,1,0:T(8,128)(2,1)} %bitcast.27, f32[256,256]{1,0:T(8,128)} %copy-done.1, f32[256,256]{1,0:T(8,128)} %copy-done.2), custom_call_target="tpu_custom_call" | custom-call | flops 30000001024 | bytes 10485760 | tf_op jit(solution)/shard_map/pallas_call | solution.py:311
  94.5 0.0 all-to-all-done.1.x_ref
  94.5 0.0 copy-start
  94.5 8.0 %all-to-all-start = ((bf16[16,256,256]{2,1,0:T(8,128)(2,1)}), bf16[16,256,256]{2,1,0:T(8,128)(2,1)S(1)}, u32[]{:S(2)}, u32[]{:S(2)}) async-start(bf16[16,256,256]{2,1,0:T(8,128)(2,1)} %get-tuple-element.17), calls=%async_computation | async-start | bytes 4194304 | tf_op jit(solution)/shard_map/all_to_all | solution.py:473
  102.5 0.8 and_select_fusion.2.slots
  103.4 0.0 copy-done
  103.4 2.5 %shard_map.62.start_ref = f32[4,256,256]{2,1,0:T(8,128)S(1)} custom-call(s32[16]{0:T(128)S(1)} %and_select_fusion.2.slots, bf16[16,256,256]{2,1,0:T(8,128)(2,1)} %all-to-all-done.1.x_ref, bf16[2,256,256]{2,1,0:T(8,128)(2,1)S(1)} %copy-done), custom_call_target="tpu_custom_call" | custom-call | flops 4000000 | bytes 4194304 | tf_op jit(solution)/shard_map/pallas_call | solution.py:396
  105.9 44.3 %all-to-all-done.x_ref = bf16[16,256,256]{2,1,0:T(8,128)(2,1)S(1)} async-done(((bf16[16,256,256]{2,1,0:T(8,128)(2,1)}), bf16[16,256,256]{2,1,0:T(8,128)(2,1)S(1)}, u32[]{:S(2)}, u32[]{:S(2)}) %all-to-all-start) | async-done | bytes 2097184 | tf_op jit(solution)/shard_map/all_to_all | solution.py:473
  150.2 1.0 shard_map.64
  151.1 6.5 %collective-permute-start.5 = (f32[2,128,256]{2,1,0:T(8,128)S(1)}, f32[2,128,256]{2,1,0:T(8,128)S(1)}, u32[]{:S(2)}, u32[]{:S(2)}) collective-permute-start(f32[2,128,256]{2,1,0:T(8,128)S(1)} %get-tuple-element.21), channel_id=1, source_target_pairs={{0,16},{1,17},{2,18},{3,19},{4,20},{5,21},{6,22},{7,23},{8,24},{9,... | collective-permute-start | bytes 786440 | tf_op jit(solution)/shard_map/ppermute | solution.py:478
  157.6 1.0 shard_map.63
  158.6 3.2 %collective-permute-start.4 = (f32[2,128,256]{2,1,0:T(8,128)S(1)}, f32[2,128,256]{2,1,0:T(8,128)S(1)}, u32[]{:S(2)}, u32[]{:S(2)}) collective-permute-start(f32[2,128,256]{2,1,0:T(8,128)S(1)} %get-tuple-element.19), channel_id=1, source_target_pairs={{0,16},{1,17},{2,18},{3,19},{4,20},{5,21},{6,22},{7,23},{8,24},{9,... | collective-permute-start | bytes 786440 | tf_op jit(solution)/shard_map/ppermute | solution.py:476
  161.9 14.3 %collective-permute-done.5 = f32[2,128,256]{2,1,0:T(8,128)S(1)} collective-permute-done((f32[2,128,256]{2,1,0:T(8,128)S(1)}, f32[2,128,256]{2,1,0:T(8,128)S(1)}, u32[]{:S(2)}, u32[]{:S(2)}) %collective-permute-start.5) | collective-permute-done | bytes 262176 | tf_op jit(solution)/shard_map/ppermute | solution.py:478
  176.2 5.0 %collective-permute-done.4 = f32[2,128,256]{2,1,0:T(8,128)S(1)} collective-permute-done((f32[2,128,256]{2,1,0:T(8,128)S(1)}, f32[2,128,256]{2,1,0:T(8,128)S(1)}, u32[]{:S(2)}, u32[]{:S(2)}) %collective-permute-start.4) | collective-permute-done | bytes 262176 | tf_op jit(solution)/shard_map/ppermute | solution.py:476
  181.2 0.8 pad_maximum_fusion
  (6 shorter events, 0.1 us)
Async XLA Ops:
  7.2 57.0 %all-gather.3.cloned.1.call-start = ((), (), s32[]{:S(2)}) async-start(), calls=%async_computation.2 | async-start | bytes 6684672 | tf_op jit(solution)/shard_map/all_gather | solution.py:464
  9.9 10.2 %collective-permute-start = (bf16[256,256]{1,0:T(8,128)(2,1)S(1)}, bf16[256,256]{1,0:T(8,128)(2,1)S(1)}, u32[]{:S(2)}, u32[]{:S(2)}) collective-permute-start(bf16[256,256]{1,0:T(8,128)(2,1)S(1)} %slice.9), channel_id=1, source_target_pairs={{0,256},{1,257},{2,258},{3,259},{4,260},{5,261},{6,262},{7,263},{8... | collective-permute-start | bytes 393224 | tf_op jit(solution)/shard_map/ppermute | solution.py:437
  20.2 3.8 %collective-permute-start.1 = (bf16[256,256]{1,0:T(8,128)(2,1)S(1)}, bf16[256,256]{1,0:T(8,128)(2,1)S(1)}, u32[]{:S(2)}, u32[]{:S(2)}) collective-permute-start(bf16[256,256]{1,0:T(8,128)(2,1)S(1)} %broadcast_select_fusion), channel_id=1, source_target_pairs={{0,128},{256,384},{1,129},{257,385},{2,130},{258,386},{3,131},{259... | collective-permute-start | bytes 393224 | tf_op jit(solution)/shard_map/ppermute | solution.py:437
  24.0 3.8 %collective-permute-start.2 = (bf16[256,256]{1,0:T(8,128)(2,1)S(1)}, bf16[256,256]{1,0:T(8,128)(2,1)S(1)}, u32[]{:S(2)}, u32[]{:S(2)}) collective-permute-start(bf16[256,256]{1,0:T(8,128)(2,1)S(1)} %broadcast_select_fusion.1), channel_id=1, source_target_pairs={{0,64},{128,192},{256,320},{384,448},{1,65},{129,193},{257,321},{3... | collective-permute-start | bytes 393224 | tf_op jit(solution)/shard_map/ppermute | solution.py:437
  27.8 17.9 %collective-permute-start.3 = (bf16[256,256]{1,0:T(8,128)(2,1)S(1)}, bf16[256,256]{1,0:T(8,128)(2,1)S(1)}, u32[]{:S(2)}, u32[]{:S(2)}) collective-permute-start(bf16[256,256]{1,0:T(8,128)(2,1)S(1)} %broadcast_select_fusion.2), channel_id=1, source_target_pairs={{0,32},{64,96},{128,160},{192,224},{256,288},{320,352},{384,416},{... | collective-permute-start | bytes 393224 | tf_op jit(solution)/shard_map/ppermute | solution.py:437
  33.0 10.9 %copy-start.3 = (s32[32]{0:T(128)S(1)}, s32[32]{0:T(128)}, u32[]{:S(2)}) copy-start(s32[32]{0:T(128)} %param.5) | copy-start | bytes 388
  33.0 61.5 %all-to-all-start.1 = ((bf16[16,256,256]{2,1,0:T(8,128)(2,1)}), bf16[16,256,256]{2,1,0:T(8,128)(2,1)}, u32[]{:S(2)}, u32[]{:S(2)}) async-start(bf16[16,256,256]{2,1,0:T(8,128)(2,1)} %shard_map.61), calls=%async_computation.1 | async-start | bytes 4194304 | tf_op jit(solution)/shard_map/all_to_all | solution.py:467
  55.2 0.7 copy-start.1
  55.9 0.7 copy-start.2
  94.5 8.9 %copy-start = (bf16[2,256,256]{2,1,0:T(8,128)(2,1)S(1)}, bf16[2,256,256]{2,1,0:T(8,128)(2,1)}, u32[]{:S(2)}) copy-start(bf16[2,256,256]{2,1,0:T(8,128)(2,1)} %anc_ref.1) | copy-start | bytes 786436
  94.5 55.7 %all-to-all-start = ((bf16[16,256,256]{2,1,0:T(8,128)(2,1)}), bf16[16,256,256]{2,1,0:T(8,128)(2,1)S(1)}, u32[]{:S(2)}, u32[]{:S(2)}) async-start(bf16[16,256,256]{2,1,0:T(8,128)(2,1)} %get-tuple-element.17), calls=%async_computation | async-start | bytes 4194304 | tf_op jit(solution)/shard_map/all_to_all | solution.py:473
  151.1 25.0 %collective-permute-start.5 = (f32[2,128,256]{2,1,0:T(8,128)S(1)}, f32[2,128,256]{2,1,0:T(8,128)S(1)}, u32[]{:S(2)}, u32[]{:S(2)}) collective-permute-start(f32[2,128,256]{2,1,0:T(8,128)S(1)} %get-tuple-element.21), channel_id=1, source_target_pairs={{0,16},{1,17},{2,18},{3,19},{4,20},{5,21},{6,22},{7,23},{8,24},{9,... | collective-permute-start | bytes 786440 | tf_op jit(solution)/shard_map/ppermute | solution.py:478
  158.6 22.6 %collective-permute-start.4 = (f32[2,128,256]{2,1,0:T(8,128)S(1)}, f32[2,128,256]{2,1,0:T(8,128)S(1)}, u32[]{:S(2)}, u32[]{:S(2)}) collective-permute-start(f32[2,128,256]{2,1,0:T(8,128)S(1)} %get-tuple-element.19), channel_id=1, source_target_pairs={{0,16},{1,17},{2,18},{3,19},{4,20},{5,21},{6,22},{7,23},{8,24},{9,... | collective-permute-start | bytes 786440 | tf_op jit(solution)/shard_map/ppermute | solution.py:476
Sparse Core Ops, SparseCore 0:
  10.7 53.4 all-gather.2
